TPU v7x, 32 devices: a whole 2x2x4 slice. The times are simulated.
32 devices in a mesh: dp: 16 (over z, x, core), slab: 2 (over y).
Axes of the slice: x: 2, y: 2, z: 4, core: 2. Of those that a mesh axis runs over, the one named last changes fastest.
Arguments:
- point_feats: bfloat16 [16, 8, 64, 128], P('dp', 'slab'), may hold values from -6 to 6
- point_coords: bfloat16 [16, 8, 3, 128], P('dp', 'slab'), may hold values from 0 to 1
- slot_block: int32 [16, 2, 2, 4], P('dp', 'slab'), may hold values from 0 to 3
- slot_cell: int32 [16, 2, 2, 4], P('dp', 'slab'), may hold values from 0 to 8191, as said below
- slot_count: int32 [16, 2, 2], P('dp', 'slab'), may hold values from 1 to 4, as said below
- cotangent: float32 [16, 16, 16, 16, 128], P('dp', 'slab'), may hold values from -6 to 6
- offset_map: float32 [64, 3], replicated, may hold values from -12 to 12
- offset_bias: float32 [64], replicated, may hold values from -4 to 4
- kernel_mix: bfloat16 [64, 64, 64], replicated, may hold values from -0.75 to 0.75
- lift_weight: bfloat16 [64, 64], replicated, may hold values from -0.75 to 0.75
Outputs:
- spectral_grad: float32 [64, 16, 16, 16, 128], P('dp', 'slab')
Inputs may be any that keep to these rules, and one draw needn't show every extreme that they name: `slot_cell`: cell row of a slot on its receiving slab index. `slot_count`: in every sample one receiving slab index, drawn from the seed, gets 4 live slots from every sending slab index.
All inputs are finite; a program needn't handle non-finite values.
Results may differ from a plain program's by a relative error of at most 0.0031.
Values may be sent and summed in bfloat16 or wider, within the bound.
No kernel may reach another device: no remote copies, remote signals or barrier semaphores. Data moves between devices by JAX's collectives and lax.ppermute only.
A program may use at most 128 MiB of HBM per device.

v0:
```python
import functools
import math

import jax
import jax.numpy as jnp
from jax import lax
from jax.experimental import pallas as pl
from jax.experimental.pallas import tpu as pltpu
from jax.sharding import PartitionSpec as P

GX = 128
GY = 128
GZ = 128
VMEM_LIMIT = 48 * 1024 * 1024
HIGH = lax.Precision.HIGHEST
ROWS0 = (((0,), (0,)), ((), ()))


def slot_kernel(
    peer_ref, block_ref, cell_ref, count_ref, zcoef_ref, feats_ref, coords_ref, map_ref,
    bias_ref, mix_ref, out_ref, acc_ref, part_ref, turned_ref,
):
    peer = peer_ref[0]
    capacity = block_ref.shape[1]
    hidden, channels = mix_ref.shape[0], mix_ref.shape[1]
    points = feats_ref.shape[2]
    planes = peer_ref[1]
    width = capacity * channels
    tags = []
    for j in range(capacity):
        block = block_ref[peer, j]
        cell = cell_ref[peer, j]
        row_x = peer * planes + lax.div(cell, GY)
        row_y = lax.rem(cell, GY)
        pos_x = (row_x.astype(jnp.float32) + 0.5) * (1.0 / GX)
        pos_y = (row_y.astype(jnp.float32) + 0.5) * (1.0 / GY)
        spots = coords_ref[block].astype(jnp.float32)
        point_part = (
            map_ref[:, 0:1] * spots[0:1, :]
            + map_ref[:, 1:2] * spots[1:2, :]
            + map_ref[:, 2:3] * spots[2:3, :]
        )
        shift = map_ref[:, 0:1] * pos_x + map_ref[:, 1:2] * pos_y + bias_ref[...]
        part_ref[j] = shift - point_part
        turned_ref[:, j * channels : (j + 1) * channels] = (
            feats_ref[block].astype(jnp.float32).T.astype(jnp.bfloat16)
        )
        tags.append(jnp.where(j < count_ref[peer], cell, -1).astype(jnp.float32))
    acc_ref[...] = jnp.zeros_like(acc_ref)
    pos_z = (lax.broadcasted_iota(jnp.int32, (GZ, points), 0).astype(jnp.float32) + 0.5) * (
        1.0 / GZ
    )
    diag = (
        lax.broadcasted_iota(jnp.int32, (width, width), 0) // channels
        == lax.broadcasted_iota(jnp.int32, (width, width), 1) // channels
    )
    step = 4

    def body(it, carry):
        mixed, weights = [], []
        for u in range(step):
            h = it * step + u
            mix = mix_ref[h]
            wide = jnp.concatenate([mix] * capacity, axis=1)
            tall = jnp.concatenate([wide] * capacity, axis=0)
            spread = jnp.where(diag, tall, jnp.zeros_like(tall))
            mixed.append(
                jnp.dot(turned_ref[...], spread, preferred_element_type=jnp.float32).astype(
                    jnp.bfloat16
                )
            )
            cell_z = pos_z * zcoef_ref[h]
            rows = [
                jnp.maximum(cell_z + part_ref[j, pl.ds(h, 1), :], 0.0).astype(jnp.bfloat16)
                for j in range(capacity)
            ]
            weights.append(jnp.concatenate(rows, axis=0))
        acc_ref[...] += jnp.dot(
            jnp.concatenate(weights, axis=1),
            jnp.concatenate(mixed, axis=0),
            preferred_element_type=jnp.float32,
        )
        return carry

    lax.fori_loop(0, hidden // step, body, 0)
    for j in range(capacity):
        terms = acc_ref[j * GZ : (j + 1) * GZ, j * channels : (j + 1) * channels]
        out_ref[j * channels : (j + 1) * channels, :] = terms.T * (1.0 / points)
    row = lax.broadcasted_iota(jnp.int32, (8, GZ), 0)
    tag_rows = jnp.full((8, GZ), -1.0, jnp.float32)
    for j in range(capacity):
        tag_rows = jnp.where(row == j, tags[j], tag_rows)
    out_ref[capacity * channels :, :] = tag_rows


def slot_terms(peer_info, slot_block, slot_cell, slot_count, zcoef, feats, coords, offset_map,
               offset_bias, kernel_mix):
    capacity = slot_block.shape[1]
    channels, points = feats.shape[1], feats.shape[2]
    hidden = kernel_mix.shape[0]
    smem = pl.BlockSpec(memory_space=pltpu.SMEM)
    vmem = pl.BlockSpec(memory_space=pltpu.VMEM)
    width = capacity * channels
    return pl.pallas_call(
        slot_kernel,
        out_shape=jax.ShapeDtypeStruct((width + 8, GZ), jnp.float32),
        in_specs=[smem] * 5 + [vmem] * 5,
        out_specs=vmem,
        scratch_shapes=[
            pltpu.VMEM((capacity * GZ, width), jnp.float32),
            pltpu.VMEM((capacity, hidden, points), jnp.float32),
            pltpu.VMEM((points, width), jnp.bfloat16),
        ],
        compiler_params=pltpu.CompilerParams(vmem_limit_bytes=VMEM_LIMIT),
        cost_estimate=pl.CostEstimate(
            flops=2 * capacity * GZ * hidden * points * width, bytes_accessed=2 << 20,
            transcendentals=0,
        ),
        name="slot_terms",
    )(peer_info, slot_block, slot_cell, slot_count, zcoef, feats, coords, offset_map, offset_bias,
      kernel_mix)


def lift_kernel(groups, capacity, dests, copies, *refs):
    terms = refs[:groups]
    lift_ref, table_ref, out_ref, tag_ref, wide_ref = refs[groups:]
    channels = lift_ref.shape[0]
    kept = channels // dests
    slots = groups * capacity
    lanes = out_ref.shape[1]
    per = 2 * slots

    def tag_of(m):
        base = capacity * channels + m % capacity
        return terms[m // capacity][base : base + 1, :]

    def terms_of(m):
        base = (m % capacity) * channels
        return terms[m // capacity][base : base + channels, :]

    for n in range(slots):
        tag = tag_of(n)
        live = tag >= 0.0
        summed = jnp.zeros((channels, GZ), jnp.float32)
        leader = live
        for m in range(slots):
            same = (tag_of(m) == tag) & live
            summed = summed + jnp.where(same, terms_of(m), 0.0)
            if m < n:
                leader = leader & jnp.logical_not(same)
        latent = summed.astype(jnp.bfloat16)
        lifted = jax.nn.gelu(
            jnp.dot(lift_ref[...], latent, preferred_element_type=jnp.float32)
        )
        lifted = jnp.where(leader, lifted, 0.0)
        for i in range(kept):
            wide_ref[n * dests : (n + 1) * dests, i * GZ : (i + 1) * GZ] = lifted[
                i * dests : (i + 1) * dests, :
            ]
        tag_ref[n : n + 1, :] = tag
    modes = jnp.dot(
        wide_ref[...], table_ref[...], precision=HIGH, preferred_element_type=jnp.float32
    )
    tags = tag_ref[:, :lanes]
    for n in range(slots):
        piece = modes[n * dests : (n + 1) * dests, :]
        for t in range(copies):
            out_ref[pl.ds(t * per + n, dests, stride=copies * per), :] = piece
    for d in range(dests * copies):
        out_ref[d * per + slots : (d + 1) * per, :] = tags


def lift_slots(terms, lift_rows, table, capacity, dests, copies):
    groups = len(terms)
    channels = lift_rows.shape[0]
    slots = groups * capacity
    lanes = table.shape[1]
    vmem = pl.BlockSpec(memory_space=pltpu.VMEM)
    return pl.pallas_call(
        functools.partial(lift_kernel, groups, capacity, dests, copies),
        out_shape=jax.ShapeDtypeStruct((dests * copies * 2 * slots, lanes), jnp.float32),
        in_specs=[vmem] * (groups + 2),
        out_specs=vmem,
        scratch_shapes=[
            pltpu.VMEM((slots, GZ), jnp.float32),
            pltpu.VMEM((slots * dests, channels // dests * GZ), jnp.float32),
        ],
        compiler_params=pltpu.CompilerParams(vmem_limit_bytes=VMEM_LIMIT),
        cost_estimate=pl.CostEstimate(
            flops=1 << 27, bytes_accessed=1 << 20, transcendentals=1 << 16
        ),
        name="lift_slots",
    )(*terms, lift_rows, table)


def modes_kernel(samples, slabs, slots, planes, scale, group, order_ref, recv_ref, freq_ref,
                 out_ref, all_ref):
    lanes = recv_ref.shape[1]
    total = freq_ref.shape[1]
    half = lanes // 2
    per = 2 * slots

    def body(q, carry):
        sample = order_ref[q]
        waves, values = [], []
        for t in range(slabs):
            base = pl.multiple_of((sample * slabs + t) * per, 8)
            piece = recv_ref[pl.ds(base, slots), :]
            tag = jnp.maximum(recv_ref[pl.ds(base + slots, slots), :][:, 0:1], 0.0)
            local_x = jnp.floor(tag * (1.0 / GY))
            turns = (local_x + t * planes) * (1.0 / GX) * freq_ref[0:1, :] + (
                tag - local_x * GY
            ) * (1.0 / GY) * freq_ref[1:2, :]
            values.append(piece)
            waves.append((turns - jnp.floor(turns)) * (2.0 * math.pi))
        angle = jnp.concatenate(waves, axis=0)
        plain = jnp.concatenate(values, axis=0)
        crossed = jnp.concatenate([plain[:, half:], -plain[:, :half]], axis=1)
        modes = lax.dot_general(
            jnp.concatenate([jnp.cos(angle), jnp.sin(angle)], axis=0),
            jnp.concatenate([plain, crossed], axis=0),
            ROWS0,
            precision=HIGH,
            preferred_element_type=jnp.float32,
        )
        all_ref[pl.ds(q, total, stride=samples), :] = modes * scale
        return carry

    lax.fori_loop(0, samples, body, 0)
    span = group * samples
    for block in range(total // group):
        out_ref[block] = all_ref[block * span : (block + 1) * span, :].T.astype(jnp.bfloat16)


def sample_modes(order, recv, freqs, samples, slabs, slots, planes, scale, group):
    lanes = recv.shape[1]
    total = freqs.shape[1]
    vmem = pl.BlockSpec(memory_space=pltpu.VMEM)
    return pl.pallas_call(
        functools.partial(modes_kernel, samples, slabs, slots, planes, scale, group),
        out_shape=jax.ShapeDtypeStruct((total // group, lanes, group * samples), jnp.bfloat16),
        in_specs=[pl.BlockSpec(memory_space=pltpu.SMEM), vmem, vmem],
        out_specs=vmem,
        scratch_shapes=[pltpu.VMEM((total * samples, lanes), jnp.float32)],
        compiler_params=pltpu.CompilerParams(vmem_limit_bytes=VMEM_LIMIT),
        cost_estimate=pl.CostEstimate(
            flops=1 << 27, bytes_accessed=1 << 20, transcendentals=1 << 16
        ),
        name="sample_modes",
    )(order, recv, freqs)


def grad_kernel(samples, group, depth, aliased, *refs):
    modes_ref, pick_ref, mask_ref = refs[:3]
    rows_refs = refs[3 : 3 + samples]
    out_ref = refs[3 + samples + aliased]
    lanes = modes_ref.shape[1]
    half_rows = lanes // 2
    kept = out_ref.shape[0]
    half = out_ref.shape[2] // 2
    span = samples * depth
    block = modes_ref[0]
    for g in range(group):
        left = jnp.dot(
            block, pick_ref[:, g * span : (g + 1) * span], preferred_element_type=jnp.float32
        )
        left = (left * mask_ref[...]).astype(jnp.bfloat16)
        right = jnp.concatenate([r[g * depth : (g + 1) * depth, :] for r in rows_refs], axis=0)
        both = jnp.dot(left, right, preferred_element_type=jnp.float32)
        plain, turned = both[:half_rows], both[half_rows:]
        total = plain + jnp.concatenate([turned[:, half:], -turned[:, :half]], axis=1)
        for i in range(kept):
            out_ref[i, g * depth : (g + 1) * depth, :] = total[i * depth : (i + 1) * depth]


def grad_chunk(modes, pick, mask, rows, kept, group, depth, chunk, chunks, previous):
    samples = len(rows)
    lanes = modes.shape[1]
    chunk_rows, width = rows[0].shape
    tile = group * depth
    steps = chunk_rows // tile
    in_specs = [
        pl.BlockSpec((1, lanes, group * samples), lambda s: (chunk * steps + s, 0, 0)),
        pl.BlockSpec(pick.shape, lambda s: (0, 0)),
        pl.BlockSpec(mask.shape, lambda s: (0, 0)),
    ] + [pl.BlockSpec((tile, width), lambda s: (s, 0))] * samples
    operands = [modes, pick, mask, *rows]
    aliases = {}
    if previous is not None:
        in_specs.append(pl.BlockSpec(memory_space=pl.ANY))
        aliases = {len(operands): 0}
        operands.append(previous)
    return pl.pallas_call(
        functools.partial(grad_kernel, samples, group, depth, int(previous is not None)),
        out_shape=jax.ShapeDtypeStruct((kept, chunk_rows * chunks, width), jnp.float32),
        grid=(steps,),
        in_specs=in_specs,
        out_specs=pl.BlockSpec((kept, tile, width), lambda s: (0, chunk * steps + s, 0)),
        input_output_aliases=aliases,
        compiler_params=pltpu.CompilerParams(vmem_limit_bytes=VMEM_LIMIT),
        cost_estimate=pl.CostEstimate(
            flops=2 * chunk_rows * lanes * samples * width * 2,
            bytes_accessed=chunk_rows * width * (2 * samples + 4 * kept),
            transcendentals=0,
        ),
        name="grad_chunk",
    )(*operands)


def chip_ring(chips):
    order = list(range(0, chips, 2))
    return order + [c for c in range(chips - 1, 0, -1) if c % 2]


def ring_perm(chips, step):
    order = chip_ring(chips)
    return [
        (2 * order[p] + core, 2 * order[(p + step) % chips] + core)
        for p in range(chips)
        for core in (0, 1)
    ]


def gather_chunk(rows, devices, forward):
    chips = devices // 2
    swap = [(d, d ^ 1) for d in range(devices)]
    half = chips // 2
    ahead = half if forward else chips - 1 - half
    chain = {0: rows}
    up = down = rows
    for s in range(1, max(ahead, chips - 1 - ahead) + 1):
        if s <= ahead:
            up = lax.ppermute(up, "dp", ring_perm(chips, 1))
            chain[s] = up
        if s <= chips - 1 - ahead:
            down = lax.ppermute(down, "dp", ring_perm(chips, -1))
            chain[chips - s] = down
    result = []
    for s in range(chips):
        result += [chain[s], lax.ppermute(chain[s], "dp", swap)]
    return result


def ring_order(devices):
    chips = devices // 2
    order = chip_ring(chips)
    place = [order.index(c) for c in range(chips)]
    table = []
    for d in range(devices):
        chip, core = d // 2, d % 2
        row = []
        for s in range(chips):
            source = order[(place[chip] - s) % chips]
            row += [2 * source + core, 2 * source + 1 - core]
        table.append(row)
    return jnp.array(table, jnp.int32)


def per_device(
    point_feats, point_coords, slot_block, slot_cell, slot_count, cotangent, offset_map,
    offset_bias, kernel_mix, lift_weight,
):
    slabs = lax.axis_size("slab")
    devices = lax.axis_size("dp")
    slab_index = lax.axis_index("slab")
    channels = point_feats.shape[2]
    mode_count = cotangent.shape[2]
    capacity = slot_block.shape[3]
    width = cotangent.shape[4]
    planes = GX // slabs
    kept = channels // devices
    lanes = 2 * kept * mode_count
    slots = slabs * capacity
    local_x = cotangent.shape[1]
    total = local_x * mode_count
    chunks = 2
    group = min(8, total // chunks)

    rows = cotangent[0].reshape(-1, width).astype(jnp.bfloat16)
    size = rows.shape[0] // chunks
    gathered = [
        gather_chunk(rows[c * size : (c + 1) * size], devices, c % 2 == 0) for c in range(chunks)
    ]

    terms = []
    for s in list(range(1, slabs)) + [0]:
        peer = lax.rem(slab_index + s, slabs)
        part = slot_terms(
            jnp.stack([peer, jnp.int32(planes)]), slot_block[0, 0], slot_cell[0, 0],
            slot_count[0, 0], offset_map[:, 2], point_feats[0], point_coords[0], offset_map,
            offset_bias[:, None], kernel_mix,
        )
        if s:
            part = lax.ppermute(part, "slab", [(t, (t + s) % slabs) for t in range(slabs)])
        terms.append(part)

    cells_z = jnp.arange(GZ, dtype=jnp.int32)
    mode_freq = jnp.arange(mode_count, dtype=jnp.int32)
    z_turn = jnp.mod(cells_z[:, None] * mode_freq[None, :], GZ).astype(jnp.float32) * (
        2.0 * math.pi / GZ
    )
    z_table = jnp.stack([jnp.cos(z_turn), -jnp.sin(z_turn)], axis=1)
    table = (
        jnp.eye(kept, dtype=jnp.float32)[:, None, None, :, None] * z_table[None, :, :, None, :]
    ).reshape(kept * GZ, lanes)
    lift_rows = lift_weight.T.reshape(devices, kept, channels).swapaxes(0, 1).reshape(
        channels, channels
    )
    payload = lift_slots(terms, lift_rows, table, capacity, devices, slabs)
    recv = lax.all_to_all(
        payload.reshape(devices * slabs, 2 * slots, lanes), ("dp", "slab"), split_axis=0,
        concat_axis=0, tiled=True,
    ).reshape(payload.shape)

    signed = jnp.where(mode_freq < mode_count // 2, mode_freq, mode_freq - mode_count)
    grid_x = lax.dynamic_slice_in_dim(signed, slab_index * local_x, local_x)
    freqs = jnp.stack(
        [jnp.repeat(grid_x, mode_count), jnp.tile(signed, local_x)]
    ).astype(jnp.float32)
    order = ring_order(devices)[lax.axis_index("dp")]
    scale = 1.0 / math.sqrt(GZ * slabs * slabs * capacity)
    modes = sample_modes(order, recv, freqs, devices, slabs, slots, planes, scale, group)

    span = devices * mode_count
    pick_row = jnp.arange(group * devices, dtype=jnp.int32)[:, None]
    pick_col = jnp.arange(group * span, dtype=jnp.int32)[None, :]
    pick = (pick_row == pick_col // mode_count).astype(jnp.bfloat16)
    mask = (
        jnp.arange(lanes, dtype=jnp.int32)[:, None] % mode_count
        == jnp.arange(span, dtype=jnp.int32)[None, :] % mode_count
    ).astype(jnp.float32)
    result = None
    for c in range(chunks):
        result = grad_chunk(
            modes, pick, mask, gathered[c], kept, group, mode_count, c, chunks, result
        )
    return result.reshape(kept, local_x, mode_count, mode_count, width)


def solution(mesh):
    placed = (
        P("dp", "slab", None, None),
        P("dp", "slab", None, None),
        P("dp", "slab", None, None),
        P("dp", "slab", None, None),
        P("dp", "slab", None),
        P("dp", "slab", None, None, None),
        P(),
        P(),
        P(),
        P(),
    )
    return jax.shard_map(
        per_device,
        mesh=mesh,
        in_specs=placed,
        out_specs=P("dp", "slab", None, None, None),
        check_vma=False,
    )
```

profile of v0, /device:TPU:0, one launch (start us, length us, event | category | flops | bytes accessed | tf_op | source)
XLA Modules:
  0.0 123.1 jit_solution(9617514425626754487)
XLA Ops:
  7.1 10.8 %slot_terms.2 = f32[264,128]{1,0:T(8,128)S(1)} custom-call(s32[2]{0:T(128)S(1)} %pad_add_fusion.1.peer_ref, s32[2,4]{1,0:T(2,128)S(1)} %bitcast.46, s32[2,4]{1,0:T(2,128)S(1)} %bitcast.48, s32[2]{0:T(128)S(1)} %bitcast.50, f32[64]{0:T(128)S(1)} %slice_bitcast_fusion.zcoef_ref, bf16[4,64,128]{2,1,0:T(8,128)(2,1)S(1)} %bitcast.44, ...), custom_call_target="tpu_custom_call" | custom-call | flops 2147483648 | bytes 2097152 | tf_op jit(solution)/shard_map/slot_terms/pallas_call | solution.py:104
  17.9 3.0 %collective-permute-start = (f32[264,128]{1,0:T(8,128)S(1)}, f32[264,128]{1,0:T(8,128)S(1)}, u32[]{:S(2)}, u32[]{:S(2)}) collective-permute-start(f32[264,128]{1,0:T(8,128)S(1)} %slot_terms.2), channel_id=1, source_target_pairs={{0,1},{1,0},{2,3},{3,2},{4,5},{5,4},{6,7},{7,6},{8,9},{9,8},{10,11... | collective-permute-start | bytes 405512 | tf_op jit(solution)/shard_map/ppermute | solution.py:394
  21.1 1.5 %collective-permute-start.8 = (bf16[1024,128]{1,0:T(8,128)(2,1)S(1)}, bf16[1024,128]{1,0:T(8,128)(2,1)S(1)}, u32[]{:S(2)}, u32[]{:S(2)}) collective-permute-start(bf16[1024,128]{1,0:T(8,128)(2,1)S(1)} %bitcast.37), channel_id=1, source_target_pairs={{0,4},{2,6},{8,0},{10,2},{16,8},{18,10},{24,16},{26,18},{28,24},{3... | collective-permute-start | bytes 786440 | tf_op jit(solution)/shard_map/ppermute | solution.py:336
  23.2 1.5 %collective-permute-start.25 = (bf16[1024,128]{1,0:T(8,128)(2,1)S(1)}, bf16[1024,128]{1,0:T(8,128)(2,1)S(1)}, u32[]{:S(2)}, u32[]{:S(2)}) collective-permute-start(bf16[1024,128]{1,0:T(8,128)(2,1)S(1)} %bitcast.32), channel_id=1, source_target_pairs={{0,4},{2,6},{8,0},{10,2},{16,8},{18,10},{24,16},{26,18},{28,24},{3... | collective-permute-start | bytes 786440 | tf_op jit(solution)/shard_map/ppermute | solution.py:336
  24.7 1.6 %collective-permute-start.17 = (bf16[1024,128]{1,0:T(8,128)(2,1)S(1)}, bf16[1024,128]{1,0:T(8,128)(2,1)S(1)}, u32[]{:S(2)}, u32[]{:S(2)}) collective-permute-start(bf16[1024,128]{1,0:T(8,128)(2,1)S(1)} %bitcast.33), channel_id=1, source_target_pairs={{0,8},{2,10},{8,16},{10,18},{16,24},{18,26},{24,28},{26,30},{28,20... | collective-permute-start | bytes 786440 | tf_op jit(solution)/shard_map/ppermute | solution.py:333
  27.0 3.4 %collective-permute-done.8.refs_17_ = bf16[1024,128]{1,0:T(8,128)(2,1)S(1)} collective-permute-done((bf16[1024,128]{1,0:T(8,128)(2,1)S(1)}, bf16[1024,128]{1,0:T(8,128)(2,1)S(1)}, u32[]{:S(2)}, u32[]{:S(2)}) %collective-permute-start.8) | collective-permute-done | bytes 262176 | tf_op jit(solution)/shard_map/ppermute | solution.py:336
  30.4 1.5 %collective-permute-done.2.refs_5_ = bf16[1024,128]{1,0:T(8,128)(2,1)S(1)} collective-permute-done((bf16[1024,128]{1,0:T(8,128)(2,1)S(1)}, bf16[1024,128]{1,0:T(8,128)(2,1)S(1)}, u32[]{:S(2)}, u32[]{:S(2)}) %collective-permute-start.2) | collective-permute-done | bytes 262176 | tf_op jit(solution)/shard_map/ppermute | solution.py:333
  32.7 1.6 %collective-permute-start.9 = (bf16[1024,128]{1,0:T(8,128)(2,1)S(1)}, bf16[1024,128]{1,0:T(8,128)(2,1)S(1)}, u32[]{:S(2)}, u32[]{:S(2)}) collective-permute-start(bf16[1024,128]{1,0:T(8,128)(2,1)S(1)} %collective-permute-done.8.refs_17_), channel_id=1, source_target_pairs={{0,4},{2,6},{8,0},{10,2},{16,8},{18,10},{24,16},{26,18},{28,24},{3... | collective-permute-start | bytes 786440 | tf_op jit(solution)/shard_map/ppermute | solution.py:336
  34.6 1.6 %collective-permute-start.4 = (bf16[1024,128]{1,0:T(8,128)(2,1)S(1)}, bf16[1024,128]{1,0:T(8,128)(2,1)}, u32[]{:S(2)}, u32[]{:S(2)}) collective-permute-start(bf16[1024,128]{1,0:T(8,128)(2,1)S(1)} %collective-permute-done.2.refs_5_), channel_id=1, source_target_pairs={{0,8},{2,10},{8,16},{10,18},{16,24},{18,26},{24,28},{26,30},{28,20... | collective-permute-start | bytes 786440 | tf_op jit(solution)/shard_map/ppermute | solution.py:333
  36.1 1.6 %collective-permute-start.19 = (bf16[1024,128]{1,0:T(8,128)(2,1)S(1)}, bf16[1024,128]{1,0:T(8,128)(2,1)S(1)}, u32[]{:S(2)}, u32[]{:S(2)}) collective-permute-start(bf16[1024,128]{1,0:T(8,128)(2,1)S(1)} %collective-permute-done.17.refs_5_), channel_id=1, source_target_pairs={{0,8},{2,10},{8,16},{10,18},{16,24},{18,26},{24,28},{26,30},{28,20... | collective-permute-start | bytes 786440 | tf_op jit(solution)/shard_map/ppermute | solution.py:333
  41.3 1.6 %collective-permute-start.26 = (bf16[1024,128]{1,0:T(8,128)(2,1)S(1)}, bf16[1024,128]{1,0:T(8,128)(2,1)S(1)}, u32[]{:S(2)}, u32[]{:S(2)}) collective-permute-start(bf16[1024,128]{1,0:T(8,128)(2,1)S(1)} %collective-permute-done.25.refs_17_), channel_id=1, source_target_pairs={{0,4},{2,6},{8,0},{10,2},{16,8},{18,10},{24,16},{26,18},{28,24},{3... | collective-permute-start | bytes 786440 | tf_op jit(solution)/shard_map/ppermute | solution.py:336
  43.9 4.4 %collective-permute-done.19.refs_7_ = bf16[1024,128]{1,0:T(8,128)(2,1)S(1)} collective-permute-done((bf16[1024,128]{1,0:T(8,128)(2,1)S(1)}, bf16[1024,128]{1,0:T(8,128)(2,1)S(1)}, u32[]{:S(2)}, u32[]{:S(2)}) %collective-permute-start.19) | collective-permute-done | bytes 262176 | tf_op jit(solution)/shard_map/ppermute | solution.py:333
  49.3 1.5 %broadcast_multiply_fusion = f32[4,128,2,4,16]{1,0,4,3,2:T(4,128)} fusion(f32[128,2,16]{0,2,1:T(8,128)} %pad_maximum_fusion, f32[4,4]{0,1:T(4,128)} %fusion.11), kind=kLoop, calls=%fused_computation.3 | loop fusion | flops 65536 | bytes 278592 | tf_op jit(solution)/shard_map/mul | solution.py:404
  50.8 1.6 %collective-permute-start.27 = (bf16[1024,128]{1,0:T(8,128)(2,1)S(1)}, bf16[1024,128]{1,0:T(8,128)(2,1)}, u32[]{:S(2)}, u32[]{:S(2)}) collective-permute-start(bf16[1024,128]{1,0:T(8,128)(2,1)S(1)} %collective-permute-done.26.refs_15_), channel_id=1, source_target_pairs={{0,4},{2,6},{8,0},{10,2},{16,8},{18,10},{24,16},{26,18},{28,24},{3... | collective-permute-start | bytes 786440 | tf_op jit(solution)/shard_map/ppermute | solution.py:336
  52.5 1.6 %collective-permute-start.10 = (bf16[1024,128]{1,0:T(8,128)(2,1)}, bf16[1024,128]{1,0:T(8,128)(2,1)}, u32[]{:S(2)}, u32[]{:S(2)}) collective-permute-start(bf16[1024,128]{1,0:T(8,128)(2,1)} %copy-done.8), channel_id=1, source_target_pairs={{0,4},{2,6},{8,0},{10,2},{16,8},{18,10},{24,16},{26,18},{28,24},{3... | collective-permute-start | bytes 786440 | tf_op jit(solution)/shard_map/ppermute | solution.py:336
  59.2 1.7 %copy.30 = f32[16,8,4,128]{3,1,2,0:T(8,128)} copy(f32[16,8,4,128]{3,2,1,0:T(4,128)} %bitcast.52) | data formatting | bytes 524288
  67.5 10.8 %slot_terms.3.refs_1_ = f32[264,128]{1,0:T(8,128)S(1)} custom-call(s32[2]{0:T(128)S(1)} %copy-done.25, s32[2,4]{1,0:T(2,128)S(1)} %bitcast.47, s32[2,4]{1,0:T(2,128)S(1)} %bitcast.49, s32[2]{0:T(128)S(1)} %bitcast.51, f32[64]{0:T(128)S(1)} %copy-done.27, bf16[4,64,128]{2,1,0:T(8,128)(2,1)S(1)} %bitcast.45, bf16[4,3,128]{2,1,0:T(4,128)(2,1)S(1)} %bitcast.43, ...), custom_call_target="tpu_custom_call" | custom-call | flops 2147483648 | bytes 2097152 | tf_op jit(solution)/shard_map/slot_terms/pallas_call | solution.py:104
  78.4 1.4 %lift_slots.1 = f32[512,128]{1,0:T(8,128)} custom-call(f32[264,128]{1,0:T(8,128)S(1)} %collective-permute-done.refs_0_, f32[264,128]{1,0:T(8,128)S(1)} %slot_terms.3.refs_1_, bf16[64,64]{1,0:T(8,128)(2,1)S(1)} %bitcast.41, f32[512,128]{1,0:T(8,128)S(1)} %copy.26.refs_3_), custom_call_target="tpu_custom_call" | custom-call | flops 134217728 | bytes 1048576 | tf_op jit(solution)/shard_map/lift_slots/pallas_call | solution.py:179
  79.8 4.3 %all-to-all-start = ((f32[32,16,128]{2,1,0:T(8,128)}), f32[32,16,128]{2,1,0:T(8,128)S(1)}, u32[]{:S(2)}, u32[]{:S(2)}) async-start(f32[32,16,128]{2,1,0:T(8,128)} %bitcast.14), calls=%async_computation | async-start | bytes 524288 | tf_op jit(solution)/shard_map/all_to_all | solution.py:410
  84.7 1.8 %collective-permute-start.11 = (bf16[1024,128]{1,0:T(8,128)(2,1)}, bf16[1024,128]{1,0:T(8,128)(2,1)S(1)}, u32[]{:S(2)}, u32[]{:S(2)}) collective-permute-start(bf16[1024,128]{1,0:T(8,128)(2,1)} %collective-permute-done.10.refs_13_), channel_id=1, source_target_pairs={{0,4},{2,6},{8,0},{10,2},{16,8},{18,10},{24,16},{26,18},{28,24},{3... | collective-permute-start | bytes 786440 | tf_op jit(solution)/shard_map/ppermute | solution.py:336
  87.8 8.9 %collective-permute-done.11.refs_11_ = bf16[1024,128]{1,0:T(8,128)(2,1)S(1)} collective-permute-done((bf16[1024,128]{1,0:T(8,128)(2,1)}, bf16[1024,128]{1,0:T(8,128)(2,1)S(1)}, u32[]{:S(2)}, u32[]{:S(2)}) %collective-permute-start.11) | collective-permute-done | bytes 262176 | tf_op jit(solution)/shard_map/ppermute | solution.py:336
  100.2 7.2 %sample_modes.1.refs_0_ = bf16[16,128,128]{2,1,0:T(8,128)(2,1)S(1)} custom-call(s32[16]{0:T(128)S(1)} %dynamic-slice_bitcast_fusion.order_ref, f32[512,128]{1,0:T(8,128)S(1)} %bitcast.36, f32[2,128]{1,0:T(2,128)S(1)} %add_convert_fusion.freq_ref), custom_call_target="tpu_custom_call" | custom-call | flops 134217728 | bytes 1048576 | tf_op jit(solution)/shard_map/sample_modes/pallas_call | solution.py:239
  107.5 7.8 %grad_chunk.2.refs_19_ = f32[4,2048,128]{2,1,0:T(8,128)} custom-call(bf16[16,128,128]{2,1,0:T(8,128)(2,1)S(1)} %sample_modes.1.refs_0_, bf16[128,2048]{1,0:T(8,128)(2,1)S(1)} %fusion.refs_1_, f32[128,256]{1,0:T(8,128)S(1)} %compare_convert_fusion.refs_2_, bf16[1024,128]{1,0:T(8,128)(2,1)S(1)} %bitcast.35, ...), custom_call_target="tpu_custom_call" | custom-call | flops 1073741824 | bytes 6291456 | tf_op jit(solution)/shard_map/grad_chunk/pallas_call | solution.py:293
  115.3 7.8 %grad_chunk.3 = f32[4,2048,128]{2,1,0:T(8,128)} custom-call(bf16[16,128,128]{2,1,0:T(8,128)(2,1)S(1)} %sample_modes.1.refs_0_, bf16[128,2048]{1,0:T(8,128)(2,1)S(1)} %fusion.refs_1_, f32[128,256]{1,0:T(8,128)S(1)} %compare_convert_fusion.refs_2_, bf16[1024,128]{1,0:T(8,128)(2,1)S(1)} %bitcast.40, ...), custom_call_target="tpu_custom_call", output_to_operand_aliasing={{}: (19, {})} | custom-call | flops 1073741824 | bytes 6291456 | tf_op jit(solution)/shard_map/grad_chunk/pallas_call | solution.py:293
  (133 shorter events, 32.3 us)
Async XLA Ops:
  21.1 9.3 %collective-permute-start.8 = (bf16[1024,128]{1,0:T(8,128)(2,1)S(1)}, bf16[1024,128]{1,0:T(8,128)(2,1)S(1)}, u32[]{:S(2)}, u32[]{:S(2)}) collective-permute-start(bf16[1024,128]{1,0:T(8,128)(2,1)S(1)} %bitcast.37), channel_id=1, source_target_pairs={{0,4},{2,6},{8,0},{10,2},{16,8},{18,10},{24,16},{26,18},{28,24},{3... | collective-permute-start | bytes 786440 | tf_op jit(solution)/shard_map/ppermute | solution.py:336
  23.2 11.3 %collective-permute-start.25 = (bf16[1024,128]{1,0:T(8,128)(2,1)S(1)}, bf16[1024,128]{1,0:T(8,128)(2,1)S(1)}, u32[]{:S(2)}, u32[]{:S(2)}) collective-permute-start(bf16[1024,128]{1,0:T(8,128)(2,1)S(1)} %bitcast.32), channel_id=1, source_target_pairs={{0,4},{2,6},{8,0},{10,2},{16,8},{18,10},{24,16},{26,18},{28,24},{3... | collective-permute-start | bytes 786440 | tf_op jit(solution)/shard_map/ppermute | solution.py:336
  24.7 11.4 %collective-permute-start.17 = (bf16[1024,128]{1,0:T(8,128)(2,1)S(1)}, bf16[1024,128]{1,0:T(8,128)(2,1)S(1)}, u32[]{:S(2)}, u32[]{:S(2)}) collective-permute-start(bf16[1024,128]{1,0:T(8,128)(2,1)S(1)} %bitcast.33), channel_id=1, source_target_pairs={{0,8},{2,10},{8,16},{10,18},{16,24},{18,26},{24,28},{26,30},{28,20... | collective-permute-start | bytes 786440 | tf_op jit(solution)/shard_map/ppermute | solution.py:333
  34.6 9.3 %collective-permute-start.4 = (bf16[1024,128]{1,0:T(8,128)(2,1)S(1)}, bf16[1024,128]{1,0:T(8,128)(2,1)}, u32[]{:S(2)}, u32[]{:S(2)}) collective-permute-start(bf16[1024,128]{1,0:T(8,128)(2,1)S(1)} %collective-permute-done.2.refs_5_), channel_id=1, source_target_pairs={{0,8},{2,10},{8,16},{10,18},{16,24},{18,26},{24,28},{26,30},{28,20... | collective-permute-start | bytes 786440 | tf_op jit(solution)/shard_map/ppermute | solution.py:333
  36.1 12.1 %collective-permute-start.19 = (bf16[1024,128]{1,0:T(8,128)(2,1)S(1)}, bf16[1024,128]{1,0:T(8,128)(2,1)S(1)}, u32[]{:S(2)}, u32[]{:S(2)}) collective-permute-start(bf16[1024,128]{1,0:T(8,128)(2,1)S(1)} %collective-permute-done.17.refs_5_), channel_id=1, source_target_pairs={{0,8},{2,10},{8,16},{10,18},{16,24},{18,26},{24,28},{26,30},{28,20... | collective-permute-start | bytes 786440 | tf_op jit(solution)/shard_map/ppermute | solution.py:333
  38.9 11.9 %collective-permute-start.3 = (bf16[1024,128]{1,0:T(8,128)(2,1)S(1)}, bf16[1024,128]{1,0:T(8,128)(2,1)}, u32[]{:S(2)}, u32[]{:S(2)}) collective-permute-start(bf16[1024,128]{1,0:T(8,128)(2,1)S(1)} %collective-permute-done.2.refs_5_), channel_id=1, source_target_pairs={{0,2},{2,0},{4,6},{6,4},{8,10},{10,8},{12,14},{14,12},{16,18},{18,... | collective-permute-start | bytes 786440 | tf_op jit(solution)/shard_map/ppermute | solution.py:340
  39.6 12.8 %collective-permute-start.30 = (bf16[1024,128]{1,0:T(8,128)(2,1)S(1)}, bf16[1024,128]{1,0:T(8,128)(2,1)S(1)}, u32[]{:S(2)}, u32[]{:S(2)}) collective-permute-start(bf16[1024,128]{1,0:T(8,128)(2,1)S(1)} %collective-permute-done.25.refs_17_), channel_id=1, source_target_pairs={{0,2},{2,0},{4,6},{6,4},{8,10},{10,8},{12,14},{14,12},{16,18},{18,... | collective-permute-start | bytes 786440 | tf_op jit(solution)/shard_map/ppermute | solution.py:340
  41.3 9.5 %collective-permute-start.26 = (bf16[1024,128]{1,0:T(8,128)(2,1)S(1)}, bf16[1024,128]{1,0:T(8,128)(2,1)S(1)}, u32[]{:S(2)}, u32[]{:S(2)}) collective-permute-start(bf16[1024,128]{1,0:T(8,128)(2,1)S(1)} %collective-permute-done.25.refs_17_), channel_id=1, source_target_pairs={{0,4},{2,6},{8,0},{10,2},{16,8},{18,10},{24,16},{26,18},{28,24},{3... | collective-permute-start | bytes 786440 | tf_op jit(solution)/shard_map/ppermute | solution.py:336
  43.8 10.2 %collective-permute-start.18 = (bf16[1024,128]{1,0:T(8,128)(2,1)S(1)}, bf16[1024,128]{1,0:T(8,128)(2,1)S(1)}, u32[]{:S(2)}, u32[]{:S(2)}) collective-permute-start(bf16[1024,128]{1,0:T(8,128)(2,1)S(1)} %collective-permute-done.17.refs_5_), channel_id=1, source_target_pairs={{0,2},{2,0},{4,6},{6,4},{8,10},{10,8},{12,14},{14,12},{16,18},{18,... | collective-permute-start | bytes 786440 | tf_op jit(solution)/shard_map/ppermute | solution.py:340
  50.8 33.8 %collective-permute-start.29 = (bf16[1024,128]{1,0:T(8,128)(2,1)S(1)}, bf16[1024,128]{1,0:T(8,128)(2,1)}, u32[]{:S(2)}, u32[]{:S(2)}) collective-permute-start(bf16[1024,128]{1,0:T(8,128)(2,1)S(1)} %collective-permute-done.26.refs_15_), channel_id=1, source_target_pairs={{0,2},{2,0},{4,6},{6,4},{8,10},{10,8},{12,14},{14,12},{16,18},{18,... | collective-permute-start | bytes 786440 | tf_op jit(solution)/shard_map/ppermute | solution.py:340
  50.8 35.6 %collective-permute-start.27 = (bf16[1024,128]{1,0:T(8,128)(2,1)S(1)}, bf16[1024,128]{1,0:T(8,128)(2,1)}, u32[]{:S(2)}, u32[]{:S(2)}) collective-permute-start(bf16[1024,128]{1,0:T(8,128)(2,1)S(1)} %collective-permute-done.26.refs_15_), channel_id=1, source_target_pairs={{0,4},{2,6},{8,0},{10,2},{16,8},{18,10},{24,16},{26,18},{28,24},{3... | collective-permute-start | bytes 786440 | tf_op jit(solution)/shard_map/ppermute | solution.py:336
  52.5 31.6 %collective-permute-start.10 = (bf16[1024,128]{1,0:T(8,128)(2,1)}, bf16[1024,128]{1,0:T(8,128)(2,1)}, u32[]{:S(2)}, u32[]{:S(2)}) collective-permute-start(bf16[1024,128]{1,0:T(8,128)(2,1)} %copy-done.8), channel_id=1, source_target_pairs={{0,4},{2,6},{8,0},{10,2},{16,8},{18,10},{24,16},{26,18},{28,24},{3... | collective-permute-start | bytes 786440 | tf_op jit(solution)/shard_map/ppermute | solution.py:336
  54.1 30.3 %collective-permute-start.6 = (bf16[1024,128]{1,0:T(8,128)(2,1)}, bf16[1024,128]{1,0:T(8,128)(2,1)}, u32[]{:S(2)}, u32[]{:S(2)}) collective-permute-start(bf16[1024,128]{1,0:T(8,128)(2,1)} %collective-permute-done.4.refs_7_), channel_id=1, source_target_pairs={{0,8},{2,10},{8,16},{10,18},{16,24},{18,26},{24,28},{26,30},{28,20... | collective-permute-start | bytes 786440 | tf_op jit(solution)/shard_map/ppermute | solution.py:333
  55.6 30.9 %collective-permute-start.23 = (bf16[1024,128]{1,0:T(8,128)(2,1)}, bf16[1024,128]{1,0:T(8,128)(2,1)}, u32[]{:S(2)}, u32[]{:S(2)}) collective-permute-start(bf16[1024,128]{1,0:T(8,128)(2,1)} %collective-permute-done.21.refs_9_), channel_id=1, source_target_pairs={{0,8},{2,10},{8,16},{10,18},{16,24},{18,26},{24,28},{26,30},{28,20... | collective-permute-start | bytes 786440 | tf_op jit(solution)/shard_map/ppermute | solution.py:333
  79.8 20.4 %all-to-all-start = ((f32[32,16,128]{2,1,0:T(8,128)}), f32[32,16,128]{2,1,0:T(8,128)S(1)}, u32[]{:S(2)}, u32[]{:S(2)}) async-start(f32[32,16,128]{2,1,0:T(8,128)} %bitcast.14), calls=%async_computation | async-start | bytes 524288 | tf_op jit(solution)/shard_map/all_to_all | solution.py:410
  84.4 12.9 %collective-permute-start.22 = (bf16[1024,128]{1,0:T(8,128)(2,1)}, bf16[1024,128]{1,0:T(8,128)(2,1)}, u32[]{:S(2)}, u32[]{:S(2)}) collective-permute-start(bf16[1024,128]{1,0:T(8,128)(2,1)} %collective-permute-done.21.refs_9_), channel_id=1, source_target_pairs={{0,2},{2,0},{4,6},{6,4},{8,10},{10,8},{12,14},{14,12},{16,18},{18,... | collective-permute-start | bytes 786440 | tf_op jit(solution)/shard_map/ppermute | solution.py:340
  84.7 12.1 %collective-permute-start.11 = (bf16[1024,128]{1,0:T(8,128)(2,1)}, bf16[1024,128]{1,0:T(8,128)(2,1)S(1)}, u32[]{:S(2)}, u32[]{:S(2)}) collective-permute-start(bf16[1024,128]{1,0:T(8,128)(2,1)} %collective-permute-done.10.refs_13_), channel_id=1, source_target_pairs={{0,4},{2,6},{8,0},{10,2},{16,8},{18,10},{24,16},{26,18},{28,24},{3... | collective-permute-start | bytes 786440 | tf_op jit(solution)/shard_map/ppermute | solution.py:336
  86.4 10.3 %collective-permute-start.28 = (bf16[1024,128]{1,0:T(8,128)(2,1)}, bf16[1024,128]{1,0:T(8,128)(2,1)}, u32[]{:S(2)}, u32[]{:S(2)}) collective-permute-start(bf16[1024,128]{1,0:T(8,128)(2,1)} %collective-permute-done.27.refs_13_), channel_id=1, source_target_pairs={{0,2},{2,0},{4,6},{6,4},{8,10},{10,8},{12,14},{14,12},{16,18},{18,... | collective-permute-start | bytes 786440 | tf_op jit(solution)/shard_map/ppermute | solution.py:340
  86.4 10.9 %collective-permute-start.24 = (bf16[1024,128]{1,0:T(8,128)(2,1)}, bf16[1024,128]{1,0:T(8,128)(2,1)}, u32[]{:S(2)}, u32[]{:S(2)}) collective-permute-start(bf16[1024,128]{1,0:T(8,128)(2,1)} %collective-permute-done.23.refs_11_), channel_id=1, source_target_pairs={{0,2},{2,0},{4,6},{6,4},{8,10},{10,8},{12,14},{14,12},{16,18},{18,... | collective-permute-start | bytes 786440 | tf_op jit(solution)/shard_map/ppermute | solution.py:340
  87.7 27.5 %collective-permute-start.14 = (bf16[1024,128]{1,0:T(8,128)(2,1)}, bf16[1024,128]{1,0:T(8,128)(2,1)}, u32[]{:S(2)}, u32[]{:S(2)}) collective-permute-start(bf16[1024,128]{1,0:T(8,128)(2,1)} %copy-done.8), channel_id=1, source_target_pairs={{0,2},{2,0},{4,6},{6,4},{8,10},{10,8},{12,14},{14,12},{16,18},{18,... | collective-permute-start | bytes 786440 | tf_op jit(solution)/shard_map/ppermute | solution.py:340
  96.8 18.5 %collective-permute-start.5 = (bf16[1024,128]{1,0:T(8,128)(2,1)}, bf16[1024,128]{1,0:T(8,128)(2,1)}, u32[]{:S(2)}, u32[]{:S(2)}) collective-permute-start(bf16[1024,128]{1,0:T(8,128)(2,1)} %collective-permute-done.4.refs_7_), channel_id=1, source_target_pairs={{0,2},{2,0},{4,6},{6,4},{8,10},{10,8},{12,14},{14,12},{16,18},{18,... | collective-permute-start | bytes 786440 | tf_op jit(solution)/shard_map/ppermute | solution.py:340
  96.8 18.5 %collective-permute-start.13 = (bf16[1024,128]{1,0:T(8,128)(2,1)}, bf16[1024,128]{1,0:T(8,128)(2,1)}, u32[]{:S(2)}, u32[]{:S(2)}) collective-permute-start(bf16[1024,128]{1,0:T(8,128)(2,1)} %collective-permute-done.10.refs_13_), channel_id=1, source_target_pairs={{0,2},{2,0},{4,6},{6,4},{8,10},{10,8},{12,14},{14,12},{16,18},{18,... | collective-permute-start | bytes 786440 | tf_op jit(solution)/shard_map/ppermute | solution.py:340
  97.3 18.0 %collective-permute-start.7 = (bf16[1024,128]{1,0:T(8,128)(2,1)}, bf16[1024,128]{1,0:T(8,128)(2,1)}, u32[]{:S(2)}, u32[]{:S(2)}) collective-permute-start(bf16[1024,128]{1,0:T(8,128)(2,1)} %collective-permute-done.6.refs_9_), channel_id=1, source_target_pairs={{0,2},{2,0},{4,6},{6,4},{8,10},{10,8},{12,14},{14,12},{16,18},{18,... | collective-permute-start | bytes 786440 | tf_op jit(solution)/shard_map/ppermute | solution.py:340
  97.4 17.9 %collective-permute-start.12 = (bf16[1024,128]{1,0:T(8,128)(2,1)S(1)}, bf16[1024,128]{1,0:T(8,128)(2,1)}, u32[]{:S(2)}, u32[]{:S(2)}) collective-permute-start(bf16[1024,128]{1,0:T(8,128)(2,1)S(1)} %collective-permute-done.11.refs_11_), channel_id=1, source_target_pairs={{0,2},{2,0},{4,6},{6,4},{8,10},{10,8},{12,14},{14,12},{16,18},{18,... | collective-permute-start | bytes 786440 | tf_op jit(solution)/shard_map/ppermute | solution.py:340
  (37 other events, 365.0 us)
where the time goes:
time: 125 us; the launch traced here: 123 us
  Pallas kernels  45.9 us (37%)
  starting transfers between devices  27.6 us (22%)
  local copies, waits for them, and re-layouts  21.8 us (17%)
  waiting for transfers between devices  21.8 us (17%)
  other arithmetic  5.55 us (4%)
    pallas_call x2, Pallas kernels, slot_terms(): pl.pallas_call(slot_kernel, out_shape=jax.ShapeDtypeStruct((width + 8, GZ...  21.7 us
    unnamed x62, local copies, waits for them, and re-layouts  15.6 us
    pallas_call x2, Pallas kernels, grad_chunk(): pl.pallas_call(functools.partial(grad_kernel, samples, group, depth, int(...  15.6 us
    ppermute x7, waiting for transfers between devices, gather_chunk(): down = lax.ppermute(down, 'dp', ring_perm(chips, -1))  13.9 us
    ppermute x7, starting transfers between devices, gather_chunk(): down = lax.ppermute(down, 'dp', ring_perm(chips, -1))  11.1 us
    ppermute x7, waiting for transfers between devices, gather_chunk(): up = lax.ppermute(up, 'dp', ring_perm(chips, 1))  7.9 us
    pallas_call x1, Pallas kernels, sample_modes(): pl.pallas_call(functools.partial(modes_kernel, samples, slabs, slots, pla...  7.21 us
    ppermute x7, starting transfers between devices, gather_chunk(): up = lax.ppermute(up, 'dp', ring_perm(chips, 1))  6.46 us
  transfers between devices with their start and end apart: 32, of which 8 were waited for; matrix products, arithmetic and copies ran while one was open for 11% of the time, Pallas kernels for 22%

commit v1 on v0

v1 whole, which is shorter than its diff:
```python
import functools
import math

import jax
import jax.numpy as jnp
from jax import lax
from jax.experimental import pallas as pl
from jax.experimental.pallas import tpu as pltpu
from jax.sharding import PartitionSpec as P

GX = 128
GY = 128
GZ = 128
MIB = 1024 * 1024


def in_hbm(*arrays):
    return [pltpu.with_memory_space_constraint(a, pltpu.HBM) for a in arrays]


def work(micros):
    return pl.CostEstimate(flops=int(micros * 10**9), bytes_accessed=1024, transcendentals=0)


HIGH = lax.Precision.HIGHEST
ROWS0 = (((0,), (0,)), ((), ()))


def slot_kernel(slabs, planes, block_hbm, cell_hbm, count_hbm, feats_hbm, coords_hbm, map_hbm, bias_hbm, mix_hbm, after_hbm, *refs):
    del after_hbm
    outs = refs[:slabs]
    (block_ref, cell_ref, count_ref, feats_ref, coords_ref, map_ref, bias_ref, mix_ref, list_ref,
     turned_ref, mixed_ref, part_ref, coef_ref, flat_ref, acc_ref, spot_ref, sems) = refs[slabs:]
    me = lax.axis_index("slab")
    pairs = [(block_hbm, block_ref), (cell_hbm, cell_ref), (count_hbm, count_ref), (feats_hbm, feats_ref),
             (coords_hbm, coords_ref), (map_hbm, map_ref), (bias_hbm, bias_ref), (mix_hbm, mix_ref)]
    copies = [pltpu.make_async_copy(a, b, sems.at[i]) for i, (a, b) in enumerate(pairs)]
    for c in copies: c.start()
    capacity = block_ref.shape[1]
    blocks, channels, points = feats_ref.shape
    hidden = mix_ref.shape[0]
    width = blocks * channels
    base = capacity * channels + 8
    row8 = lax.broadcasted_iota(jnp.int32, (8, points), 0)
    pos_z = (lax.broadcasted_iota(jnp.int32, (GZ, points), 0).astype(jnp.float32) + 0.5) * (1.0 / GZ)
    for c in copies[:7]: c.wait()
    spot_ref[...] = coords_ref[...].astype(jnp.float32)
    for b in range(blocks):
        turned_ref[:, b * channels : (b + 1) * channels] = feats_ref[b].astype(jnp.float32).T.astype(jnp.bfloat16)
    cat = jnp.concatenate([map_ref[...], bias_ref[...], jnp.zeros((4, hidden), jnp.float32)], axis=0)
    coef_ref[...] = lax.dot_general(cat, jnp.where(row8 == 2, 1.0, 0.0), ROWS0, precision=HIGH, preferred_element_type=jnp.float32)
    live = jnp.int32(0)
    for r in range(slabs):
        peer = lax.rem(me + r, slabs)
        tag_rows = jnp.full((8, points), -1.0, jnp.float32)
        for j in range(capacity):
            n = r * capacity + j
            block = block_ref[peer, j]
            cell = cell_ref[peer, j]
            alive = j < count_ref[peer]
            @pl.when(alive)
            def _():
                list_ref[live] = n
                list_ref[live + 1] = n
            live = live + alive.astype(jnp.int32)
            list_ref[slabs * capacity + 1 + n] = block
            pos_x = ((peer * planes + lax.div(cell, GY)).astype(jnp.float32) + 0.5) * (1.0 / GX)
            pos_y = (lax.rem(cell, GY).astype(jnp.float32) + 0.5) * (1.0 / GY)
            q0 = spot_ref[0, pl.ds(block, 1), :]
            q1 = spot_ref[1, pl.ds(block, 1), :]
            q2 = spot_ref[2, pl.ds(block, 1), :]
            side = jnp.where(row8 == 0, pos_x - q0, jnp.where(row8 == 1, pos_y - q1, jnp.where(row8 == 2, -q2, jnp.where(row8 == 3, 1.0, 0.0))))
            part_ref[n] = lax.dot_general(cat, side, ROWS0, precision=HIGH, preferred_element_type=jnp.float32)
            tag_rows = jnp.where(row8 == j, jnp.where(alive, cell, -1).astype(jnp.float32), tag_rows)
        flat_ref[r * base + capacity * channels : (r + 1) * base, :] = tag_rows
    copies[7].wait()
    lane = lax.broadcasted_iota(jnp.int32, (channels, 2 * channels), 1)
    left = turned_ref[...]

    step = max(1, min(hidden // 2, 512 // (blocks * blocks)))

    def mix_step(it, carry):
        for u in range(step):
            h = it * step + u
            mix = mix_ref[h]
            wide = jnp.concatenate([mix, mix], axis=1)
            zero = jnp.zeros_like(wide)
            halves = (jnp.where(lane < channels, wide, zero), jnp.where(lane < channels, zero, wide))
            rows = [jnp.concatenate([halves[b % 2] if b // 2 == t else zero for t in range(blocks // 2)], axis=1) for b in range(blocks)]
            mixed_ref[pl.ds(pl.multiple_of(h * points, points), points), :] = jnp.dot(left, jnp.concatenate(rows, axis=0), preferred_element_type=jnp.float32).astype(jnp.bfloat16)
        return carry
    lax.fori_loop(0, hidden // step, mix_step, 0)

    def pair(it, carry):
        ids = [list_ref[2 * it], list_ref[2 * it + 1]]
        part = 8
        for k in range(0, hidden, part):
            cols = []
            for h in range(k, k + part):
                cell_z = pos_z * coef_ref[h : h + 1, :]
                cols.append(jnp.concatenate([jnp.maximum(cell_z + part_ref[n, h : h + 1, :], 0.0).astype(jnp.bfloat16) for n in ids], axis=0))
            got = jnp.dot(jnp.concatenate(cols, axis=1), mixed_ref[k * points : (k + part) * points, :], preferred_element_type=jnp.float32)
            if k: acc_ref[...] += got
            else: acc_ref[...] = got
        for j, n in enumerate(ids):
            block = list_ref[slabs * capacity + 1 + n]
            pick = acc_ref[j * GZ : (j + 1) * GZ, : 2 * channels]
            for t in range(1, blocks // 2):
                pick = jnp.where(block // 2 == t, acc_ref[j * GZ : (j + 1) * GZ, 2 * t * channels : 2 * (t + 1) * channels], pick)
            turned = pick.T * (1.0 / points)
            start = pl.multiple_of((n // capacity) * base + (n % capacity) * channels, 8)
            flat_ref[pl.ds(start, channels), :] = jnp.where(block % 2 == 1, turned[channels:], turned[:channels])
        return carry
    lax.fori_loop(0, (live + 1) // 2, pair, 0)
    for r in range(slabs):
        outs[r][...] = flat_ref[r * base : (r + 1) * base, :]

def slot_terms(slot_block, slot_cell, slot_count, feats, coords, offset_map, offset_bias, kernel_mix, planes, after):
    slabs, capacity = slot_block.shape
    blocks, channels, points = feats.shape
    hidden = kernel_mix.shape[0]
    base = capacity * channels + 8
    slots = slabs * capacity
    width = blocks * channels
    slot_limit = hidden * points * width * 2 + 16 * MIB
    hbm = pl.BlockSpec(memory_space=pltpu.HBM)
    vmem = pl.BlockSpec(memory_space=pltpu.VMEM)
    return pl.pallas_call(
        functools.partial(slot_kernel, slabs, planes),
        out_shape=[jax.ShapeDtypeStruct((base, GZ), jnp.float32)] * slabs,
        in_specs=[hbm] * 8 + [pl.BlockSpec(memory_space=pl.ANY)],
        out_specs=[vmem] * slabs,
        scratch_shapes=[
            pltpu.SMEM((slabs, capacity), jnp.int32), pltpu.SMEM((slabs, capacity), jnp.int32), pltpu.SMEM((slabs,), jnp.int32),
            pltpu.VMEM(feats.shape, feats.dtype), pltpu.VMEM(coords.shape, coords.dtype), pltpu.VMEM(offset_map.shape, jnp.float32),
            pltpu.VMEM(offset_bias.shape, jnp.float32), pltpu.VMEM(kernel_mix.shape, kernel_mix.dtype),
            pltpu.SMEM((2 * slots + 2,), jnp.int32),
            pltpu.VMEM((points, width), jnp.bfloat16), pltpu.VMEM((hidden * points, width), jnp.bfloat16),
            pltpu.VMEM((slots, hidden, points), jnp.float32), pltpu.VMEM((hidden, points), jnp.float32),
            pltpu.VMEM((slabs * base, GZ), jnp.float32), pltpu.VMEM((2 * GZ, width), jnp.float32), pltpu.VMEM(coords.shape, jnp.float32),
            pltpu.SemaphoreType.DMA((8,)),
        ],
        compiler_params=pltpu.CompilerParams(vmem_limit_bytes=slot_limit),
        cost_estimate=work(1),
        name="slot_terms",
    )(*in_hbm(slot_block, slot_cell, slot_count, feats, coords, offset_map, offset_bias, kernel_mix),
      after)


def lift_kernel(groups, capacity, dests, copies, mode_count, *refs):
    terms = refs[:groups]
    lift_ref, out_ref, tag_ref, row_ref, wide_ref, table_ref = refs[groups:]
    channels = lift_ref.shape[0]
    kept = channels // dests
    slots = groups * capacity
    lanes = table_ref.shape[1]
    tiles = lanes // GZ
    per = (tiles + 1) * slots
    cells = lax.broadcasted_iota(jnp.int32, (GZ, lanes), 0)
    lane = lax.broadcasted_iota(jnp.int32, (GZ, lanes), 1)
    step = cells * (lane % mode_count) + jnp.where(lane >= lanes // 2, GZ // 4, 0)
    waves = jnp.cos((step % GZ).astype(jnp.float32) * (2.0 * math.pi / GZ))
    for i in range(kept):
        mine = lane // mode_count % kept == i
        table_ref[i * GZ : (i + 1) * GZ, :] = jnp.where(mine, waves, 0.0)

    def tag_of(m):
        base = capacity * channels + m % capacity
        return terms[m // capacity][base : base + 1, :]

    def terms_of(m):
        base = (m % capacity) * channels
        return terms[m // capacity][base : base + channels, :]

    for n in range(slots):
        tag = tag_of(n)
        live = tag >= 0.0
        summed = jnp.zeros((channels, GZ), jnp.float32)
        leader = live
        for m in range(slots):
            same = (tag_of(m) == tag) & live
            summed = summed + jnp.where(same, terms_of(m), 0.0)
            if m < n:
                leader = leader & jnp.logical_not(same)
        latent = summed.astype(jnp.bfloat16)
        lifted = jax.nn.gelu(
            lax.dot_general(lift_ref[...], latent, ROWS0, preferred_element_type=jnp.float32)
        )
        row_ref[n] = jnp.where(leader, lifted, 0.0)
        for i in range(kept):
            wide_ref[n * dests : (n + 1) * dests, i * GZ : (i + 1) * GZ] = row_ref[
                n, pl.ds(i, dests, stride=kept), :
            ]
        tag_ref[n : n + 1, :] = tag
    modes = jnp.dot(
        wide_ref[...], table_ref[...], precision=HIGH, preferred_element_type=jnp.float32
    )
    for n in range(slots):
        piece = modes[n * dests : (n + 1) * dests, :]
        for t in range(copies):
            for u in range(tiles):
                out_ref[pl.ds(t * per + u * slots + n, dests, stride=copies * per), :] = piece[
                    :, u * GZ : (u + 1) * GZ
                ]
    for d in range(dests * copies):
        out_ref[d * per + tiles * slots : (d + 1) * per, :] = tag_ref[...]


def lift_slots(terms, lift_weight, capacity, dests, copies, mode_count):
    groups = len(terms)
    channels = lift_weight.shape[0]
    slots = groups * capacity
    kept = channels // dests
    lanes = 2 * kept * mode_count
    vmem = pl.BlockSpec(memory_space=pltpu.VMEM)
    return pl.pallas_call(
        functools.partial(lift_kernel, groups, capacity, dests, copies, mode_count),
        out_shape=jax.ShapeDtypeStruct((dests * copies * (lanes // GZ + 1) * slots, GZ), jnp.float32),
        in_specs=[vmem] * (groups + 1),
        out_specs=vmem,
        scratch_shapes=[
            pltpu.VMEM((slots, GZ), jnp.float32),
            pltpu.VMEM((slots, channels, GZ), jnp.float32),
            pltpu.VMEM((slots * dests, kept * GZ), jnp.float32),
            pltpu.VMEM((kept * GZ, lanes), jnp.float32),
        ],
        compiler_params=pltpu.CompilerParams(vmem_limit_bytes=16 * MIB),
        cost_estimate=work(0.1),
        name="lift_slots",
    )(*terms, lift_weight)


def modes_kernel(samples, slabs, slots, planes, scale, group, mode_count, recv_ref, out_ref,
                 all_ref):
    tiles = all_ref.shape[0]
    total = all_ref.shape[1] // samples
    half = tiles * GZ // 2
    per = (tiles + 1) * slots
    device = lax.axis_index("dp")
    first_x = (lax.axis_index("slab") * 2 + lax.rem(device, 2)) * (total // mode_count)
    spot = lax.broadcasted_iota(jnp.int32, (1, total), 1)
    freq_x = first_x + spot // mode_count
    freq_y = spot % mode_count
    freq_x = jnp.where(freq_x < mode_count // 2, freq_x, freq_x - mode_count).astype(jnp.float32)
    freq_y = jnp.where(freq_y < mode_count // 2, freq_y, freq_y - mode_count).astype(jnp.float32)

    def body(q, carry):
        sample = ring_sample(device, q, samples)
        waves, values = [], []
        for t in range(slabs):
            base = pl.multiple_of((sample * slabs + t) * per, 8)
            piece = jnp.concatenate(
                [recv_ref[pl.ds(base + u * slots, slots), :] for u in range(tiles)], axis=1
            )
            tag = jnp.maximum(recv_ref[pl.ds(base + tiles * slots, slots), :][:, 0:1], 0.0)
            local_x = jnp.floor(tag * (1.0 / GY))
            turns = (local_x + t * planes) * (1.0 / GX) * freq_x + (
                tag - local_x * GY
            ) * (1.0 / GY) * freq_y
            values.append(piece)
            waves.append((turns - jnp.floor(turns)) * (2.0 * math.pi))
        angle = jnp.concatenate(waves, axis=0)
        plain = jnp.concatenate(values, axis=0)
        crossed = jnp.concatenate([plain[:, half:], -plain[:, :half]], axis=1)
        modes = lax.dot_general(
            jnp.concatenate([jnp.cos(angle), jnp.sin(angle)], axis=0),
            jnp.concatenate([plain, crossed], axis=0),
            ROWS0,
            precision=HIGH,
            preferred_element_type=jnp.float32,
        )
        for u in range(tiles):
            all_ref[u, pl.ds(q, total, stride=samples), :] = (
                modes[:, u * GZ : (u + 1) * GZ] * scale
            )
        return carry

    lax.fori_loop(0, samples, body, 0, unroll=4)
    span = group * samples
    for block in range(total // group):
        for u in range(tiles):
            out_ref[block, u * GZ : (u + 1) * GZ, :] = all_ref[
                u, block * span : (block + 1) * span, :
            ].T.astype(jnp.bfloat16)


def sample_modes(recv, samples, slabs, slots, planes, scale, group, total, mode_count, lanes):
    vmem = pl.BlockSpec(memory_space=pltpu.VMEM)
    return pl.pallas_call(
        functools.partial(
            modes_kernel, samples, slabs, slots, planes, scale, group, mode_count
        ),
        out_shape=jax.ShapeDtypeStruct((total // group, lanes, group * samples), jnp.bfloat16),
        in_specs=[vmem],
        out_specs=vmem,
        scratch_shapes=[pltpu.VMEM((lanes // GZ, total * samples, GZ), jnp.float32)],
        compiler_params=pltpu.CompilerParams(vmem_limit_bytes=16 * MIB),
        cost_estimate=work(0.2),
        name="sample_modes",
    )(recv)


def grad_kernel(samples, group, depth, aliased, core_ref, modes_ref, *refs):
    rows_refs = refs[:samples]
    own_ref, other_ref, pick_ref, mask_ref = refs[samples + aliased :]
    lanes = modes_ref.shape[1]
    half_rows = lanes // 2
    kept = own_ref.shape[0]
    half = own_ref.shape[2] // 2
    span = samples * depth
    first = core_ref[0] == 0

    @pl.when(pl.program_id(0) == 0)
    def _():
        row = lax.broadcasted_iota(jnp.int32, pick_ref.shape, 0)
        col = lax.broadcasted_iota(jnp.int32, pick_ref.shape, 1)
        pick_ref[...] = jnp.where(row == col // depth, 1.0, 0.0).astype(jnp.bfloat16)
        row = lax.broadcasted_iota(jnp.int32, mask_ref.shape, 0)
        col = lax.broadcasted_iota(jnp.int32, mask_ref.shape, 1)
        mask_ref[...] = jnp.where(row % depth == col % depth, 1.0, 0.0)

    lefts = []
    for block in range(modes_ref.shape[0]):
        modes = modes_ref[block]
        for g in range(group):
            left = jnp.dot(
                modes, pick_ref[:, g * span : (g + 1) * span], preferred_element_type=jnp.float32
            )
            lefts.append((left * mask_ref[...]).astype(jnp.bfloat16))
    for g, left in enumerate(lefts):
        spot = slice(g * depth, (g + 1) * depth)
        right = jnp.concatenate([r[spot, :] for r in rows_refs], axis=0)
        both = jnp.dot(left, right, preferred_element_type=jnp.float32)
        plain, turned = both[:half_rows], both[half_rows:]
        total = plain + jnp.concatenate([turned[:, half:], -turned[:, :half]], axis=1)
        low, high = total[: half_rows // 2], total[half_rows // 2 :]
        own, other = jnp.where(first, low, high), jnp.where(first, high, low)
        for i in range(kept):
            own_ref[i, spot, :] = own[i * depth : (i + 1) * depth]
            other_ref[i, spot, :] = other[i * depth : (i + 1) * depth]


def grad_chunk(core, modes, rows, kept, group, depth, chunk, chunks, previous):
    samples = len(rows)
    lanes = modes.shape[1]
    total_rows, width = rows[0].shape
    size = total_rows // chunks
    blocks = min(2, size // (group * depth))
    tile = blocks * group * depth
    steps = size // tile
    in_specs = [
        pl.BlockSpec((blocks, lanes, group * samples), lambda s, c: (chunk * steps + s, 0, 0)),
    ]
    in_specs += [pl.BlockSpec((tile, width), lambda s, c: (chunk * steps + s, 0))] * samples
    operands = [modes, *rows]
    aliases = {}
    if previous is not None:
        in_specs.append(pl.BlockSpec(memory_space=pl.ANY))
        aliases = {1 + len(operands): 0}
        operands.append(previous)
    return pl.pallas_call(
        functools.partial(grad_kernel, samples, group, depth, int(previous is not None)),
        out_shape=[
            jax.ShapeDtypeStruct((kept, 2 * total_rows, width), jnp.float32),
            jax.ShapeDtypeStruct((kept, size, width), jnp.float32),
        ],
        grid_spec=pltpu.PrefetchScalarGridSpec(
            num_scalar_prefetch=1,
            grid=(steps,),
            in_specs=in_specs,
            out_specs=[
                pl.BlockSpec(
                    (kept, tile, width), lambda s, c: (0, (c[0] * chunks + chunk) * steps + s, 0)
                ),
                pl.BlockSpec((kept, tile, width), lambda s, c: (0, s, 0)),
            ],
            scratch_shapes=[
                pltpu.VMEM((group * samples, group * samples * depth), jnp.bfloat16),
                pltpu.VMEM((lanes, samples * depth), jnp.float32),
            ],
        ),
        input_output_aliases=aliases,
        compiler_params=pltpu.CompilerParams(vmem_limit_bytes=24 * MIB),
        cost_estimate=work(1),
        name="grad_chunk",
    )(core, *operands)


def place_kernel(core_ref, part_ref, old_ref, out_ref):
    del core_ref, old_ref
    out_ref[...] = part_ref[...]


def place_chunk(core, part, result, chunk, chunks):
    kept, size, width = part.shape
    steps = 2
    tile = size // steps
    return pl.pallas_call(
        place_kernel,
        out_shape=jax.ShapeDtypeStruct(result.shape, result.dtype),
        grid_spec=pltpu.PrefetchScalarGridSpec(
            num_scalar_prefetch=1,
            grid=(steps,),
            in_specs=[
                pl.BlockSpec((kept, tile, width), lambda s, c: (0, s, 0)),
                pl.BlockSpec(memory_space=pl.ANY),
            ],
            out_specs=pl.BlockSpec(
                (kept, tile, width),
                lambda s, c: (0, ((1 - c[0]) * chunks + chunk) * steps + s, 0),
            ),
        ),
        input_output_aliases={2: 0},
        compiler_params=pltpu.CompilerParams(vmem_limit_bytes=8 * MIB),
        cost_estimate=work(0.2),
        name="place_chunk",
    )(core, part, result)


def cast_kernel(parts, rows_hbm, keep_ref, give_ref, held_ref, sems):
    size = held_ref.shape[0] // (2 * parts)
    core = lax.rem(lax.axis_index("dp"), 2)
    halves = [(keep_ref, core * parts), (give_ref, (1 - core) * parts)]
    copies, jobs = [], []
    for h, (out, first) in enumerate(halves):
        for i in range(parts):
            source = pl.ds(pl.multiple_of((first + i) * size, size), size)
            spot = pl.ds((h * parts + i) * size, size)
            copies.append(
                pltpu.make_async_copy(
                    rows_hbm.at[source, :], held_ref.at[spot, :], sems.at[h * parts + i]
                )
            )
            jobs.append((out, pl.ds(i * size, size), spot))
    for copy in copies:
        copy.start()
    for copy, (out, place, spot) in zip(copies, jobs):
        copy.wait()
        out[place, :] = held_ref[spot, :].astype(jnp.bfloat16)


def cast_rows(rows):
    parts = 2
    total, width = rows.shape
    return pl.pallas_call(
        functools.partial(cast_kernel, parts),
        out_shape=[jax.ShapeDtypeStruct((total // 2, width), jnp.bfloat16)] * 2,
        in_specs=[pl.BlockSpec(memory_space=pltpu.HBM)],
        out_specs=[pl.BlockSpec(memory_space=pltpu.VMEM)] * 2,
        scratch_shapes=[
            pltpu.VMEM(rows.shape, jnp.float32),
            pltpu.SemaphoreType.DMA((2 * parts,)),
        ],
        compiler_params=pltpu.CompilerParams(vmem_limit_bytes=8 * MIB),
        cost_estimate=work(0.1),
        name="cast_rows",
    )(*in_hbm(rows))


def chip_ring(chips):
    order = list(range(0, chips, 2))
    return order + [c for c in range(chips - 1, 0, -1) if c % 2]


def ring_perm(chips, step):
    order = chip_ring(chips)
    return [
        (2 * order[p] + core, 2 * order[(p + step) % chips] + core)
        for p in range(chips)
        for core in (0, 1)
    ]


def ring_sample(device, q, devices):
    chips = devices // 2
    up = (chips + 1) // 2
    chip = lax.div(device, 2)
    place = jnp.where(lax.rem(chip, 2) == 0, lax.div(chip, 2), chips - 1 - lax.div(chip, 2))
    spot = lax.rem(place - lax.div(q, 2) + chips, chips)
    source = jnp.where(spot < up, 2 * spot, 2 * (chips - 1 - spot) + 1)
    return 2 * source + lax.rem(lax.rem(device, 2) + lax.rem(q, 2), 2)


def joint_kernel(count, total, *refs):
    for old, new in zip(refs[:count], refs[total:]):
        new[...] = old[...]


def joint(arrays, *after):
    vmem = pl.BlockSpec(memory_space=pltpu.VMEM)
    total = len(arrays) + len(after)
    return pl.pallas_call(
        functools.partial(joint_kernel, len(arrays), total),
        out_shape=[jax.ShapeDtypeStruct(a.shape, a.dtype) for a in arrays],
        in_specs=[vmem] * total,
        out_specs=[vmem] * len(arrays),
        compiler_params=pltpu.CompilerParams(vmem_limit_bytes=8 * MIB),
        cost_estimate=work(0.01),
        name="joint",
    )(*arrays, *after)


def per_device(
    point_feats, point_coords, slot_block, slot_cell, slot_count, cotangent, offset_map,
    offset_bias, kernel_mix, lift_weight,
):
    slabs = lax.axis_size("slab")
    devices = lax.axis_size("dp")
    channels = point_feats.shape[2]
    mode_count = cotangent.shape[2]
    capacity = slot_block.shape[3]
    width = cotangent.shape[4]
    planes = GX // slabs
    kept = channels // devices
    slots = slabs * capacity
    local_x = cotangent.shape[1]
    total = local_x // 2 * mode_count
    chunks = 2
    group = min(8, total // chunks)
    chips = devices // 2
    far = chips // 2

    def up(rows):
        return lax.ppermute(rows, "dp", ring_perm(chips, 1))

    def down(rows):
        return lax.ppermute(rows, "dp", ring_perm(chips, -1))

    def swap(rows):
        return lax.ppermute(rows, "dp", [(d, d ^ 1) for d in range(devices)])

    own, twin = {}, {}
    own[0], given = cast_rows(cotangent[0].reshape(-1, width))
    own[1], own[chips - 1] = up(own[0]), down(own[0])
    twin[0] = swap(given)
    twin[1], twin[chips - 1] = up(twin[0]), down(twin[0])
    terms = list(slot_terms(
        slot_block[0, 0], slot_cell[0, 0], slot_count[0, 0], point_feats[0],
        jnp.swapaxes(point_coords[0], 0, 1), offset_map.T, offset_bias[None], kernel_mix, planes,
        twin[0],
    ))
    own[1], own[chips - 1], *terms = joint([own[1], own[chips - 1], *terms])
    own[2], own[chips - 2] = up(own[1]), down(own[chips - 1])
    for s in range(1, slabs):
        terms[s] = lax.ppermute(terms[s], "slab", [(t, (t + s) % slabs) for t in range(slabs)])
    twin[1], twin[chips - 1], *terms = joint([twin[1], twin[chips - 1], *terms], own[1])
    twin[2], twin[chips - 2] = up(twin[1]), down(twin[chips - 1])
    payload = lift_slots(terms, lift_weight, capacity, chips, 2 * slabs, mode_count)
    own[2], own[chips - 2], payload = joint([own[2], own[chips - 2], payload], twin[1])
    recv = lax.all_to_all(
        payload.reshape(devices * slabs, -1, GZ), ("dp", "slab"),
        split_axis=0, concat_axis=0, tiled=True,
    ).reshape(payload.shape)
    own[3], own[chips - 3] = up(own[2]), down(own[chips - 2])
    twin[2], twin[chips - 2] = joint([twin[2], twin[chips - 2]], own[2])
    scale = 1.0 / math.sqrt(GZ * slabs * slabs * capacity)
    modes = sample_modes(
        recv, devices, slabs, slots, planes, scale, group, total, mode_count, 4 * kept * mode_count
    )
    twin[3], twin[chips - 3] = up(twin[2]), down(twin[chips - 2])
    for s in range(4, far):
        own[s], own[chips - s] = up(own[s - 1]), down(own[chips - s + 1])
        twin[s], twin[chips - s] = up(twin[s - 1]), down(twin[chips - s + 1])
    own[far - 1], own[far + 1] = joint([own[far - 1], own[far + 1]], twin[2])
    twin[far - 1], twin[far + 1] = joint([twin[far - 1], twin[far + 1]], own[far - 1])
    own[far], twin[far] = up(own[far - 1]), down(twin[far + 1])

    rows = [r for p in range(chips) for r in (own[p], twin[p])]
    core = lax.rem(lax.axis_index("dp"), 2).reshape(1)
    result, parts = None, []
    for c in range(chunks):
        result, part = grad_chunk(core, modes, rows, kept, group, mode_count, c, chunks, result)
        parts.append(swap(part))
    for c, part in enumerate(parts):
        result = place_chunk(core, part, result, c, chunks)
    return result.reshape(kept, local_x, mode_count, mode_count, width)


def solution(mesh):
    placed = (
        P("dp", "slab", None, None),
        P("dp", "slab", None, None),
        P("dp", "slab", None, None),
        P("dp", "slab", None, None),
        P("dp", "slab", None),
        P("dp", "slab", None, None, None),
        P(),
        P(),
        P(),
        P(),
    )
    return jax.shard_map(
        per_device,
        mesh=mesh,
        in_specs=placed,
        out_specs=P("dp", "slab", None, None, None),
        check_vma=False,
    )
```

time: 125 us -> 78.1 us (0.62); the launches traced: 123 us -> 77.7 us
  Pallas kernels: 45.9 us -> 25.9 us
  local copies, waits for them, and re-layouts: 21.8 us -> 3.3 us
  other arithmetic: 5.55 us -> 0 us
    unnamed x62 -> x10, local copies, waits for them, and re-layouts: 15.6 us -> 3.3 us
    pallas_call x2 -> x10, Pallas kernels: 21.7 us -> 12.2 us  [the longest x1 7.09 us: slot_terms(): pl.pallas_call(functools.partial(slot_kernel, slabs, planes), out_shape=[...]
    pallas_call x2, Pallas kernels: 15.6 us -> 9.15 us  [grad_chunk(): pl.pallas_call(functools.partial(grad_kernel, samples, group, depth, int(...]
    pallas_call x1, Pallas kernels: 7.21 us -> 2.82 us  [sample_modes(): pl.pallas_call(functools.partial(modes_kernel, samples, slabs, slots, pla...]
    ppermute x31 -> x18, starting transfers between devices: 23.4 us -> 21.5 us  [the longest x7 13.8 us: down(): return lax.ppermute(rows, 'dp', ring_perm(chips, -1))]
    all_to_all x1, starting transfers between devices: 4.27 us -> 6.06 us  [per_device(): lax.all_to_all(payload.reshape(devices * slabs, -1, GZ), ('dp', 'slab'),...]
    mul x1 -> x0, other arithmetic: 1.52 us -> none  [per_device(): jnp.eye(kept, dtype=jnp.float32)[:, None, None, :, None]]
    convert_element_type x5 -> x0, other arithmetic: 1.5 us -> none  [the longest x1 0.72 us: per_device(): mask = (jnp.arange(lanes, dtype=jnp.int32)[:, None] % mode_count == jnp.a...]
  transfers between devices with their start and end apart: 32 -> 19, of which waited for: 8 -> 6; matrix products, arithmetic and copies ran while one was open for 11% -> 0% of each run, Pallas kernels for 22% -> 25%
where the time goes in v1:
time: 78.1 us; the launch traced here: 77.7 us
  starting transfers between devices  27.6 us (35%)
  Pallas kernels  25.9 us (33%)
  waiting for transfers between devices  20.7 us (27%)
  local copies, waits for them, and re-layouts  3.3 us (4%)
    ppermute x7, waiting for transfers between devices, down(): return lax.ppermute(rows, 'dp', ring_perm(chips, -1))  16.2 us
    ppermute x7, starting transfers between devices, down(): return lax.ppermute(rows, 'dp', ring_perm(chips, -1))  13.8 us
    pallas_call x2, Pallas kernels, grad_chunk(): pl.pallas_call(functools.partial(grad_kernel, samples, group, depth, int(...  9.15 us
    pallas_call x1, Pallas kernels, slot_terms(): pl.pallas_call(functools.partial(slot_kernel, slabs, planes), out_shape=[...  7.09 us
    all_to_all x1, starting transfers between devices, per_device(): lax.all_to_all(payload.reshape(devices * slabs, -1, GZ), ('dp', 'slab'),...  6.06 us
    ppermute x7, starting transfers between devices, up(): return lax.ppermute(rows, 'dp', ring_perm(chips, 1))  4.83 us
    unnamed x10, local copies, waits for them, and re-layouts  3.3 us
    ppermute x1, waiting for transfers between devices, per_device(): lax.ppermute(terms[s], 'slab', [(t, (t + s) % slabs) for t in range(slabs)])  3.13 us
  transfers between devices with their start and end apart: 19, of which 6 were waited for; matrix products, arithmetic and copies ran while one was open for 0% of the time, Pallas kernels for 25%

profile of v1, /device:TPU:0, one launch (start us, length us, event | category | flops | bytes accessed | tf_op | source)
XLA Modules:
  0.0 77.7 jit_solution(14890528397386730333)
XLA Ops:
  0.0 1.2 %cast_rows.1 = (bf16[1024,128]{1,0:T(8,128)(2,1)S(1)}, bf16[1024,128]{1,0:T(8,128)(2,1)S(1)}) custom-call(f32[2048,128]{1,0:T(8,128)} %bitcast.15), custom_call_target="tpu_custom_call" | custom-call | flops 100000000 | bytes 1024 | tf_op jit(solution)/shard_map/cast_rows/pallas_call | solution.py:445
  1.8 2.6 %collective-permute-start.1 = (bf16[1024,128]{1,0:T(8,128)(2,1)S(1)}, bf16[1024,128]{1,0:T(8,128)(2,1)S(1)}, u32[]{:S(2)}, u32[]{:S(2)}) collective-permute-start(bf16[1024,128]{1,0:T(8,128)(2,1)S(1)} %get-tuple-element.30.refs_0_), channel_id=1, source_target_pairs={{0,4},{2,6},{8,0},{10,2},{16,8},{18,10},{24,16},{26,18},{28,24},{3... | collective-permute-start | bytes 786440 | tf_op jit(solution)/shard_map/ppermute | solution.py:527
  4.5 1.9 %collective-permute-start.6 = (bf16[1024,128]{1,0:T(8,128)(2,1)S(1)}, bf16[1024,128]{1,0:T(8,128)(2,1)S(1)}, u32[]{:S(2)}, u32[]{:S(2)}) collective-permute-start(bf16[1024,128]{1,0:T(8,128)(2,1)S(1)} %collective-permute-done.2.after_hbm.refs_1_), channel_id=1, source_target_pairs={{0,4},{2,6},{8,0},{10,2},{16,8},{18,10},{24,16},{26,18},{28,24},{3... | collective-permute-start | bytes 786440 | tf_op jit(solution)/shard_map/ppermute | solution.py:527
  6.5 7.1 %slot_terms.1 = (f32[264,128]{1,0:T(8,128)S(1)}, f32[264,128]{1,0:T(8,128)S(1)}) custom-call(s32[2,4]{1,0:T(2,128)} %bitcast.19, s32[2,4]{1,0:T(2,128)} %bitcast.20, s32[2]{0:T(128)} %bitcast.21, bf16[4,64,128]{2,1,0:T(8,128)(2,1)} %bitcast.16, bf16[3,4,128]{2,1,0:T(4,128)(2,1)} %bitcast.17, f32[3,64]{1,0:T(4,128)} %bitcast.18, f32[1,64]{1,0:T(1,128)} %bitcast.22, ...), custom_call_target="tpu_custom_call" | custom-call | flops 1000000000 | bytes 1024 | tf_op jit(solution)/shard_map/slot_terms/pallas_call | solution.py:128
  13.7 1.9 %collective-permute-start.4 = (bf16[1024,128]{1,0:T(8,128)(2,1)S(1)}, bf16[1024,128]{1,0:T(8,128)(2,1)S(1)}, u32[]{:S(2)}, u32[]{:S(2)}) collective-permute-start(bf16[1024,128]{1,0:T(8,128)(2,1)S(1)} %get-tuple-element.35.refs_14_), channel_id=1, source_target_pairs={{0,4},{2,6},{8,0},{10,2},{16,8},{18,10},{24,16},{26,18},{28,24},{3... | collective-permute-start | bytes 786440 | tf_op jit(solution)/shard_map/ppermute | solution.py:527
  15.8 1.9 %collective-permute-start.7 = (f32[264,128]{1,0:T(8,128)S(1)}, f32[264,128]{1,0:T(8,128)S(1)}, u32[]{:S(2)}, u32[]{:S(2)}) collective-permute-start(f32[264,128]{1,0:T(8,128)S(1)} %get-tuple-element.37), channel_id=1, source_target_pairs={{0,1},{1,0},{2,3},{3,2},{4,5},{5,4},{6,7},{7,6},{8,9},{9,8},{10,11... | collective-permute-start | bytes 405512 | tf_op jit(solution)/shard_map/ppermute | solution.py:545
  17.7 3.1 %collective-permute-done.7.refs_3_ = f32[264,128]{1,0:T(8,128)S(1)} collective-permute-done((f32[264,128]{1,0:T(8,128)S(1)}, f32[264,128]{1,0:T(8,128)S(1)}, u32[]{:S(2)}, u32[]{:S(2)}) %collective-permute-start.7) | collective-permute-done | bytes 135200 | tf_op jit(solution)/shard_map/ppermute | solution.py:545
  20.9 1.9 %collective-permute-start.9 = (bf16[1024,128]{1,0:T(8,128)(2,1)S(1)}, bf16[1024,128]{1,0:T(8,128)(2,1)S(1)}, u32[]{:S(2)}, u32[]{:S(2)}) collective-permute-start(bf16[1024,128]{1,0:T(8,128)(2,1)S(1)} %get-tuple-element.43.refs_15_), channel_id=1, source_target_pairs={{0,4},{2,6},{8,0},{10,2},{16,8},{18,10},{24,16},{26,18},{28,24},{3... | collective-permute-start | bytes 786440 | tf_op jit(solution)/shard_map/ppermute | solution.py:527
  22.9 1.7 %lift_slots.1.refs_2_ = f32[768,128]{1,0:T(8,128)S(1)} custom-call(f32[264,128]{1,0:T(8,128)S(1)} %get-tuple-element.38.refs_0_, f32[264,128]{1,0:T(8,128)S(1)} %get-tuple-element.39.refs_1_, bf16[64,64]{1,0:T(8,128)(2,1)S(1)} %copy-done.4), custom_call_target="tpu_custom_call" | custom-call | flops 100000000 | bytes 1024 | tf_op jit(solution)/shard_map/lift_slots/pallas_call | solution.py:216
  25.7 6.1 %all-to-all-start = ((f32[32,24,128]{2,1,0:T(8,128)}), f32[32,24,128]{2,1,0:T(8,128)S(1)}, u32[]{:S(2)}, u32[]{:S(2)}) async-start(f32[32,24,128]{2,1,0:T(8,128)} %bitcast.10), calls=%async_computation | async-start | bytes 786432 | tf_op jit(solution)/shard_map/all_to_all | solution.py:550
  31.7 1.8 %collective-permute-start.11 = (bf16[1024,128]{1,0:T(8,128)(2,1)S(1)}, bf16[1024,128]{1,0:T(8,128)(2,1)S(1)}, u32[]{:S(2)}, u32[]{:S(2)}) collective-permute-start(bf16[1024,128]{1,0:T(8,128)(2,1)S(1)} %get-tuple-element.45.refs_12_), channel_id=1, source_target_pairs={{0,4},{2,6},{8,0},{10,2},{16,8},{18,10},{24,16},{26,18},{28,24},{3... | collective-permute-start | bytes 786440 | tf_op jit(solution)/shard_map/ppermute | solution.py:527
  35.5 1.8 %collective-permute-start.13 = (bf16[1024,128]{1,0:T(8,128)(2,1)S(1)}, bf16[1024,128]{1,0:T(8,128)(2,1)S(1)}, u32[]{:S(2)}, u32[]{:S(2)}) collective-permute-start(bf16[1024,128]{1,0:T(8,128)(2,1)S(1)} %get-tuple-element.47.refs_13_), channel_id=1, source_target_pairs={{0,4},{2,6},{8,0},{10,2},{16,8},{18,10},{24,16},{26,18},{28,24},{3... | collective-permute-start | bytes 786440 | tf_op jit(solution)/shard_map/ppermute | solution.py:527
  37.6 9.4 %collective-permute-done.11.refs_1_ = bf16[1024,128]{1,0:T(8,128)(2,1)S(1)} collective-permute-done((bf16[1024,128]{1,0:T(8,128)(2,1)S(1)}, bf16[1024,128]{1,0:T(8,128)(2,1)S(1)}, u32[]{:S(2)}, u32[]{:S(2)}) %collective-permute-start.11) | collective-permute-done | bytes 262176 | tf_op jit(solution)/shard_map/ppermute | solution.py:527
  47.0 3.6 %collective-permute-start.14 = (bf16[1024,128]{1,0:T(8,128)(2,1)S(1)}, bf16[1024,128]{1,0:T(8,128)(2,1)}, u32[]{:S(2)}, u32[]{:S(2)}) collective-permute-start(bf16[1024,128]{1,0:T(8,128)(2,1)S(1)} %get-tuple-element.46.refs_2_.refs_6_), channel_id=1, source_target_pairs={{0,8},{2,10},{8,16},{10,18},{16,24},{18,26},{24,28},{26,30},{28,20... | collective-permute-start | bytes 786440 | tf_op jit(solution)/shard_map/ppermute | solution.py:524
  50.7 1.5 %collective-permute-done.13.refs_1_ = bf16[1024,128]{1,0:T(8,128)(2,1)S(1)} collective-permute-done((bf16[1024,128]{1,0:T(8,128)(2,1)S(1)}, bf16[1024,128]{1,0:T(8,128)(2,1)S(1)}, u32[]{:S(2)}, u32[]{:S(2)}) %collective-permute-start.13) | collective-permute-done | bytes 262176 | tf_op jit(solution)/shard_map/ppermute | solution.py:527
  53.6 1.9 %collective-permute-start.15 = (bf16[1024,128]{1,0:T(8,128)(2,1)}, bf16[1024,128]{1,0:T(8,128)(2,1)}, u32[]{:S(2)}, u32[]{:S(2)}) collective-permute-start(bf16[1024,128]{1,0:T(8,128)(2,1)} %get-tuple-element.49.refs_11_), channel_id=1, source_target_pairs={{0,4},{2,6},{8,0},{10,2},{16,8},{18,10},{24,16},{26,18},{28,24},{3... | collective-permute-start | bytes 786440 | tf_op jit(solution)/shard_map/ppermute | solution.py:527
  55.5 2.8 %sample_modes.1.modes_ref = bf16[8,256,128]{2,1,0:T(8,128)(2,1)S(1)} custom-call(f32[768,128]{1,0:T(8,128)S(1)} %bitcast.14), custom_call_target="tpu_custom_call" | custom-call | flops 200000000 | bytes 1024 | tf_op jit(solution)/shard_map/sample_modes/pallas_call | solution.py:289
  58.4 5.3 %collective-permute-done.15.refs_9_ = bf16[1024,128]{1,0:T(8,128)(2,1)} collective-permute-done((bf16[1024,128]{1,0:T(8,128)(2,1)}, bf16[1024,128]{1,0:T(8,128)(2,1)}, u32[]{:S(2)}, u32[]{:S(2)}) %collective-permute-start.15) | collective-permute-done | bytes 262176 | tf_op jit(solution)/shard_map/ppermute | solution.py:527
  63.7 0.9 %copy-done.1 = bf16[1024,128]{1,0:T(8,128)(2,1)S(1)} copy-done((bf16[1024,128]{1,0:T(8,128)(2,1)S(1)}, bf16[1024,128]{1,0:T(8,128)(2,1)}, u32[]{:S(2)}) %copy-start.1) | copy-done | bytes 262168
  64.6 4.6 %grad_chunk.2 = (f32[4,2048,128]{2,1,0:T(8,128)}, f32[4,512,128]{2,1,0:T(8,128)S(1)}) custom-call(s32[1]{0:T(128)} %bitcast.core_ref, bf16[8,256,128]{2,1,0:T(8,128)(2,1)S(1)} %sample_modes.1.modes_ref, bf16[1024,128]{1,0:T(8,128)(2,1)S(1)} %get-tuple-element.30.refs_0_, bf16[1024,128]{1,0:T(8,128)(2,1)S(1)} %collective-permute-done.2.after_hbm.refs_1_, ...), custom_call_target="tpu_custom_call" | custom-call | flops 1000000000 | bytes 1024 | tf_op jit(solution)/shard_map/grad_chunk/pallas_call | solution.py:361
  69.2 4.6 %grad_chunk.3 = (f32[4,2048,128]{2,1,0:T(8,128)}, f32[4,512,128]{2,1,0:T(8,128)S(1)}) custom-call(s32[1]{0:T(128)} %bitcast.core_ref, bf16[8,256,128]{2,1,0:T(8,128)(2,1)S(1)} %sample_modes.1.modes_ref, bf16[1024,128]{1,0:T(8,128)(2,1)S(1)} %get-tuple-element.30.refs_0_, ...), custom_call_target="tpu_custom_call", output_to_operand_aliasing={{0}: (18, {})} | custom-call | flops 1000000000 | bytes 1024 | tf_op jit(solution)/shard_map/grad_chunk/pallas_call | solution.py:361
  74.3 1.1 %place_chunk.2.old_ref = f32[4,2048,128]{2,1,0:T(8,128)} custom-call(s32[1]{0:T(128)} %bitcast.core_ref, f32[4,512,128]{2,1,0:T(8,128)S(1)} %collective-permute-done.17.part_ref, f32[4,2048,128]{2,1,0:T(8,128)} %get-tuple-element.54.old_ref), custom_call_target="tpu_custom_call", output_to_operand_aliasing={{}: (2, {})} | custom-call | flops 200000000 | bytes 1024 | tf_op jit(solution)/shard_map/place_chunk/pallas_call | solution.py:398
  75.4 1.2 %collective-permute-done.16.part_ref = f32[4,512,128]{2,1,0:T(8,128)S(1)} collective-permute-done((f32[4,512,128]{2,1,0:T(8,128)S(1)}, f32[4,512,128]{2,1,0:T(8,128)S(1)}, u32[]{:S(2)}, u32[]{:S(2)}) %collective-permute-start.16) | collective-permute-done | bytes 1048608 | tf_op jit(solution)/shard_map/ppermute | solution.py:530
  76.6 1.1 %place_chunk.3 = f32[4,2048,128]{2,1,0:T(8,128)} custom-call(s32[1]{0:T(128)} %bitcast.core_ref, f32[4,512,128]{2,1,0:T(8,128)S(1)} %collective-permute-done.16.part_ref, f32[4,2048,128]{2,1,0:T(8,128)} %place_chunk.2.old_ref), custom_call_target="tpu_custom_call", output_to_operand_aliasing={{}: (2, {})} | custom-call | flops 200000000 | bytes 1024 | tf_op jit(solution)/shard_map/place_chunk/pallas_call | solution.py:398
  (38 shorter events, 6.5 us)
Async XLA Ops:
  0.0 22.9 %copy-start.4 = (bf16[64,64]{1,0:T(8,128)(2,1)S(1)}, bf16[64,64]{1,0:T(8,128)(2,1)}, u32[]{:S(2)}) copy-start(bf16[64,64]{1,0:T(8,128)(2,1)} %refs_2_.1) | copy-start | bytes 24580
  1.3 3.2 %collective-permute-start.2 = (bf16[1024,128]{1,0:T(8,128)(2,1)S(1)}, bf16[1024,128]{1,0:T(8,128)(2,1)S(1)}, u32[]{:S(2)}, u32[]{:S(2)}) collective-permute-start(bf16[1024,128]{1,0:T(8,128)(2,1)S(1)} %get-tuple-element.31), channel_id=1, source_target_pairs={{0,2},{2,0},{4,6},{6,4},{8,10},{10,8},{12,14},{14,12},{16,18},{18,... | collective-permute-start | bytes 786440 | tf_op jit(solution)/shard_map/ppermute | solution.py:530
  1.8 11.9 %collective-permute-start.1 = (bf16[1024,128]{1,0:T(8,128)(2,1)S(1)}, bf16[1024,128]{1,0:T(8,128)(2,1)S(1)}, u32[]{:S(2)}, u32[]{:S(2)}) collective-permute-start(bf16[1024,128]{1,0:T(8,128)(2,1)S(1)} %get-tuple-element.30.refs_0_), channel_id=1, source_target_pairs={{0,4},{2,6},{8,0},{10,2},{16,8},{18,10},{24,16},{26,18},{28,24},{3... | collective-permute-start | bytes 786440 | tf_op jit(solution)/shard_map/ppermute | solution.py:527
  4.3 9.3 %collective-permute-start = (bf16[1024,128]{1,0:T(8,128)(2,1)S(1)}, bf16[1024,128]{1,0:T(8,128)(2,1)S(1)}, u32[]{:S(2)}, u32[]{:S(2)}) collective-permute-start(bf16[1024,128]{1,0:T(8,128)(2,1)S(1)} %get-tuple-element.30.refs_0_), channel_id=1, source_target_pairs={{0,8},{2,10},{8,16},{10,18},{16,24},{18,26},{24,28},{26,30},{28,20... | collective-permute-start | bytes 786440 | tf_op jit(solution)/shard_map/ppermute | solution.py:524
  4.5 16.3 %collective-permute-start.6 = (bf16[1024,128]{1,0:T(8,128)(2,1)S(1)}, bf16[1024,128]{1,0:T(8,128)(2,1)S(1)}, u32[]{:S(2)}, u32[]{:S(2)}) collective-permute-start(bf16[1024,128]{1,0:T(8,128)(2,1)S(1)} %collective-permute-done.2.after_hbm.refs_1_), channel_id=1, source_target_pairs={{0,4},{2,6},{8,0},{10,2},{16,8},{18,10},{24,16},{26,18},{28,24},{3... | collective-permute-start | bytes 786440 | tf_op jit(solution)/shard_map/ppermute | solution.py:527
  6.4 14.5 %collective-permute-start.5 = (bf16[1024,128]{1,0:T(8,128)(2,1)S(1)}, bf16[1024,128]{1,0:T(8,128)(2,1)S(1)}, u32[]{:S(2)}, u32[]{:S(2)}) collective-permute-start(bf16[1024,128]{1,0:T(8,128)(2,1)S(1)} %collective-permute-done.2.after_hbm.refs_1_), channel_id=1, source_target_pairs={{0,8},{2,10},{8,16},{10,18},{16,24},{18,26},{24,28},{26,30},{28,20... | collective-permute-start | bytes 786440 | tf_op jit(solution)/shard_map/ppermute | solution.py:524
  13.7 11.0 %collective-permute-start.4 = (bf16[1024,128]{1,0:T(8,128)(2,1)S(1)}, bf16[1024,128]{1,0:T(8,128)(2,1)S(1)}, u32[]{:S(2)}, u32[]{:S(2)}) collective-permute-start(bf16[1024,128]{1,0:T(8,128)(2,1)S(1)} %get-tuple-element.35.refs_14_), channel_id=1, source_target_pairs={{0,4},{2,6},{8,0},{10,2},{16,8},{18,10},{24,16},{26,18},{28,24},{3... | collective-permute-start | bytes 786440 | tf_op jit(solution)/shard_map/ppermute | solution.py:527
  15.6 9.2 %collective-permute-start.3 = (bf16[1024,128]{1,0:T(8,128)(2,1)S(1)}, bf16[1024,128]{1,0:T(8,128)(2,1)S(1)}, u32[]{:S(2)}, u32[]{:S(2)}) collective-permute-start(bf16[1024,128]{1,0:T(8,128)(2,1)S(1)} %get-tuple-element.34.refs_4_.refs_2_), channel_id=1, source_target_pairs={{0,8},{2,10},{8,16},{10,18},{16,24},{18,26},{24,28},{26,30},{28,20... | collective-permute-start | bytes 786440 | tf_op jit(solution)/shard_map/ppermute | solution.py:524
  15.8 5.0 %collective-permute-start.7 = (f32[264,128]{1,0:T(8,128)S(1)}, f32[264,128]{1,0:T(8,128)S(1)}, u32[]{:S(2)}, u32[]{:S(2)}) collective-permute-start(f32[264,128]{1,0:T(8,128)S(1)} %get-tuple-element.37), channel_id=1, source_target_pairs={{0,1},{1,0},{2,3},{3,2},{4,5},{5,4},{6,7},{7,6},{8,9},{9,8},{10,11... | collective-permute-start | bytes 405512 | tf_op jit(solution)/shard_map/ppermute | solution.py:545
  20.9 12.9 %collective-permute-start.9 = (bf16[1024,128]{1,0:T(8,128)(2,1)S(1)}, bf16[1024,128]{1,0:T(8,128)(2,1)S(1)}, u32[]{:S(2)}, u32[]{:S(2)}) collective-permute-start(bf16[1024,128]{1,0:T(8,128)(2,1)S(1)} %get-tuple-element.43.refs_15_), channel_id=1, source_target_pairs={{0,4},{2,6},{8,0},{10,2},{16,8},{18,10},{24,16},{26,18},{28,24},{3... | collective-permute-start | bytes 786440 | tf_op jit(solution)/shard_map/ppermute | solution.py:527
  22.8 11.0 %collective-permute-start.8 = (bf16[1024,128]{1,0:T(8,128)(2,1)S(1)}, bf16[1024,128]{1,0:T(8,128)(2,1)S(1)}, u32[]{:S(2)}, u32[]{:S(2)}) collective-permute-start(bf16[1024,128]{1,0:T(8,128)(2,1)S(1)} %get-tuple-element.40.refs_3_), channel_id=1, source_target_pairs={{0,8},{2,10},{8,16},{10,18},{16,24},{18,26},{24,28},{26,30},{28,20... | collective-permute-start | bytes 786440 | tf_op jit(solution)/shard_map/ppermute | solution.py:524
  25.7 29.9 %all-to-all-start = ((f32[32,24,128]{2,1,0:T(8,128)}), f32[32,24,128]{2,1,0:T(8,128)S(1)}, u32[]{:S(2)}, u32[]{:S(2)}) async-start(f32[32,24,128]{2,1,0:T(8,128)} %bitcast.10), calls=%async_computation | async-start | bytes 786432 | tf_op jit(solution)/shard_map/all_to_all | solution.py:550
  31.7 15.3 %collective-permute-start.11 = (bf16[1024,128]{1,0:T(8,128)(2,1)S(1)}, bf16[1024,128]{1,0:T(8,128)(2,1)S(1)}, u32[]{:S(2)}, u32[]{:S(2)}) collective-permute-start(bf16[1024,128]{1,0:T(8,128)(2,1)S(1)} %get-tuple-element.45.refs_12_), channel_id=1, source_target_pairs={{0,4},{2,6},{8,0},{10,2},{16,8},{18,10},{24,16},{26,18},{28,24},{3... | collective-permute-start | bytes 786440 | tf_op jit(solution)/shard_map/ppermute | solution.py:527
  33.6 13.5 %collective-permute-start.10 = (bf16[1024,128]{1,0:T(8,128)(2,1)S(1)}, bf16[1024,128]{1,0:T(8,128)(2,1)S(1)}, u32[]{:S(2)}, u32[]{:S(2)}) collective-permute-start(bf16[1024,128]{1,0:T(8,128)(2,1)S(1)} %get-tuple-element.42.refs_2_.refs_4_), channel_id=1, source_target_pairs={{0,8},{2,10},{8,16},{10,18},{16,24},{18,26},{24,28},{26,30},{28,20... | collective-permute-start | bytes 786440 | tf_op jit(solution)/shard_map/ppermute | solution.py:524
  33.8 0.7 copy-start.2
  34.5 0.9 %copy-start.3 = (bf16[1024,128]{1,0:T(8,128)(2,1)S(1)}, bf16[1024,128]{1,0:T(8,128)(2,1)}, u32[]{:S(2)}) copy-start(bf16[1024,128]{1,0:T(8,128)(2,1)} %copy-done.2) | copy-start | bytes 786436
  35.5 16.6 %collective-permute-start.13 = (bf16[1024,128]{1,0:T(8,128)(2,1)S(1)}, bf16[1024,128]{1,0:T(8,128)(2,1)S(1)}, u32[]{:S(2)}, u32[]{:S(2)}) collective-permute-start(bf16[1024,128]{1,0:T(8,128)(2,1)S(1)} %get-tuple-element.47.refs_13_), channel_id=1, source_target_pairs={{0,4},{2,6},{8,0},{10,2},{16,8},{18,10},{24,16},{26,18},{28,24},{3... | collective-permute-start | bytes 786440 | tf_op jit(solution)/shard_map/ppermute | solution.py:527
  37.3 14.8 %collective-permute-start.12 = (bf16[1024,128]{1,0:T(8,128)(2,1)S(1)}, bf16[1024,128]{1,0:T(8,128)(2,1)S(1)}, u32[]{:S(2)}, u32[]{:S(2)}) collective-permute-start(bf16[1024,128]{1,0:T(8,128)(2,1)S(1)} %get-tuple-element.44.refs_2_.refs_5_), channel_id=1, source_target_pairs={{0,8},{2,10},{8,16},{10,18},{16,24},{18,26},{24,28},{26,30},{28,20... | collective-permute-start | bytes 786440 | tf_op jit(solution)/shard_map/ppermute | solution.py:524
  47.0 11.3 %collective-permute-start.14 = (bf16[1024,128]{1,0:T(8,128)(2,1)S(1)}, bf16[1024,128]{1,0:T(8,128)(2,1)}, u32[]{:S(2)}, u32[]{:S(2)}) collective-permute-start(bf16[1024,128]{1,0:T(8,128)(2,1)S(1)} %get-tuple-element.46.refs_2_.refs_6_), channel_id=1, source_target_pairs={{0,8},{2,10},{8,16},{10,18},{16,24},{18,26},{24,28},{26,30},{28,20... | collective-permute-start | bytes 786440 | tf_op jit(solution)/shard_map/ppermute | solution.py:524
  52.9 0.7 copy-start
  53.6 10.1 %collective-permute-start.15 = (bf16[1024,128]{1,0:T(8,128)(2,1)}, bf16[1024,128]{1,0:T(8,128)(2,1)}, u32[]{:S(2)}, u32[]{:S(2)}) collective-permute-start(bf16[1024,128]{1,0:T(8,128)(2,1)} %get-tuple-element.49.refs_11_), channel_id=1, source_target_pairs={{0,4},{2,6},{8,0},{10,2},{16,8},{18,10},{24,16},{26,18},{28,24},{3... | collective-permute-start | bytes 786440 | tf_op jit(solution)/shard_map/ppermute | solution.py:527
  63.7 1.0 %copy-start.1 = (bf16[1024,128]{1,0:T(8,128)(2,1)S(1)}, bf16[1024,128]{1,0:T(8,128)(2,1)}, u32[]{:S(2)}) copy-start(bf16[1024,128]{1,0:T(8,128)(2,1)} %copy-done) | copy-start | bytes 786436
  69.2 5.1 %collective-permute-start.17 = (f32[4,512,128]{2,1,0:T(8,128)S(1)}, f32[4,512,128]{2,1,0:T(8,128)S(1)}, u32[]{:S(2)}, u32[]{:S(2)}) collective-permute-start(f32[4,512,128]{2,1,0:T(8,128)S(1)} %get-tuple-element.53), channel_id=1, source_target_pairs={{0,2},{2,0},{4,6},{6,4},{8,10},{10,8},{12,14},{14,12},{16,18},{18,... | collective-permute-start | bytes 3145736 | tf_op jit(solution)/shard_map/ppermute | solution.py:530
  73.8 2.8 %collective-permute-start.16 = (f32[4,512,128]{2,1,0:T(8,128)S(1)}, f32[4,512,128]{2,1,0:T(8,128)S(1)}, u32[]{:S(2)}, u32[]{:S(2)}) collective-permute-start(f32[4,512,128]{2,1,0:T(8,128)S(1)} %get-tuple-element.52), channel_id=1, source_target_pairs={{0,2},{2,0},{4,6},{6,4},{8,10},{10,8},{12,14},{14,12},{16,18},{18,... | collective-permute-start | bytes 3145736 | tf_op jit(solution)/shard_map/ppermute | solution.py:530

commit v2 on v1

v2 whole, which is shorter than its diff:
```python
import functools
import math

import jax
import jax.numpy as jnp
from jax import lax
from jax.experimental import pallas as pl
from jax.experimental.pallas import tpu as pltpu
from jax.sharding import PartitionSpec as P

GX = 128
GY = 128
GZ = 128
MIB = 1024 * 1024


def in_hbm(*arrays):
    return [pltpu.with_memory_space_constraint(a, pltpu.HBM) for a in arrays]


def work(micros):
    return pl.CostEstimate(flops=int(micros * 10**9), bytes_accessed=1024, transcendentals=0)


HIGH = lax.Precision.HIGHEST
ROWS0 = (((0,), (0,)), ((), ()))


def slot_kernel(slabs, planes, block_hbm, cell_hbm, count_hbm, feats_hbm, coords_hbm, map_hbm, bias_hbm, mix_hbm, after_hbm, *refs):
    del after_hbm
    outs = refs[:2]
    (block_ref, cell_ref, count_ref, feats_ref, coords_ref, map_ref, bias_ref, mix_ref, list_ref,
     turned_ref, mixed_ref, part_ref, coef_ref, out_ref, acc_ref, spot_ref, sems) = refs[2:]
    me = lax.axis_index("slab")
    pairs = [(block_hbm, block_ref), (cell_hbm, cell_ref), (count_hbm, count_ref), (feats_hbm, feats_ref),
             (coords_hbm, coords_ref), (map_hbm, map_ref), (bias_hbm, bias_ref), (mix_hbm, mix_ref)]
    copies = [pltpu.make_async_copy(a, b, sems.at[i]) for i, (a, b) in enumerate(pairs)]
    for c in copies: c.start()
    capacity = block_ref.shape[1]
    blocks, channels, points = feats_ref.shape
    hidden = mix_ref.shape[0]
    width = blocks * channels
    base = capacity * channels + 8
    row8 = lax.broadcasted_iota(jnp.int32, (8, points), 0)
    pos_z = (lax.broadcasted_iota(jnp.int32, (GZ, points), 0).astype(jnp.float32) + 0.5) * (1.0 / GZ)
    for c in copies[:7]: c.wait()
    spot_ref[...] = coords_ref[...].astype(jnp.float32)
    for b in range(blocks):
        turned_ref[:, b * channels : (b + 1) * channels] = feats_ref[b].astype(jnp.float32).T.astype(jnp.bfloat16)
    cat = jnp.concatenate([map_ref[...], bias_ref[...], jnp.zeros((4, hidden), jnp.float32)], axis=0)
    live = jnp.int32(0)
    sides = [jnp.where(row8 == 2, 1.0, 0.0)]
    for r in range(slabs):
        peer = lax.rem(me + r, slabs)
        tag_rows = jnp.full((8, points), -1.0, jnp.float32)
        for j in range(capacity):
            n = r * capacity + j
            block = block_ref[peer, j]
            cell = cell_ref[peer, j]
            alive = j < count_ref[peer]
            @pl.when(alive)
            def _():
                list_ref[live] = n
                list_ref[live + 1] = n
            live = live + alive.astype(jnp.int32)
            list_ref[slabs * capacity + 1 + n] = block
            pos_x = ((peer * planes + lax.div(cell, GY)).astype(jnp.float32) + 0.5) * (1.0 / GX)
            pos_y = (lax.rem(cell, GY).astype(jnp.float32) + 0.5) * (1.0 / GY)
            q0 = spot_ref[0, pl.ds(block, 1), :]
            q1 = spot_ref[1, pl.ds(block, 1), :]
            q2 = spot_ref[2, pl.ds(block, 1), :]
            side = jnp.where(row8 == 0, pos_x - q0, jnp.where(row8 == 1, pos_y - q1, jnp.where(row8 == 2, -q2, jnp.where(row8 == 3, 1.0, 0.0))))
            sides.append(side)
            tag_rows = jnp.where(row8 == j, jnp.where(alive, cell, -1).astype(jnp.float32), tag_rows)
        out_ref[r * base + capacity * channels : (r + 1) * base, :] = tag_rows
    parts = lax.dot_general(
        cat, jnp.concatenate(sides, axis=1), ROWS0, precision=HIGH,
        preferred_element_type=jnp.float32,
    )
    coef_ref[...] = parts[:, :points]
    for n in range(slabs * capacity):
        part_ref[n] = parts[:, (n + 1) * points : (n + 2) * points]
    copies[7].wait()
    lane = lax.broadcasted_iota(jnp.int32, (channels, 2 * channels), 1)
    left = turned_ref[...]

    step = max(1, min(hidden // 2, 512 // (blocks * blocks)))

    def mix_step(it, carry):
        for u in range(step):
            h = it * step + u
            mix = mix_ref[h]
            wide = jnp.concatenate([mix, mix], axis=1)
            zero = jnp.zeros_like(wide)
            halves = (jnp.where(lane < channels, wide, zero), jnp.where(lane < channels, zero, wide))
            rows = [jnp.concatenate([halves[b % 2] if b // 2 == t else zero for t in range(blocks // 2)], axis=1) for b in range(blocks)]
            mixed_ref[pl.ds(pl.multiple_of(h * points, points), points), :] = jnp.dot(left, jnp.concatenate(rows, axis=0), preferred_element_type=jnp.float32).astype(jnp.bfloat16)
        return carry
    lax.fori_loop(0, hidden // step, mix_step, 0)

    def pair(it, carry):
        ids = [list_ref[2 * it], list_ref[2 * it + 1]]
        part = 8
        for k in range(0, hidden, part):
            cols = []
            for h in range(k, k + part):
                cell_z = pos_z * coef_ref[h : h + 1, :]
                cols.append(jnp.concatenate([jnp.maximum(cell_z + part_ref[n, h : h + 1, :], 0.0).astype(jnp.bfloat16) for n in ids], axis=0))
            got = jnp.dot(jnp.concatenate(cols, axis=1), mixed_ref[k * points : (k + part) * points, :], preferred_element_type=jnp.float32)
            if k: acc_ref[...] += got
            else: acc_ref[...] = got
        for j, n in enumerate(ids):
            block = list_ref[slabs * capacity + 1 + n]
            pick = acc_ref[j * GZ : (j + 1) * GZ, : 2 * channels]
            for t in range(1, blocks // 2):
                pick = jnp.where(block // 2 == t, acc_ref[j * GZ : (j + 1) * GZ, 2 * t * channels : 2 * (t + 1) * channels], pick)
            turned = pick.T * (1.0 / points)
            start = pl.multiple_of((n // capacity) * base + (n % capacity) * channels, 8)
            out_ref[pl.ds(start, channels), :] = jnp.where(block % 2 == 1, turned[channels:], turned[:channels])
        return carry
    lax.fori_loop(0, (live + 1) // 2, pair, 0)
    for i, out in enumerate(outs):
        out[...] = out_ref[i * out.shape[0] : (i + 1) * out.shape[0], :]

def slot_terms(slot_block, slot_cell, slot_count, feats, coords, offset_map, offset_bias, kernel_mix, planes, after):
    slabs, capacity = slot_block.shape
    blocks, channels, points = feats.shape
    hidden = kernel_mix.shape[0]
    base = capacity * channels + 8
    slots = slabs * capacity
    width = blocks * channels
    slot_limit = hidden * points * width * 2 + (10 if blocks <= 4 else 24) * MIB
    hbm = pl.BlockSpec(memory_space=pltpu.HBM)
    vmem = pl.BlockSpec(memory_space=pltpu.VMEM)
    return pl.pallas_call(
        functools.partial(slot_kernel, slabs, planes),
        out_shape=[jax.ShapeDtypeStruct((slabs * base // 2, GZ), jnp.float32)] * 2,
        in_specs=[hbm] * 8 + [pl.BlockSpec(memory_space=pl.ANY)],
        out_specs=[vmem] * 2,
        scratch_shapes=[
            pltpu.SMEM((slabs, capacity), jnp.int32), pltpu.SMEM((slabs, capacity), jnp.int32), pltpu.SMEM((slabs,), jnp.int32),
            pltpu.VMEM(feats.shape, feats.dtype), pltpu.VMEM(coords.shape, coords.dtype), pltpu.VMEM(offset_map.shape, jnp.float32),
            pltpu.VMEM(offset_bias.shape, jnp.float32), pltpu.VMEM(kernel_mix.shape, kernel_mix.dtype),
            pltpu.SMEM((2 * slots + 2,), jnp.int32),
            pltpu.VMEM((points, width), jnp.bfloat16), pltpu.VMEM((hidden * points, width), jnp.bfloat16),
            pltpu.VMEM((slots, hidden, points), jnp.float32), pltpu.VMEM((hidden, points), jnp.float32),
            pltpu.VMEM((slabs * base, GZ), jnp.float32), pltpu.VMEM((2 * GZ, width), jnp.float32), pltpu.VMEM(coords.shape, jnp.float32),
            pltpu.SemaphoreType.DMA((8,)),
        ],
        compiler_params=pltpu.CompilerParams(vmem_limit_bytes=slot_limit),
        cost_estimate=work(1),
        name="slot_terms",
    )(*in_hbm(slot_block, slot_cell, slot_count, feats, coords, offset_map, offset_bias, kernel_mix),
      after)


def lift_kernel(slabs, capacity, dests, mode_count, *refs):
    terms = refs[:slabs]
    lift_ref, out_ref, tag_ref, row_ref, wide_ref, table_ref = refs[slabs:]
    channels = lift_ref.shape[0]
    kept = channels // dests
    group = slabs * capacity
    slots = slabs * group
    base = capacity * channels + 8
    lanes = table_ref.shape[1]
    tiles = lanes // GZ
    per = out_ref.shape[0] // dests
    cells = lax.broadcasted_iota(jnp.int32, (GZ, lanes), 0)
    lane = lax.broadcasted_iota(jnp.int32, (GZ, lanes), 1)
    step = cells * (lane % mode_count) + jnp.where(lane >= lanes // 2, GZ // 4, 0)
    waves = jnp.cos((step % GZ).astype(jnp.float32) * (2.0 * math.pi / GZ))
    for i in range(kept):
        mine = lane // mode_count % kept == i
        table_ref[i * GZ : (i + 1) * GZ, :] = jnp.where(mine, waves, 0.0)

    def receiver(u, carry):
        starts = [lax.rem(u + s, slabs) * base for s in range(slabs)]

        def tag_of(m):
            first = pl.multiple_of(starts[m // capacity] + capacity * channels, 8)
            return terms[m // capacity][pl.ds(first, 8), :][m % capacity : m % capacity + 1, :]

        def terms_of(m):
            first = pl.multiple_of(starts[m // capacity] + (m % capacity) * channels, 8)
            return terms[m // capacity][pl.ds(first, channels), :]

        tags = [tag_of(m) for m in range(group)]
        for n in range(group):
            live = tags[n] >= 0.0
            summed = jnp.zeros((channels, GZ), jnp.float32)
            leader = live
            for m in range(group):
                same = (tags[m] == tags[n]) & live
                summed = summed + jnp.where(same, terms_of(m), 0.0)
                if m < n:
                    leader = leader & jnp.logical_not(same)
            latent = summed.astype(jnp.bfloat16)
            lifted = jax.nn.gelu(
                lax.dot_general(lift_ref[...], latent, ROWS0, preferred_element_type=jnp.float32)
            )
            row_ref[n] = jnp.where(leader, lifted, 0.0)
            rows = pl.ds(pl.multiple_of((u * group + n) * dests, 8), dests)
            for i in range(kept):
                wide_ref[rows, i * GZ : (i + 1) * GZ] = row_ref[
                    n, pl.ds(i, dests, stride=kept), :
                ]
        tag_ref[pl.ds(pl.multiple_of(u * group, 8), group), :] = jnp.concatenate(tags, axis=0)
        return carry

    lax.fori_loop(0, slabs, receiver, 0, unroll=slabs <= 2)
    modes = jnp.dot(
        wide_ref[...], table_ref[...], precision=HIGH, preferred_element_type=jnp.float32
    )
    for n in range(slots):
        for t in range(tiles):
            out_ref[pl.ds(t * slots + n, dests, stride=per), :] = modes[
                n * dests : (n + 1) * dests, t * GZ : (t + 1) * GZ
            ]
    row = lax.broadcasted_iota(jnp.int32, (slots, GZ), 0)
    lane = lax.broadcasted_iota(jnp.int32, (slots, GZ), 1)
    place = lax.broadcasted_iota(jnp.int32, (8, GZ), 0)
    packed = jnp.zeros((8, GZ), jnp.float32)
    for k in range((slots + GZ - 1) // GZ):
        line = jnp.sum(jnp.where(row == lane + k * GZ, tag_ref[...], 0.0), axis=0, keepdims=True)
        packed = jnp.where(place == k, line, packed)
    for d in range(dests):
        out_ref[d * per + tiles * slots : (d + 1) * per, :] = packed


def lift_slots(terms, lift_weight, capacity, dests, mode_count):
    slabs = len(terms)
    channels = lift_weight.shape[0]
    slots = slabs * slabs * capacity
    kept = channels // dests
    lanes = 2 * kept * mode_count
    per = lanes // GZ * slots + 8
    vmem = pl.BlockSpec(memory_space=pltpu.VMEM)
    return pl.pallas_call(
        functools.partial(lift_kernel, slabs, capacity, dests, mode_count),
        out_shape=jax.ShapeDtypeStruct((dests * per, GZ), jnp.float32),
        in_specs=[vmem] * (slabs + 1),
        out_specs=vmem,
        scratch_shapes=[
            pltpu.VMEM((slots, GZ), jnp.float32),
            pltpu.VMEM((slabs * capacity, channels, GZ), jnp.float32),
            pltpu.VMEM((slots * dests, kept * GZ), jnp.float32),
            pltpu.VMEM((kept * GZ, lanes), jnp.float32),
        ],
        compiler_params=pltpu.CompilerParams(
            vmem_limit_bytes=(8 if slabs <= 2 else 48) * MIB
        ),
        cost_estimate=work(0.1),
        name="lift_slots",
    )(*terms, lift_weight)


def modes_kernel(chips, slabs, slots, planes, scale, group, mode_count, *refs):
    recv_refs = refs[:2]
    out_ref, all_ref = refs[2:]
    samples = 2 * chips
    tiles = all_ref.shape[0]
    total = all_ref.shape[1] // samples
    half = tiles * GZ // 2
    per = recv_refs[0].shape[0] // chips

    device = lax.axis_index("dp")
    slab = lax.axis_index("slab")
    first_x = (slab * 2 + lax.rem(device, 2)) * (total // mode_count)
    spot = lax.broadcasted_iota(jnp.int32, (1, total), 1)
    freq_x = first_x + spot // mode_count
    freq_y = spot % mode_count
    freq_x = jnp.where(freq_x < mode_count // 2, freq_x, freq_x - mode_count)
    freq_y = jnp.where(freq_y < mode_count // 2, freq_y, freq_y - mode_count)
    freq_x, freq_y = freq_x.astype(jnp.float32), freq_y.astype(jnp.float32)

    row = lax.broadcasted_iota(jnp.int32, (slots, GZ), 0)
    lane = lax.broadcasted_iota(jnp.int32, (slots, GZ), 1)
    peer = slab + lax.broadcasted_iota(jnp.int32, (slots, 1), 0) // (slots // slabs)
    plane = jnp.where(peer >= slabs, peer - slabs, peer).astype(jnp.float32) * planes

    def body(p, carry):
        base = pl.multiple_of(ring_chip(lax.div(device, 2), p, chips) * per, 8)
        for core, ref in enumerate(recv_refs):
            plain = jnp.concatenate(
                [ref[pl.ds(base + u * slots, slots), :] for u in range(tiles)], axis=1
            )
            packed = ref[pl.ds(base + tiles * slots, 8), :]
            tag = jnp.zeros((slots, 1), jnp.float32)
            for k in range((slots + GZ - 1) // GZ):
                tag = tag + jnp.sum(
                    jnp.where(row == lane + k * GZ, packed[k : k + 1, :], 0.0),
                    axis=1,
                    keepdims=True,
                )
            tag = jnp.maximum(tag, 0.0)
            local_x = jnp.floor(tag * (1.0 / GY))
            turns = (local_x + plane) * (1.0 / GX) * freq_x + (
                tag - local_x * GY
            ) * (1.0 / GY) * freq_y
            angle = (turns - jnp.floor(turns)) * (2.0 * math.pi)
            crossed = jnp.concatenate([plain[:, half:], -plain[:, :half]], axis=1)
            modes = lax.dot_general(
                jnp.concatenate([jnp.cos(angle), jnp.sin(angle)], axis=0),
                jnp.concatenate([plain, crossed], axis=0),
                ROWS0,
                precision=HIGH,
                preferred_element_type=jnp.float32,
            )
            for u in range(tiles):
                all_ref[u, pl.ds(2 * p + core, total, stride=samples), :] = (
                    modes[:, u * GZ : (u + 1) * GZ] * scale
                )
        return carry

    lax.fori_loop(0, chips, body, 0, unroll=2)

    span = group * samples
    for block in range(total // group):
        for u in range(tiles):
            out_ref[block, u * GZ : (u + 1) * GZ, :] = all_ref[
                u, block * span : (block + 1) * span, :
            ].T.astype(jnp.bfloat16)


def sample_modes(recv, chips, slabs, slots, planes, scale, group, total, mode_count, lanes):
    samples = 2 * chips
    vmem = pl.BlockSpec(memory_space=pltpu.VMEM)
    return pl.pallas_call(
        functools.partial(modes_kernel, chips, slabs, slots, planes, scale, group, mode_count),
        out_shape=jax.ShapeDtypeStruct((total // group, lanes, group * samples), jnp.bfloat16),
        in_specs=[vmem] * len(recv),
        out_specs=vmem,
        scratch_shapes=[pltpu.VMEM((lanes // GZ, total * samples, GZ), jnp.float32)],
        compiler_params=pltpu.CompilerParams(vmem_limit_bytes=(8 if slabs <= 2 else 32) * MIB),
        cost_estimate=work(0.2),
        name="sample_modes",
    )(*recv)


def spread_kernel(depth, modes_ref, after_ref, out_ref, pick_ref, mask_ref):
    del after_ref
    group = out_ref.shape[0]
    span = out_ref.shape[2]

    @pl.when(pl.program_id(0) == 0)
    def _():
        row = lax.broadcasted_iota(jnp.int32, pick_ref.shape, 0)
        col = lax.broadcasted_iota(jnp.int32, pick_ref.shape, 1)
        pick_ref[...] = jnp.where(row == col // depth, 1.0, 0.0).astype(jnp.bfloat16)
        row = lax.broadcasted_iota(jnp.int32, mask_ref.shape, 0)
        col = lax.broadcasted_iota(jnp.int32, mask_ref.shape, 1)
        mask_ref[...] = jnp.where(row % depth == col % depth, 1.0, 0.0)

    for g in range(group):
        left = jnp.dot(
            modes_ref[0], pick_ref[:, g * span : (g + 1) * span],
            preferred_element_type=jnp.float32,
        )
        out_ref[g] = (left * mask_ref[...]).astype(jnp.bfloat16)


def spread_modes(modes, group, depth, after):
    blocks, lanes, columns = modes.shape
    span = columns // group * depth
    return pl.pallas_call(
        functools.partial(spread_kernel, depth),
        out_shape=jax.ShapeDtypeStruct((blocks * group, lanes, span), jnp.bfloat16),
        grid=(blocks,),
        in_specs=[
            pl.BlockSpec((1, lanes, columns), lambda s: (s, 0, 0)),
            pl.BlockSpec(memory_space=pl.ANY),
        ],
        out_specs=pl.BlockSpec((group, lanes, span), lambda s: (s, 0, 0)),
        scratch_shapes=[
            pltpu.VMEM((columns, group * span), jnp.bfloat16),
            pltpu.VMEM((lanes, span), jnp.float32),
        ],
        compiler_params=pltpu.CompilerParams(vmem_limit_bytes=8 * MIB),
        cost_estimate=work(0.2),
        name="spread_modes",
    )(modes, after)


def grad_kernel(chunk, chunks, depth, firsts, aliased, modes_ref, *refs):
    samples = len(firsts)
    rows_refs = refs[:samples]
    out_hbm, other_ref, own_ref, sems = refs[samples + aliased :]
    half_rows = modes_ref.shape[1] // 2
    kept, size, width = other_ref.shape
    half = width // 2
    core = lax.rem(lax.axis_index("dp"), 2)
    first = core == 0
    group = min(16, size // depth)
    tile = group * depth
    steps = size // tile

    def write(s):
        start = pl.multiple_of(s * tile, tile)
        place = pl.multiple_of((core * chunks + chunk) * size + s * tile, tile)
        return pltpu.make_async_copy(
            own_ref.at[:, pl.ds(start, tile), :], out_hbm.at[:, pl.ds(place, tile), :], sems.at[s]
        )

    def body(s, carry):
        for g in range(group):
            start = pl.multiple_of(s * tile + g * depth, depth)
            right = jnp.concatenate(
                [r[pl.ds(at + start, depth), :] for r, at in zip(rows_refs, firsts)], axis=0
            )
            left = modes_ref[(chunk * steps + s) * group + g]
            both = jnp.dot(left, right, preferred_element_type=jnp.float32)
            plain, turned = both[:half_rows], both[half_rows:]
            total = plain + jnp.concatenate([turned[:, half:], -turned[:, :half]], axis=1)
            low, high = total[: half_rows // 2], total[half_rows // 2 :]
            own, other = jnp.where(first, low, high), jnp.where(first, high, low)
            for i in range(kept):
                own_ref[i, pl.ds(start, depth), :] = own[i * depth : (i + 1) * depth]
                other_ref[i, pl.ds(start, depth), :] = other[i * depth : (i + 1) * depth]
        write(s).start()
        return carry

    lax.fori_loop(0, steps, body, 0)
    for s in range(steps):
        write(s).wait()


def grad_chunk(modes, rows, kept, depth, chunk, chunks, previous):
    size, width = rows[0][0].shape[0] // chunks, rows[0][0].shape[1]
    hbm = pl.BlockSpec(memory_space=pl.ANY)
    vmem = pl.BlockSpec(memory_space=pltpu.VMEM)
    operands = [modes, *[array for array, _ in rows]]
    in_specs = [vmem] * len(operands)
    aliases = {}
    if previous is not None:
        in_specs.append(hbm)
        aliases = {len(operands): 0}
        operands.append(previous)
    steps = size // depth // min(16, size // depth)
    firsts = [first for _, first in rows]
    return pl.pallas_call(
        functools.partial(grad_kernel, chunk, chunks, depth, firsts, int(previous is not None)),
        out_shape=[
            jax.ShapeDtypeStruct((kept, 2 * chunks * size, width), jnp.float32),
            jax.ShapeDtypeStruct((kept, size, width), jnp.float32),
        ],
        in_specs=in_specs,
        out_specs=[hbm, vmem],
        scratch_shapes=[
            pltpu.VMEM((kept, size, width), jnp.float32),
            pltpu.SemaphoreType.DMA((steps,)),
        ],
        input_output_aliases=aliases,
        compiler_params=pltpu.CompilerParams(vmem_limit_bytes=24 * MIB),
        cost_estimate=work(1),
        name="grad_chunk",
    )(*operands)


def place_kernel(chunk, chunks, part_ref, old_hbm, out_hbm, sems):
    del old_hbm
    kept, size, _ = part_ref.shape
    core = lax.rem(lax.axis_index("dp"), 2)
    start = pl.multiple_of(((1 - core) * chunks + chunk) * size, size)
    copies = [
        pltpu.make_async_copy(part_ref.at[i], out_hbm.at[i, pl.ds(start, size), :], sems.at[i])
        for i in range(kept)
    ]
    for copy in copies:
        copy.start()
    for copy in copies:
        copy.wait()


def place_chunk(part, result, chunk, chunks):
    hbm = pl.BlockSpec(memory_space=pl.ANY)
    return pl.pallas_call(
        functools.partial(place_kernel, chunk, chunks),
        out_shape=jax.ShapeDtypeStruct(result.shape, result.dtype),
        in_specs=[pl.BlockSpec(memory_space=pltpu.VMEM), hbm],
        out_specs=hbm,
        scratch_shapes=[pltpu.SemaphoreType.DMA((part.shape[0],))],
        input_output_aliases={1: 0},
        compiler_params=pltpu.CompilerParams(vmem_limit_bytes=8 * MIB),
        cost_estimate=work(0.2),
        name="place_chunk",
    )(part, result)


def cast_kernel(parts, rows_hbm, keep_ref, give_ref, held_ref, sems):
    size = held_ref.shape[0] // (2 * parts)
    core = lax.rem(lax.axis_index("dp"), 2)
    halves = [(keep_ref, core * parts), (give_ref, (1 - core) * parts)]
    copies, jobs = [], []
    for h, (out, first) in enumerate(halves):
        for i in range(parts):
            source = pl.ds(pl.multiple_of((first + i) * size, size), size)
            spot = pl.ds((h * parts + i) * size, size)
            copies.append(
                pltpu.make_async_copy(
                    rows_hbm.at[source, :], held_ref.at[spot, :], sems.at[h * parts + i]
                )
            )
            jobs.append((out, pl.ds(i * size, size), spot))
    for copy in copies:
        copy.start()
    for copy, (out, place, spot) in zip(copies, jobs):
        copy.wait()
        out[place, :] = held_ref[spot, :].astype(jnp.bfloat16)


def cast_rows(rows):
    parts = 2
    total, width = rows.shape
    return pl.pallas_call(
        functools.partial(cast_kernel, parts),
        out_shape=[jax.ShapeDtypeStruct((total // 2, width), jnp.bfloat16)] * 2,
        in_specs=[pl.BlockSpec(memory_space=pltpu.HBM)],
        out_specs=[pl.BlockSpec(memory_space=pltpu.VMEM)] * 2,
        scratch_shapes=[
            pltpu.VMEM(rows.shape, jnp.float32),
            pltpu.SemaphoreType.DMA((2 * parts,)),
        ],
        compiler_params=pltpu.CompilerParams(vmem_limit_bytes=8 * MIB),
        cost_estimate=work(0.1),
        name="cast_rows",
    )(*in_hbm(rows))


def chip_ring(chips):
    order = list(range(0, chips, 2))
    return order + [c for c in range(chips - 1, 0, -1) if c % 2]


def ring_perm(chips, step):
    order = chip_ring(chips)
    return [
        (2 * order[p] + core, 2 * order[(p + step) % chips] + core)
        for p in range(chips)
        for core in (0, 1)
    ]


def ring_chip(chip, p, chips):
    up = (chips + 1) // 2
    place = jnp.where(lax.rem(chip, 2) == 0, lax.div(chip, 2), chips - 1 - lax.div(chip, 2))
    spot = lax.rem(place - p + chips, chips)
    return jnp.where(spot < up, 2 * spot, 2 * (chips - 1 - spot) + 1)


def joint_kernel(spans, total, *refs):
    for parts, new in zip(spans, refs[total:]):
        place = 0
        for source, start, size in parts:
            new[place : place + size] = refs[source][start : start + size]
            place += size


def joint(pieces, *after):
    arrays, spans = [], []

    def known(array):
        for i, other in enumerate(arrays):
            if other is array:
                return i
        arrays.append(array)
        return len(arrays) - 1

    for piece in pieces:
        parts = piece if isinstance(piece, list) else [piece]
        parts = [p if isinstance(p, tuple) else (p, 0, p.shape[0]) for p in parts]
        spans.append([(known(array), start, size) for array, start, size in parts])
    vmem = pl.BlockSpec(memory_space=pltpu.VMEM)
    operands = [*arrays, *after]
    return pl.pallas_call(
        functools.partial(joint_kernel, spans, len(operands)),
        out_shape=[
            jax.ShapeDtypeStruct(
                (sum(part[2] for part in parts), *arrays[parts[0][0]].shape[1:]),
                arrays[parts[0][0]].dtype,
            )
            for parts in spans
        ],
        in_specs=[vmem] * len(operands),
        out_specs=[vmem] * len(spans),
        compiler_params=pltpu.CompilerParams(vmem_limit_bytes=8 * MIB),
        cost_estimate=work(0.01),
        name="joint",
    )(*operands)


def per_device(
    point_feats, point_coords, slot_block, slot_cell, slot_count, cotangent, offset_map,
    offset_bias, kernel_mix, lift_weight,
):
    slabs = lax.axis_size("slab")
    devices = lax.axis_size("dp")
    channels = point_feats.shape[2]
    mode_count = cotangent.shape[2]
    capacity = slot_block.shape[3]
    width = cotangent.shape[4]
    planes = GX // slabs
    kept = channels // devices
    slots = slabs * slabs * capacity
    local_x = cotangent.shape[1]
    total = local_x // 2 * mode_count
    chunks = 2
    group = min(8, total // chunks)
    chips = devices // 2
    far = chips // 2

    def up(rows):
        return lax.ppermute(rows, "dp", ring_perm(chips, 1))

    def down(rows):
        return lax.ppermute(rows, "dp", ring_perm(chips, -1))

    def swap(rows):
        return lax.ppermute(rows, "dp", [(d, d ^ 1) for d in range(devices)])

    own, given = cast_rows(cotangent[0].reshape(-1, width))
    size = own.shape[0]
    ups, downs = [up(own)], [down(own)]
    twin = swap(given)
    ups.append(up(twin))
    downs.append(down(twin))

    sent = slot_terms(
        slot_block[0, 0], slot_cell[0, 0], slot_count[0, 0], point_feats[0],
        jnp.swapaxes(point_coords[0], 0, 1), offset_map.T, offset_bias[None], kernel_mix, planes,
        twin,
    )
    terms = [list(sent)] + [
        [lax.ppermute(x, "slab", [(t, (t + s) % slabs) for t in range(slabs)]) for x in sent]
        for s in range(1, slabs)
    ]
    held = {}
    held[1], held[chips - 1], *terms = joint([ups, downs, *terms])

    held[2], held[chips - 2] = up(held[1]), down(held[chips - 1])
    payload = lift_slots(terms, lift_weight, capacity, chips, mode_count)
    recv = lax.all_to_all(
        payload.reshape(chips, -1, GZ), "dp", split_axis=0, concat_axis=0, tiled=True,
        axis_index_groups=[list(range(c, devices, 2)) for c in range(2)],
    ).reshape(payload.shape)
    held[2], held[chips - 2], recv = joint([held[2], held[chips - 2], recv])

    for s in range(3, far):
        held[s], held[chips - s] = up(held[s - 1]), down(held[chips - s + 1])
    scale = 1.0 / math.sqrt(GZ * slabs * slabs * capacity)
    modes = sample_modes(
        [recv, swap(recv)], chips, slabs, slots, planes, scale, group, total, mode_count,
        4 * kept * mode_count,
    )
    half = size // 2
    held[far - 1], held[far + 1], first, second = joint(
        [
            held[far - 1],
            held[far + 1],
            [(held[far - 1], 0, half), (held[far - 1], size, half)],
            [(held[far + 1], half, half), (held[far + 1], size + half, half)],
        ],
        modes,
    )

    ends = [up(first), down(second)]
    modes = spread_modes(modes, group, mode_count, first)

    result, parts = None, []
    for c in range(chunks):
        rows = [(own, c * half), (twin, c * half)]
        for p in range(1, chips):
            if p == far:
                rows += [(ends[c], 0), (ends[c], half)]
            else:
                rows += [(held[p], c * half), (held[p], size + c * half)]
        result, part = grad_chunk(modes, rows, kept, mode_count, c, chunks, result)
        parts.append(swap(part))
    for c, part in enumerate(parts):
        result = place_chunk(part, result, c, chunks)
    return result.reshape(kept, local_x, mode_count, mode_count, width)


def solution(mesh):
    placed = (
        P("dp", "slab", None, None),
        P("dp", "slab", None, None),
        P("dp", "slab", None, None),
        P("dp", "slab", None, None),
        P("dp", "slab", None),
        P("dp", "slab", None, None, None),
        P(),
        P(),
        P(),
        P(),
    )
    return jax.shard_map(
        per_device,
        mesh=mesh,
        in_specs=placed,
        out_specs=P("dp", "slab", None, None, None),
        check_vma=False,
    )
```

time: 78.1 us -> 68.1 us (0.87)
  blocking collectives: 0 us -> 14 us
  starting transfers between devices: 27.6 us -> 14.2 us
  waiting for transfers between devices: 20.7 us -> 15.7 us
  local copies, waits for them, and re-layouts: 3.3 us -> 0.01 us
  Pallas kernels: 25.9 us -> 23.9 us
    ppermute x7 -> x5, waiting for transfers between devices: 16.2 us -> 0.79 us  [down(): return lax.ppermute(rows, 'dp', ring_perm(chips, -1))]
    all_to_all x0 -> x1, blocking collectives: none -> 14 us  [per_device(): lax.all_to_all(payload.reshape(chips, -1, GZ), 'dp', split_axis=0, concat...]
    ppermute x7 -> x5, starting transfers between devices: 13.8 us -> 7.24 us  [down(): return lax.ppermute(rows, 'dp', ring_perm(chips, -1))]
    ppermute x7 -> x5, waiting for transfers between devices: 0.18 us -> 6.38 us  [up(): return lax.ppermute(rows, 'dp', ring_perm(chips, 1))]
    all_to_all x1 -> x0, starting transfers between devices: 6.06 us -> none  [per_device(): lax.all_to_all(payload.reshape(devices * slabs, -1, GZ), ('dp', 'slab'),...]
    unnamed x10 -> x2, local copies, waits for them, and re-layouts: 3.3 us -> 0.01 us
    ppermute x1 -> x2, waiting for transfers between devices: 3.13 us -> 5.87 us  [per_device(): lax.ppermute(x, 'slab', [(t, (t + s) % slabs) for t in range(slabs)])]
    pallas_call x12 -> x10, Pallas kernels: 17.6 us -> 15.6 us  [the longest x2 4.98 us: grad_chunk(): pl.pallas_call(functools.partial(grad_kernel, chunk, chunks, depth, first...]
  transfers between devices with their start and end apart: 19 -> 16, of which waited for: 6 -> 7; matrix products, arithmetic and copies ran while one was open for 0% -> 0% of each run, Pallas kernels for 25% -> 31%
where the time goes in v2:
time: 68.1 us; the launch traced here: 68 us
  Pallas kernels  23.9 us (35%)
  waiting for transfers between devices  15.7 us (23%)
  starting transfers between devices  14.2 us (21%)
  blocking collectives  14 us (21%)
    all_to_all x1, blocking collectives, per_device(): lax.all_to_all(payload.reshape(chips, -1, GZ), 'dp', split_axis=0, concat...  14 us
    ppermute x5, starting transfers between devices, down(): return lax.ppermute(rows, 'dp', ring_perm(chips, -1))  7.24 us
    pallas_call x1, Pallas kernels, slot_terms(): pl.pallas_call(functools.partial(slot_kernel, slabs, planes), out_shape=[...  7.09 us
    ppermute x5, waiting for transfers between devices, up(): return lax.ppermute(rows, 'dp', ring_perm(chips, 1))  6.38 us
    ppermute x2, waiting for transfers between devices, per_device(): lax.ppermute(x, 'slab', [(t, (t + s) % slabs) for t in range(slabs)])  5.87 us
    pallas_call x2, Pallas kernels, grad_chunk(): pl.pallas_call(functools.partial(grad_kernel, chunk, chunks, depth, first...  4.98 us
    ppermute x5, starting transfers between devices, up(): return lax.ppermute(rows, 'dp', ring_perm(chips, 1))  3.74 us
    pallas_call x1, Pallas kernels, spread_modes(): pl.pallas_call(functools.partial(spread_kernel, depth), out_shape=jax.Sha...  3.51 us
  transfers between devices with their start and end apart: 16, of which 7 were waited for; matrix products, arithmetic and copies ran while one was open for 0% of the time, Pallas kernels for 31%

profile of v2, /device:TPU:0, one launch (start us, length us, event | category | flops | bytes accessed | tf_op | source)
XLA Modules:
  0.0 68.0 jit_solution(10782248871308568196)
XLA Ops:
  0.0 1.2 %cast_rows.1 = (bf16[1024,128]{1,0:T(8,128)(2,1)S(1)}, bf16[1024,128]{1,0:T(8,128)(2,1)S(1)}) custom-call(f32[2048,128]{1,0:T(8,128)} %bitcast.15), custom_call_target="tpu_custom_call" | custom-call | flops 100000000 | bytes 1024 | tf_op jit(solution)/shard_map/cast_rows/pallas_call | solution.py:514
  1.8 2.6 %collective-permute-start.3 = (bf16[1024,128]{1,0:T(8,128)(2,1)S(1)}, bf16[1024,128]{1,0:T(8,128)(2,1)S(1)}, u32[]{:S(2)}, u32[]{:S(2)}) collective-permute-start(bf16[1024,128]{1,0:T(8,128)(2,1)S(1)} %get-tuple-element.24.refs_0_), channel_id=1, source_target_pairs={{0,4},{2,6},{8,0},{10,2},{16,8},{18,10},{24,16},{26,18},{28,24},{3... | collective-permute-start | bytes 786440 | tf_op jit(solution)/shard_map/ppermute | solution.py:615
  4.5 1.9 %collective-permute-start.4 = (bf16[1024,128]{1,0:T(8,128)(2,1)S(1)}, bf16[1024,128]{1,0:T(8,128)(2,1)S(1)}, u32[]{:S(2)}, u32[]{:S(2)}) collective-permute-start(bf16[1024,128]{1,0:T(8,128)(2,1)S(1)} %collective-permute-done.1.after_hbm.refs_1_), channel_id=1, source_target_pairs={{0,4},{2,6},{8,0},{10,2},{16,8},{18,10},{24,16},{26,18},{28,24},{3... | collective-permute-start | bytes 786440 | tf_op jit(solution)/shard_map/ppermute | solution.py:615
  6.5 7.1 %slot_terms.1 = (f32[264,128]{1,0:T(8,128)S(1)}, f32[264,128]{1,0:T(8,128)S(1)}) custom-call(s32[2,4]{1,0:T(2,128)} %bitcast.19, s32[2,4]{1,0:T(2,128)} %bitcast.20, s32[2]{0:T(128)} %bitcast.21, bf16[4,64,128]{2,1,0:T(8,128)(2,1)} %bitcast.16, bf16[3,4,128]{2,1,0:T(4,128)(2,1)} %bitcast.17, f32[3,64]{1,0:T(4,128)} %bitcast.18, f32[1,64]{1,0:T(1,128)} %bitcast.22, ...), custom_call_target="tpu_custom_call" | custom-call | flops 1000000000 | bytes 1024 | tf_op jit(solution)/shard_map/slot_terms/pallas_call | solution.py:135
  13.6 2.0 %collective-permute-start.5 = (f32[264,128]{1,0:T(8,128)S(1)}, f32[264,128]{1,0:T(8,128)S(1)}, u32[]{:S(2)}, u32[]{:S(2)}) collective-permute-start(f32[264,128]{1,0:T(8,128)S(1)} %get-tuple-element.26.refs_4_), channel_id=1, source_target_pairs={{0,1},{1,0},{2,3},{3,2},{4,5},{5,4},{6,7},{7,6},{8,9},{9,8},{10,11... | collective-permute-start | bytes 405512 | tf_op jit(solution)/shard_map/ppermute | solution.py:633
  15.7 4.4 %collective-permute-done.5.refs_6_ = f32[264,128]{1,0:T(8,128)S(1)} collective-permute-done((f32[264,128]{1,0:T(8,128)S(1)}, f32[264,128]{1,0:T(8,128)S(1)}, u32[]{:S(2)}, u32[]{:S(2)}) %collective-permute-start.5) | collective-permute-done | bytes 135200 | tf_op jit(solution)/shard_map/ppermute | solution.py:633
  20.1 1.4 %collective-permute-done.6.refs_7_ = f32[264,128]{1,0:T(8,128)S(1)} collective-permute-done((f32[264,128]{1,0:T(8,128)S(1)}, f32[264,128]{1,0:T(8,128)S(1)}, u32[]{:S(2)}, u32[]{:S(2)}) %collective-permute-start.6) | collective-permute-done | bytes 135200 | tf_op jit(solution)/shard_map/ppermute | solution.py:633
  21.7 1.8 %collective-permute-start.7 = (bf16[2048,128]{1,0:T(8,128)(2,1)S(1)}, bf16[2048,128]{1,0:T(8,128)(2,1)S(1)}, u32[]{:S(2)}, u32[]{:S(2)}) collective-permute-start(bf16[2048,128]{1,0:T(8,128)(2,1)S(1)} %get-tuple-element.28.refs_2_.refs_3_), channel_id=1, source_target_pairs={{0,8},{2,10},{8,16},{10,18},{16,24},{18,26},{24,28},{26,30},{28,20... | collective-permute-start | bytes 1572872 | tf_op jit(solution)/shard_map/ppermute | solution.py:612
  23.8 1.9 %lift_slots.1 = f32[320,128]{1,0:T(8,128)S(1)} custom-call(f32[528,128]{1,0:T(8,128)S(1)} %get-tuple-element.30.refs_0_, f32[528,128]{1,0:T(8,128)S(1)} %get-tuple-element.31.refs_1_, bf16[64,64]{1,0:T(8,128)(2,1)S(1)} %copy-done), custom_call_target="tpu_custom_call" | custom-call | flops 100000000 | bytes 1024 | tf_op jit(solution)/shard_map/lift_slots/pallas_call | solution.py:238
  25.7 14.0 %all_to_all.5 = f32[8,40,128]{2,1,0:T(8,128)S(1)} all-to-all(f32[8,40,128]{2,1,0:T(8,128)S(1)} %bitcast.14), channel_id=1, replica_groups={{0,4,8,12,16,20,24,28},{2,6,10,14,18,22,26,30},{1,5,9,13,17,21,25,29},{..., dimensions={0} | all-to-all | bytes 327680 | tf_op jit(solution)/shard_map/all_to_all | solution.py:641
  39.8 1.2 %collective-permute-start.10 = (bf16[2048,128]{1,0:T(8,128)(2,1)S(1)}, bf16[2048,128]{1,0:T(8,128)(2,1)S(1)}, u32[]{:S(2)}, u32[]{:S(2)}) collective-permute-start(bf16[2048,128]{1,0:T(8,128)(2,1)S(1)} %get-tuple-element.33.refs_4_.refs_5_), channel_id=1, source_target_pairs={{0,8},{2,10},{8,16},{10,18},{16,24},{18,26},{24,28},{26,30},{28,20... | collective-permute-start | bytes 1572872 | tf_op jit(solution)/shard_map/ppermute | solution.py:612
  40.9 0.9 %collective-permute-start.11 = (bf16[2048,128]{1,0:T(8,128)(2,1)S(1)}, bf16[2048,128]{1,0:T(8,128)(2,1)S(1)}, u32[]{:S(2)}, u32[]{:S(2)}) collective-permute-start(bf16[2048,128]{1,0:T(8,128)(2,1)S(1)} %get-tuple-element.34.refs_12_.refs_13_), channel_id=1, source_target_pairs={{0,4},{2,6},{8,0},{10,2},{16,8},{18,10},{24,16},{26,18},{28,24},{3... | collective-permute-start | bytes 1572872 | tf_op jit(solution)/shard_map/ppermute | solution.py:615
  41.9 1.4 %collective-permute-done.9.refs_1_ = f32[320,128]{1,0:T(8,128)S(1)} collective-permute-done((f32[320,128]{1,0:T(8,128)S(1)}, f32[320,128]{1,0:T(8,128)S(1)}, u32[]{:S(2)}, u32[]{:S(2)}) %collective-permute-start.9) | collective-permute-done | bytes 163872 | tf_op jit(solution)/shard_map/ppermute | solution.py:618
  43.2 3.0 %sample_modes.1.refs_2_.modes_ref = bf16[8,256,128]{2,1,0:T(8,128)(2,1)S(1)} custom-call(f32[320,128]{1,0:T(8,128)S(1)} %get-tuple-element.32.refs_0_, f32[320,128]{1,0:T(8,128)S(1)} %collective-permute-done.9.refs_1_), custom_call_target="tpu_custom_call" | custom-call | flops 200000000 | bytes 1024 | tf_op jit(solution)/shard_map/sample_modes/pallas_call | solution.py:328
  46.2 5.5 %collective-permute-done.10.refs_0_ = bf16[2048,128]{1,0:T(8,128)(2,1)S(1)} collective-permute-done((bf16[2048,128]{1,0:T(8,128)(2,1)S(1)}, bf16[2048,128]{1,0:T(8,128)(2,1)S(1)}, u32[]{:S(2)}, u32[]{:S(2)}) %collective-permute-start.10) | collective-permute-done | bytes 524320 | tf_op jit(solution)/shard_map/ppermute | solution.py:612
  51.7 0.8 %collective-permute-done.11.refs_1_ = bf16[2048,128]{1,0:T(8,128)(2,1)S(1)} collective-permute-done((bf16[2048,128]{1,0:T(8,128)(2,1)S(1)}, bf16[2048,128]{1,0:T(8,128)(2,1)S(1)}, u32[]{:S(2)}, u32[]{:S(2)}) %collective-permute-start.11) | collective-permute-done | bytes 524320 | tf_op jit(solution)/shard_map/ppermute | solution.py:615
  53.1 1.6 %collective-permute-start.12 = (bf16[1024,128]{1,0:T(8,128)(2,1)S(1)}, bf16[1024,128]{1,0:T(8,128)(2,1)S(1)}, u32[]{:S(2)}, u32[]{:S(2)}) collective-permute-start(bf16[1024,128]{1,0:T(8,128)(2,1)S(1)} %get-tuple-element.37), channel_id=1, source_target_pairs={{0,4},{2,6},{8,0},{10,2},{16,8},{18,10},{24,16},{26,18},{28,24},{3... | collective-permute-start | bytes 786440 | tf_op jit(solution)/shard_map/ppermute | solution.py:615
  54.7 3.5 %spread_modes.1.modes_ref = bf16[64,256,256]{2,1,0:T(8,128)(2,1)S(1)} custom-call(bf16[8,256,128]{2,1,0:T(8,128)(2,1)S(1)} %sample_modes.1.refs_2_.modes_ref, bf16[1024,128]{1,0:T(8,128)(2,1)S(1)} %get-tuple-element.35.after_ref), custom_call_target="tpu_custom_call" | custom-call | flops 200000000 | bytes 1024 | tf_op jit(solution)/shard_map/spread_modes/pallas_call | solution.py:365
  58.2 0.8 %collective-permute-done.13.refs_8_.refs_9_ = bf16[1024,128]{1,0:T(8,128)(2,1)S(1)} collective-permute-done((bf16[1024,128]{1,0:T(8,128)(2,1)S(1)}, bf16[1024,128]{1,0:T(8,128)(2,1)S(1)}, u32[]{:S(2)}, u32[]{:S(2)}) %collective-permute-start.13) | collective-permute-done | bytes 262176 | tf_op jit(solution)/shard_map/ppermute | solution.py:612
  59.1 2.5 %grad_chunk.2 = (f32[4,2048,128]{2,1,0:T(8,128)}, f32[4,512,128]{2,1,0:T(8,128)S(1)}) custom-call(bf16[64,256,256]{2,1,0:T(8,128)(2,1)S(1)} %spread_modes.1.modes_ref, bf16[1024,128]{1,0:T(8,128)(2,1)S(1)} %get-tuple-element.24.refs_0_, bf16[1024,128]{1,0:T(8,128)(2,1)S(1)} %collective-permute-done.1.after_hbm.refs_1_, ...), custom_call_target="tpu_custom_call" | custom-call | flops 1000000000 | bytes 1024 | tf_op jit(solution)/shard_map/grad_chunk/pallas_call | solution.py:440
  61.6 2.5 %grad_chunk.3 = (f32[4,2048,128]{2,1,0:T(8,128)}, f32[4,512,128]{2,1,0:T(8,128)S(1)}) custom-call(bf16[64,256,256]{2,1,0:T(8,128)(2,1)S(1)} %spread_modes.1.modes_ref, bf16[1024,128]{1,0:T(8,128)(2,1)S(1)} %get-tuple-element.24.refs_0_, bf16[1024,128]{1,0:T(8,128)(2,1)S(1)} %collective-permute-done.1.after_hbm.refs_1_, ...), custom_call_target="tpu_custom_call", output_to_operand_aliasing={{0}: (17, {})} | custom-call | flops 1000000000 | bytes 1024 | tf_op jit(solution)/shard_map/grad_chunk/pallas_call | solution.py:440
  64.7 1.0 %place_chunk.2.old_hbm = f32[4,2048,128]{2,1,0:T(8,128)} custom-call(f32[4,512,128]{2,1,0:T(8,128)S(1)} %collective-permute-done.15.part_ref, f32[4,2048,128]{2,1,0:T(8,128)} %get-tuple-element.42.old_hbm), custom_call_target="tpu_custom_call", output_to_operand_aliasing={{}: (1, {})} | custom-call | flops 200000000 | bytes 1024 | tf_op jit(solution)/shard_map/place_chunk/pallas_call | solution.py:476
  65.7 1.3 %collective-permute-done.14.part_ref = f32[4,512,128]{2,1,0:T(8,128)S(1)} collective-permute-done((f32[4,512,128]{2,1,0:T(8,128)S(1)}, f32[4,512,128]{2,1,0:T(8,128)S(1)}, u32[]{:S(2)}, u32[]{:S(2)}) %collective-permute-start.14) | collective-permute-done | bytes 1048608 | tf_op jit(solution)/shard_map/ppermute | solution.py:618
  67.0 1.0 %place_chunk.3 = f32[4,2048,128]{2,1,0:T(8,128)} custom-call(f32[4,512,128]{2,1,0:T(8,128)S(1)} %collective-permute-done.14.part_ref, f32[4,2048,128]{2,1,0:T(8,128)} %place_chunk.2.old_hbm), custom_call_target="tpu_custom_call", output_to_operand_aliasing={{}: (1, {})} | custom-call | flops 200000000 | bytes 1024 | tf_op jit(solution)/shard_map/place_chunk/pallas_call | solution.py:476
  (23 shorter events, 2.6 us)
Async XLA Ops:
  0.0 23.8 %copy-start = (bf16[64,64]{1,0:T(8,128)(2,1)S(1)}, bf16[64,64]{1,0:T(8,128)(2,1)}, u32[]{:S(2)}) copy-start(bf16[64,64]{1,0:T(8,128)(2,1)} %refs_2_.1) | copy-start | bytes 24580
  1.3 3.2 %collective-permute-start.1 = (bf16[1024,128]{1,0:T(8,128)(2,1)S(1)}, bf16[1024,128]{1,0:T(8,128)(2,1)S(1)}, u32[]{:S(2)}, u32[]{:S(2)}) collective-permute-start(bf16[1024,128]{1,0:T(8,128)(2,1)S(1)} %get-tuple-element.25), channel_id=1, source_target_pairs={{0,2},{2,0},{4,6},{6,4},{8,10},{10,8},{12,14},{14,12},{16,18},{18,... | collective-permute-start | bytes 786440 | tf_op jit(solution)/shard_map/ppermute | solution.py:618
  1.8 13.8 %collective-permute-start.3 = (bf16[1024,128]{1,0:T(8,128)(2,1)S(1)}, bf16[1024,128]{1,0:T(8,128)(2,1)S(1)}, u32[]{:S(2)}, u32[]{:S(2)}) collective-permute-start(bf16[1024,128]{1,0:T(8,128)(2,1)S(1)} %get-tuple-element.24.refs_0_), channel_id=1, source_target_pairs={{0,4},{2,6},{8,0},{10,2},{16,8},{18,10},{24,16},{26,18},{28,24},{3... | collective-permute-start | bytes 786440 | tf_op jit(solution)/shard_map/ppermute | solution.py:615
  4.3 11.4 %collective-permute-start = (bf16[1024,128]{1,0:T(8,128)(2,1)S(1)}, bf16[1024,128]{1,0:T(8,128)(2,1)S(1)}, u32[]{:S(2)}, u32[]{:S(2)}) collective-permute-start(bf16[1024,128]{1,0:T(8,128)(2,1)S(1)} %get-tuple-element.24.refs_0_), channel_id=1, source_target_pairs={{0,8},{2,10},{8,16},{10,18},{16,24},{18,26},{24,28},{26,30},{28,20... | collective-permute-start | bytes 786440 | tf_op jit(solution)/shard_map/ppermute | solution.py:612
  4.5 17.1 %collective-permute-start.4 = (bf16[1024,128]{1,0:T(8,128)(2,1)S(1)}, bf16[1024,128]{1,0:T(8,128)(2,1)S(1)}, u32[]{:S(2)}, u32[]{:S(2)}) collective-permute-start(bf16[1024,128]{1,0:T(8,128)(2,1)S(1)} %collective-permute-done.1.after_hbm.refs_1_), channel_id=1, source_target_pairs={{0,4},{2,6},{8,0},{10,2},{16,8},{18,10},{24,16},{26,18},{28,24},{3... | collective-permute-start | bytes 786440 | tf_op jit(solution)/shard_map/ppermute | solution.py:615
  6.4 15.2 %collective-permute-start.2 = (bf16[1024,128]{1,0:T(8,128)(2,1)S(1)}, bf16[1024,128]{1,0:T(8,128)(2,1)S(1)}, u32[]{:S(2)}, u32[]{:S(2)}) collective-permute-start(bf16[1024,128]{1,0:T(8,128)(2,1)S(1)} %collective-permute-done.1.after_hbm.refs_1_), channel_id=1, source_target_pairs={{0,8},{2,10},{8,16},{10,18},{16,24},{18,26},{24,28},{26,30},{28,20... | collective-permute-start | bytes 786440 | tf_op jit(solution)/shard_map/ppermute | solution.py:612
  13.6 6.5 %collective-permute-start.5 = (f32[264,128]{1,0:T(8,128)S(1)}, f32[264,128]{1,0:T(8,128)S(1)}, u32[]{:S(2)}, u32[]{:S(2)}) collective-permute-start(f32[264,128]{1,0:T(8,128)S(1)} %get-tuple-element.26.refs_4_), channel_id=1, source_target_pairs={{0,1},{1,0},{2,3},{3,2},{4,5},{5,4},{6,7},{7,6},{8,9},{9,8},{10,11... | collective-permute-start | bytes 405512 | tf_op jit(solution)/shard_map/ppermute | solution.py:633
  15.6 6.0 %collective-permute-start.6 = (f32[264,128]{1,0:T(8,128)S(1)}, f32[264,128]{1,0:T(8,128)S(1)}, u32[]{:S(2)}, u32[]{:S(2)}) collective-permute-start(f32[264,128]{1,0:T(8,128)S(1)} %get-tuple-element.27.refs_5_), channel_id=1, source_target_pairs={{0,1},{1,0},{2,3},{3,2},{4,5},{5,4},{6,7},{7,6},{8,9},{9,8},{10,11... | collective-permute-start | bytes 405512 | tf_op jit(solution)/shard_map/ppermute | solution.py:633
  21.7 18.0 %collective-permute-start.7 = (bf16[2048,128]{1,0:T(8,128)(2,1)S(1)}, bf16[2048,128]{1,0:T(8,128)(2,1)S(1)}, u32[]{:S(2)}, u32[]{:S(2)}) collective-permute-start(bf16[2048,128]{1,0:T(8,128)(2,1)S(1)} %get-tuple-element.28.refs_2_.refs_3_), channel_id=1, source_target_pairs={{0,8},{2,10},{8,16},{10,18},{16,24},{18,26},{24,28},{26,30},{28,20... | collective-permute-start | bytes 1572872 | tf_op jit(solution)/shard_map/ppermute | solution.py:612
  23.5 16.2 %collective-permute-start.8 = (bf16[2048,128]{1,0:T(8,128)(2,1)S(1)}, bf16[2048,128]{1,0:T(8,128)(2,1)S(1)}, u32[]{:S(2)}, u32[]{:S(2)}) collective-permute-start(bf16[2048,128]{1,0:T(8,128)(2,1)S(1)} %get-tuple-element.29.refs_14_.refs_15_), channel_id=1, source_target_pairs={{0,4},{2,6},{8,0},{10,2},{16,8},{18,10},{24,16},{26,18},{28,24},{3... | collective-permute-start | bytes 1572872 | tf_op jit(solution)/shard_map/ppermute | solution.py:615
  39.8 12.0 %collective-permute-start.10 = (bf16[2048,128]{1,0:T(8,128)(2,1)S(1)}, bf16[2048,128]{1,0:T(8,128)(2,1)S(1)}, u32[]{:S(2)}, u32[]{:S(2)}) collective-permute-start(bf16[2048,128]{1,0:T(8,128)(2,1)S(1)} %get-tuple-element.33.refs_4_.refs_5_), channel_id=1, source_target_pairs={{0,8},{2,10},{8,16},{10,18},{16,24},{18,26},{24,28},{26,30},{28,20... | collective-permute-start | bytes 1572872 | tf_op jit(solution)/shard_map/ppermute | solution.py:612
  40.9 11.6 %collective-permute-start.11 = (bf16[2048,128]{1,0:T(8,128)(2,1)S(1)}, bf16[2048,128]{1,0:T(8,128)(2,1)S(1)}, u32[]{:S(2)}, u32[]{:S(2)}) collective-permute-start(bf16[2048,128]{1,0:T(8,128)(2,1)S(1)} %get-tuple-element.34.refs_12_.refs_13_), channel_id=1, source_target_pairs={{0,4},{2,6},{8,0},{10,2},{16,8},{18,10},{24,16},{26,18},{28,24},{3... | collective-permute-start | bytes 1572872 | tf_op jit(solution)/shard_map/ppermute | solution.py:615
  41.9 1.4 %collective-permute-start.9 = (f32[320,128]{1,0:T(8,128)S(1)}, f32[320,128]{1,0:T(8,128)S(1)}, u32[]{:S(2)}, u32[]{:S(2)}) collective-permute-start(f32[320,128]{1,0:T(8,128)S(1)} %get-tuple-element.32.refs_0_), channel_id=1, source_target_pairs={{0,2},{2,0},{4,6},{6,4},{8,10},{10,8},{12,14},{14,12},{16,18},{18,... | collective-permute-start | bytes 491528 | tf_op jit(solution)/shard_map/ppermute | solution.py:618
  52.6 6.4 %collective-permute-start.13 = (bf16[1024,128]{1,0:T(8,128)(2,1)S(1)}, bf16[1024,128]{1,0:T(8,128)(2,1)S(1)}, u32[]{:S(2)}, u32[]{:S(2)}) collective-permute-start(bf16[1024,128]{1,0:T(8,128)(2,1)S(1)} %get-tuple-element.35.after_ref), channel_id=1, source_target_pairs={{0,8},{2,10},{8,16},{10,18},{16,24},{18,26},{24,28},{26,30},{28,20... | collective-permute-start | bytes 786440 | tf_op jit(solution)/shard_map/ppermute | solution.py:612
  53.1 8.6 %collective-permute-start.12 = (bf16[1024,128]{1,0:T(8,128)(2,1)S(1)}, bf16[1024,128]{1,0:T(8,128)(2,1)S(1)}, u32[]{:S(2)}, u32[]{:S(2)}) collective-permute-start(bf16[1024,128]{1,0:T(8,128)(2,1)S(1)} %get-tuple-element.37), channel_id=1, source_target_pairs={{0,4},{2,6},{8,0},{10,2},{16,8},{18,10},{24,16},{26,18},{28,24},{3... | collective-permute-start | bytes 786440 | tf_op jit(solution)/shard_map/ppermute | solution.py:615
  61.5 3.1 %collective-permute-start.15 = (f32[4,512,128]{2,1,0:T(8,128)S(1)}, f32[4,512,128]{2,1,0:T(8,128)S(1)}, u32[]{:S(2)}, u32[]{:S(2)}) collective-permute-start(f32[4,512,128]{2,1,0:T(8,128)S(1)} %get-tuple-element.41), channel_id=1, source_target_pairs={{0,2},{2,0},{4,6},{6,4},{8,10},{10,8},{12,14},{14,12},{16,18},{18,... | collective-permute-start | bytes 3145736 | tf_op jit(solution)/shard_map/ppermute | solution.py:618
  64.1 2.8 %collective-permute-start.14 = (f32[4,512,128]{2,1,0:T(8,128)S(1)}, f32[4,512,128]{2,1,0:T(8,128)S(1)}, u32[]{:S(2)}, u32[]{:S(2)}) collective-permute-start(f32[4,512,128]{2,1,0:T(8,128)S(1)} %get-tuple-element.40), channel_id=1, source_target_pairs={{0,2},{2,0},{4,6},{6,4},{8,10},{10,8},{12,14},{14,12},{16,18},{18,... | collective-permute-start | bytes 3145736 | tf_op jit(solution)/shard_map/ppermute | solution.py:618

commit v3 on v2

--- a/solution.py
+++ b/solution.py
@@ -156,7 +156,8 @@
 
 def lift_kernel(slabs, capacity, dests, mode_count, *refs):
     terms = refs[:slabs]
-    lift_ref, out_ref, tag_ref, row_ref, wide_ref, table_ref = refs[slabs:]
+    lift_ref, out_ref, token_ref, tag_ref, row_ref, wide_ref, table_ref = refs[slabs:]
+    token_ref[...] = jnp.zeros_like(token_ref)
     channels = lift_ref.shape[0]
     kept = channels // dests
     group = slabs * capacity
@@ -237,9 +238,12 @@
     vmem = pl.BlockSpec(memory_space=pltpu.VMEM)
     return pl.pallas_call(
         functools.partial(lift_kernel, slabs, capacity, dests, mode_count),
-        out_shape=jax.ShapeDtypeStruct((dests * per, GZ), jnp.float32),
+        out_shape=[
+            jax.ShapeDtypeStruct((dests * per, GZ), jnp.float32),
+            jax.ShapeDtypeStruct((8, GZ), jnp.float32),
+        ],
         in_specs=[vmem] * (slabs + 1),
-        out_specs=vmem,
+        out_specs=[vmem] * 2,
         scratch_shapes=[
             pltpu.VMEM((slots, GZ), jnp.float32),
             pltpu.VMEM((slabs * capacity, channels, GZ), jnp.float32),
@@ -256,7 +260,8 @@
 
 def modes_kernel(chips, slabs, slots, planes, scale, group, mode_count, *refs):
     recv_refs = refs[:2]
-    out_ref, all_ref = refs[2:]
+    out_ref, token_ref, all_ref = refs[2:]
+    token_ref[...] = jnp.zeros_like(token_ref)
     samples = 2 * chips
     tiles = all_ref.shape[0]
     total = all_ref.shape[1] // samples
@@ -312,7 +317,7 @@
                 )
         return carry
 
-    lax.fori_loop(0, chips, body, 0, unroll=2)
+    lax.fori_loop(0, chips, body, 0, unroll=4)
 
     span = group * samples
     for block in range(total // group):
@@ -327,9 +332,12 @@
     vmem = pl.BlockSpec(memory_space=pltpu.VMEM)
     return pl.pallas_call(
         functools.partial(modes_kernel, chips, slabs, slots, planes, scale, group, mode_count),
-        out_shape=jax.ShapeDtypeStruct((total // group, lanes, group * samples), jnp.bfloat16),
+        out_shape=[
+            jax.ShapeDtypeStruct((total // group, lanes, group * samples), jnp.bfloat16),
+            jax.ShapeDtypeStruct((8, GZ), jnp.float32),
+        ],
         in_specs=[vmem] * len(recv),
-        out_specs=vmem,
+        out_specs=[vmem] * 2,
         scratch_shapes=[pltpu.VMEM((lanes // GZ, total * samples, GZ), jnp.float32)],
         compiler_params=pltpu.CompilerParams(vmem_limit_bytes=(8 if slabs <= 2 else 32) * MIB),
         cost_estimate=work(0.2),
@@ -382,9 +390,8 @@
 
 
 def grad_kernel(chunk, chunks, depth, firsts, aliased, modes_ref, *refs):
-    samples = len(firsts)
-    rows_refs = refs[:samples]
-    out_hbm, other_ref, own_ref, sems = refs[samples + aliased :]
+    count = 1 + max(index for index, _ in firsts)
+    out_hbm, other_ref, own_ref, sems = refs[count + aliased :]
     half_rows = modes_ref.shape[1] // 2
     kept, size, width = other_ref.shape
     half = width // 2
@@ -401,11 +408,11 @@
             own_ref.at[:, pl.ds(start, tile), :], out_hbm.at[:, pl.ds(place, tile), :], sems.at[s]
         )
 
-    def body(s, carry):
+    for s in range(steps):
         for g in range(group):
-            start = pl.multiple_of(s * tile + g * depth, depth)
+            start = s * tile + g * depth
             right = jnp.concatenate(
-                [r[pl.ds(at + start, depth), :] for r, at in zip(rows_refs, firsts)], axis=0
+                [refs[i][at + start : at + start + depth, :] for i, at in firsts], axis=0
             )
             left = modes_ref[(chunk * steps + s) * group + g]
             both = jnp.dot(left, right, preferred_element_type=jnp.float32)
@@ -417,18 +424,20 @@
                 own_ref[i, pl.ds(start, depth), :] = own[i * depth : (i + 1) * depth]
                 other_ref[i, pl.ds(start, depth), :] = other[i * depth : (i + 1) * depth]
         write(s).start()
-        return carry
-
-    lax.fori_loop(0, steps, body, 0)
     for s in range(steps):
         write(s).wait()
 
 
 def grad_chunk(modes, rows, kept, depth, chunk, chunks, previous):
-    size, width = rows[0][0].shape[0] // chunks, rows[0][0].shape[1]
+    arrays, firsts = [], []
+    for array, first in rows:
+        if not any(array is known for known in arrays):
+            arrays.append(array)
+        firsts.append(([array is known for known in arrays].index(True), first))
+    size, width = arrays[0].shape[0] // chunks, arrays[0].shape[1]
     hbm = pl.BlockSpec(memory_space=pl.ANY)
     vmem = pl.BlockSpec(memory_space=pltpu.VMEM)
-    operands = [modes, *[array for array, _ in rows]]
+    operands = [modes, *arrays]
     in_specs = [vmem] * len(operands)
     aliases = {}
     if previous is not None:
@@ -436,7 +445,6 @@
         aliases = {len(operands): 0}
         operands.append(previous)
     steps = size // depth // min(16, size // depth)
-    firsts = [first for _, first in rows]
     return pl.pallas_call(
         functools.partial(grad_kernel, chunk, chunks, depth, firsts, int(previous is not None)),
         out_shape=[
@@ -450,7 +458,7 @@
             pltpu.SemaphoreType.DMA((steps,)),
         ],
         input_output_aliases=aliases,
-        compiler_params=pltpu.CompilerParams(vmem_limit_bytes=24 * MIB),
+        compiler_params=pltpu.CompilerParams(vmem_limit_bytes=12 * MIB),
         cost_estimate=work(1),
         name="grad_chunk",
     )(*operands)
@@ -461,9 +469,16 @@
     kept, size, _ = part_ref.shape
     core = lax.rem(lax.axis_index("dp"), 2)
     start = pl.multiple_of(((1 - core) * chunks + chunk) * size, size)
+    cuts = sems.shape[0] // kept
+    rows = size // cuts
     copies = [
-        pltpu.make_async_copy(part_ref.at[i], out_hbm.at[i, pl.ds(start, size), :], sems.at[i])
+        pltpu.make_async_copy(
+            part_ref.at[i, pl.ds(c * rows, rows), :],
+            out_hbm.at[i, pl.ds(start + c * rows, rows), :],
+            sems.at[i * cuts + c],
+        )
         for i in range(kept)
+        for c in range(cuts)
     ]
     for copy in copies:
         copy.start()
@@ -582,7 +597,7 @@
         ],
         in_specs=[vmem] * len(operands),
         out_specs=[vmem] * len(spans),
-        compiler_params=pltpu.CompilerParams(vmem_limit_bytes=8 * MIB),
+        compiler_params=pltpu.CompilerParams(vmem_limit_bytes=4 * MIB),
         cost_estimate=work(0.01),
         name="joint",
     )(*operands)
@@ -608,6 +623,8 @@
     chips = devices // 2
     far = chips // 2
 
+    scale = 1.0 / math.sqrt(GZ * slabs * slabs * capacity)
+
     def up(rows):
         return lax.ppermute(rows, "dp", ring_perm(chips, 1))
 
@@ -629,37 +646,41 @@
         jnp.swapaxes(point_coords[0], 0, 1), offset_map.T, offset_bias[None], kernel_mix, planes,
         twin,
     )
-    terms = [list(sent)] + [
+    pair = {}
+    *outs, first, second = joint([*ups, *downs, *sent])
+    pair[1], pair[chips - 1], sent = outs[:2], outs[2:], [first, second]
+
+    pair[2] = [up(rows) for rows in pair[1]]
+    pair[chips - 2] = [down(rows) for rows in pair[chips - 1]]
+    terms = [sent] + [
         [lax.ppermute(x, "slab", [(t, (t + s) % slabs) for t in range(slabs)]) for x in sent]
         for s in range(1, slabs)
     ]
-    held = {}
-    held[1], held[chips - 1], *terms = joint([ups, downs, *terms])
-
-    held[2], held[chips - 2] = up(held[1]), down(held[chips - 1])
-    payload = lift_slots(terms, lift_weight, capacity, chips, mode_count)
+    terms = joint(terms)
+    payload, lift_done = lift_slots(terms, lift_weight, capacity, chips, mode_count)
     recv = lax.all_to_all(
         payload.reshape(chips, -1, GZ), "dp", split_axis=0, concat_axis=0, tiled=True,
         axis_index_groups=[list(range(c, devices, 2)) for c in range(2)],
     ).reshape(payload.shape)
-    held[2], held[chips - 2], recv = joint([held[2], held[chips - 2], recv])
+    outs = joint([*pair[2], *pair[chips - 2]], lift_done)
+    sent_on = {2: outs[:2], chips - 2: outs[2:]}
 
     for s in range(3, far):
-        held[s], held[chips - s] = up(held[s - 1]), down(held[chips - s + 1])
-    scale = 1.0 / math.sqrt(GZ * slabs * slabs * capacity)
-    modes = sample_modes(
+        pair[s] = [up(rows) for rows in sent_on.get(s - 1, pair[s - 1])]
+        pair[chips - s] = [
+            down(rows) for rows in sent_on.get(chips - s + 1, pair[chips - s + 1])
+        ]
+    modes, modes_done = sample_modes(
         [recv, swap(recv)], chips, slabs, slots, planes, scale, group, total, mode_count,
         4 * kept * mode_count,
     )
     half = size // 2
-    held[far - 1], held[far + 1], first, second = joint(
+    first, second = joint(
         [
-            held[far - 1],
-            held[far + 1],
-            [(held[far - 1], 0, half), (held[far - 1], size, half)],
-            [(held[far + 1], half, half), (held[far + 1], size + half, half)],
-        ],
-        modes,
+            [(rows, 0, half) for rows in pair[far - 1]],
+            [(rows, half, half) for rows in pair[far + 1]],
+        ],
+        modes_done,
     )
 
     ends = [up(first), down(second)]
@@ -672,7 +693,7 @@
             if p == far:
                 rows += [(ends[c], 0), (ends[c], half)]
             else:
-                rows += [(held[p], c * half), (held[p], size + c * half)]
+                rows += [(array, c * half) for array in pair[p]]
         result, part = grad_chunk(modes, rows, kept, mode_count, c, chunks, result)
         parts.append(swap(part))
     for c, part in enumerate(parts):

time: 68.1 us -> 65.6 us (0.963)
  blocking collectives: 14 us -> 0 us
  starting transfers between devices: 14.2 us -> 22.9 us
  Pallas kernels: 23.9 us -> 25.3 us
  waiting for transfers between devices: 15.7 us -> 17 us
    all_to_all x1 -> x0, blocking collectives: 14 us -> none  [per_device(): lax.all_to_all(payload.reshape(chips, -1, GZ), 'dp', split_axis=0, concat...]
    ppermute x5 -> x7, waiting for transfers between devices: 0.79 us -> 6.41 us  [down(): return lax.ppermute(rows, 'dp', ring_perm(chips, -1))]
    all_to_all x0 -> x1, starting transfers between devices: none -> 4.79 us  [per_device(): lax.all_to_all(payload.reshape(chips, -1, GZ), 'dp', split_axis=0, concat...]
    ppermute x2, waiting for transfers between devices: 5.87 us -> 1.85 us  [per_device(): lax.ppermute(x, 'slab', [(t, (t + s) % slabs) for t in range(slabs)])]
    ppermute x5 -> x7, starting transfers between devices: 3.74 us -> 7.01 us  [up(): return lax.ppermute(rows, 'dp', ring_perm(chips, 1))]
    ppermute x5 -> x7, waiting for transfers between devices: 6.38 us -> 3.33 us  [up(): return lax.ppermute(rows, 'dp', ring_perm(chips, 1))]
    all_to_all x0 -> x1, waiting for transfers between devices: none -> 2.52 us  [per_device(): lax.all_to_all(payload.reshape(chips, -1, GZ), 'dp', split_axis=0, concat...]
    pallas_call x3 -> x4, Pallas kernels: 0.28 us -> 1.19 us  [joint(): pl.pallas_call(functools.partial(joint_kernel, spans, len(operands)), out...]
  transfers between devices with their start and end apart: 16 -> 21, of which waited for: 7 -> 10; matrix products, arithmetic and copies ran while one was open for 0% -> 0% of each run, Pallas kernels for 31% -> 35%
where the time goes in v3:
time: 65.6 us; the launch traced here: 65.4 us
  Pallas kernels  25.3 us (39%)
  starting transfers between devices  22.9 us (35%)
  waiting for transfers between devices  17 us (26%)
    ppermute x7, starting transfers between devices, down(): return lax.ppermute(rows, 'dp', ring_perm(chips, -1))  7.84 us
    pallas_call x1, Pallas kernels, slot_terms(): pl.pallas_call(functools.partial(slot_kernel, slabs, planes), out_shape=[...  7.09 us
    ppermute x7, starting transfers between devices, up(): return lax.ppermute(rows, 'dp', ring_perm(chips, 1))  7.01 us
    ppermute x7, waiting for transfers between devices, down(): return lax.ppermute(rows, 'dp', ring_perm(chips, -1))  6.41 us
    all_to_all x1, starting transfers between devices, per_device(): lax.all_to_all(payload.reshape(chips, -1, GZ), 'dp', split_axis=0, concat...  4.79 us
    pallas_call x2, Pallas kernels, grad_chunk(): pl.pallas_call(functools.partial(grad_kernel, chunk, chunks, depth, first...  4.32 us
    pallas_call x1, Pallas kernels, spread_modes(): pl.pallas_call(functools.partial(spread_kernel, depth), out_shape=jax.Sha...  3.53 us
    pallas_call x1, Pallas kernels, sample_modes(): pl.pallas_call(functools.partial(modes_kernel, chips, slabs, slots, plane...  3.43 us
  transfers between devices with their start and end apart: 21, of which 10 were waited for; matrix products, arithmetic and copies ran while one was open for 0% of the time, Pallas kernels for 35%

profile of v3, /device:TPU:0, one launch (start us, length us, event | category | flops | bytes accessed | tf_op | source)
XLA Modules:
  0.0 65.4 jit_solution(6439642057914237487)
XLA Ops:
  0.0 1.2 %cast_rows.1 = (bf16[1024,128]{1,0:T(8,128)(2,1)S(1)}, bf16[1024,128]{1,0:T(8,128)(2,1)S(1)}) custom-call(f32[2048,128]{1,0:T(8,128)} %bitcast.13), custom_call_target="tpu_custom_call" | custom-call | flops 100000000 | bytes 1024 | tf_op jit(solution)/shard_map/cast_rows/pallas_call | solution.py:529
  1.8 2.6 %collective-permute-start.3 = (bf16[1024,128]{1,0:T(8,128)(2,1)S(1)}, bf16[1024,128]{1,0:T(8,128)(2,1)S(1)}, u32[]{:S(2)}, u32[]{:S(2)}) collective-permute-start(bf16[1024,128]{1,0:T(8,128)(2,1)S(1)} %get-tuple-element.31.refs_0_), channel_id=1, source_target_pairs={{0,4},{2,6},{8,0},{10,2},{16,8},{18,10},{24,16},{26,18},{28,24},{3... | collective-permute-start | bytes 786440 | tf_op jit(solution)/shard_map/ppermute | solution.py:632
  4.5 1.9 %collective-permute-start.4 = (bf16[1024,128]{1,0:T(8,128)(2,1)S(1)}, bf16[1024,128]{1,0:T(8,128)(2,1)S(1)}, u32[]{:S(2)}, u32[]{:S(2)}) collective-permute-start(bf16[1024,128]{1,0:T(8,128)(2,1)S(1)} %collective-permute-done.1.after_hbm.refs_1_), channel_id=1, source_target_pairs={{0,4},{2,6},{8,0},{10,2},{16,8},{18,10},{24,16},{26,18},{28,24},{3... | collective-permute-start | bytes 786440 | tf_op jit(solution)/shard_map/ppermute | solution.py:632
  6.5 7.1 %slot_terms.1 = (f32[264,128]{1,0:T(8,128)S(1)}, f32[264,128]{1,0:T(8,128)S(1)}) custom-call(s32[2,4]{1,0:T(2,128)} %bitcast.17, s32[2,4]{1,0:T(2,128)} %bitcast.18, s32[2]{0:T(128)} %bitcast.19, bf16[4,64,128]{2,1,0:T(8,128)(2,1)} %bitcast.14, bf16[3,4,128]{2,1,0:T(4,128)(2,1)} %bitcast.15, f32[3,64]{1,0:T(4,128)} %bitcast.16, f32[1,64]{1,0:T(1,128)} %bitcast.20, ...), custom_call_target="tpu_custom_call" | custom-call | flops 1000000000 | bytes 1024 | tf_op jit(solution)/shard_map/slot_terms/pallas_call | solution.py:135
  13.6 3.3 %collective-permute-done.4.refs_3_ = bf16[1024,128]{1,0:T(8,128)(2,1)S(1)} collective-permute-done((bf16[1024,128]{1,0:T(8,128)(2,1)S(1)}, bf16[1024,128]{1,0:T(8,128)(2,1)S(1)}, u32[]{:S(2)}, u32[]{:S(2)}) %collective-permute-start.4) | collective-permute-done | bytes 262176 | tf_op jit(solution)/shard_map/ppermute | solution.py:632
  16.9 1.4 %collective-permute-done.2.refs_1_ = bf16[1024,128]{1,0:T(8,128)(2,1)S(1)} collective-permute-done((bf16[1024,128]{1,0:T(8,128)(2,1)S(1)}, bf16[1024,128]{1,0:T(8,128)(2,1)S(1)}, u32[]{:S(2)}, u32[]{:S(2)}) %collective-permute-start.2) | collective-permute-done | bytes 262176 | tf_op jit(solution)/shard_map/ppermute | solution.py:629
  18.4 1.6 %collective-permute-start.5 = (f32[264,128]{1,0:T(8,128)S(1)}, f32[264,128]{1,0:T(8,128)S(1)}, u32[]{:S(2)}, u32[]{:S(2)}) collective-permute-start(f32[264,128]{1,0:T(8,128)S(1)} %get-tuple-element.35.refs_0_), channel_id=1, source_target_pairs={{0,1},{1,0},{2,3},{3,2},{4,5},{5,4},{6,7},{7,6},{8,9},{9,8},{10,11... | collective-permute-start | bytes 405512 | tf_op jit(solution)/shard_map/ppermute | solution.py:656
  20.9 1.7 %collective-permute-start.9 = (bf16[1024,128]{1,0:T(8,128)(2,1)S(1)}, bf16[1024,128]{1,0:T(8,128)(2,1)S(1)}, u32[]{:S(2)}, u32[]{:S(2)}) collective-permute-start(bf16[1024,128]{1,0:T(8,128)(2,1)S(1)} %get-tuple-element.42.refs_3_), channel_id=1, source_target_pairs={{0,8},{2,10},{8,16},{10,18},{16,24},{18,26},{24,28},{26,30},{28,20... | collective-permute-start | bytes 786440 | tf_op jit(solution)/shard_map/ppermute | solution.py:629
  22.9 1.9 %collective-permute-done.5.refs_2_ = f32[264,128]{1,0:T(8,128)S(1)} collective-permute-done((f32[264,128]{1,0:T(8,128)S(1)}, f32[264,128]{1,0:T(8,128)S(1)}, u32[]{:S(2)}, u32[]{:S(2)}) %collective-permute-start.5) | collective-permute-done | bytes 135200 | tf_op jit(solution)/shard_map/ppermute | solution.py:656
  24.8 1.6 %collective-permute-start.11 = (bf16[1024,128]{1,0:T(8,128)(2,1)S(1)}, bf16[1024,128]{1,0:T(8,128)(2,1)S(1)}, u32[]{:S(2)}, u32[]{:S(2)}) collective-permute-start(bf16[1024,128]{1,0:T(8,128)(2,1)S(1)} %get-tuple-element.44.refs_14_), channel_id=1, source_target_pairs={{0,4},{2,6},{8,0},{10,2},{16,8},{18,10},{24,16},{26,18},{28,24},{3... | collective-permute-start | bytes 786440 | tf_op jit(solution)/shard_map/ppermute | solution.py:632
  26.4 2.5 %lift_slots.1 = (f32[320,128]{1,0:T(8,128)}, f32[8,128]{1,0:T(8,128)S(1)}) custom-call(f32[528,128]{1,0:T(8,128)S(1)} %get-tuple-element.37.refs_0_, f32[528,128]{1,0:T(8,128)S(1)} %get-tuple-element.38.refs_1_, bf16[64,64]{1,0:T(8,128)(2,1)S(1)} %copy-done.2), custom_call_target="tpu_custom_call" | custom-call | flops 100000000 | bytes 1024 | tf_op jit(solution)/shard_map/lift_slots/pallas_call | solution.py:239
  28.9 4.8 %all-to-all-start = ((f32[8,40,128]{2,1,0:T(8,128)}), f32[8,40,128]{2,1,0:T(8,128)}, u32[]{:S(2)}, u32[]{:S(2)}) async-start(f32[8,40,128]{2,1,0:T(8,128)} %bitcast.9), calls=%async_computation | async-start | bytes 327680 | tf_op jit(solution)/shard_map/all_to_all | solution.py:661
  33.7 1.2 %collective-permute-done.11.refs_3_.refs_12_ = bf16[1024,128]{1,0:T(8,128)(2,1)S(1)} collective-permute-done((bf16[1024,128]{1,0:T(8,128)(2,1)S(1)}, bf16[1024,128]{1,0:T(8,128)(2,1)S(1)}, u32[]{:S(2)}, u32[]{:S(2)}) %collective-permute-start.11) | collective-permute-done | bytes 262176 | tf_op jit(solution)/shard_map/ppermute | solution.py:632
  36.0 1.6 %collective-permute-start.12 = (bf16[1024,128]{1,0:T(8,128)(2,1)}, bf16[1024,128]{1,0:T(8,128)(2,1)S(1)}, u32[]{:S(2)}, u32[]{:S(2)}) collective-permute-start(bf16[1024,128]{1,0:T(8,128)(2,1)} %get-tuple-element.46), channel_id=1, source_target_pairs={{0,8},{2,10},{8,16},{10,18},{16,24},{18,26},{24,28},{26,30},{28,20... | collective-permute-start | bytes 786440 | tf_op jit(solution)/shard_map/ppermute | solution.py:629
  37.6 1.5 %collective-permute-start.13 = (bf16[1024,128]{1,0:T(8,128)(2,1)}, bf16[1024,128]{1,0:T(8,128)(2,1)S(1)}, u32[]{:S(2)}, u32[]{:S(2)}) collective-permute-start(bf16[1024,128]{1,0:T(8,128)(2,1)} %get-tuple-element.47), channel_id=1, source_target_pairs={{0,8},{2,10},{8,16},{10,18},{16,24},{18,26},{24,28},{26,30},{28,20... | collective-permute-start | bytes 786440 | tf_op jit(solution)/shard_map/ppermute | solution.py:629
  40.0 2.5 %all-to-all-done = f32[8,40,128]{2,1,0:T(8,128)} async-done(((f32[8,40,128]{2,1,0:T(8,128)}), f32[8,40,128]{2,1,0:T(8,128)}, u32[]{:S(2)}, u32[]{:S(2)}) %all-to-all-start) | async-done | bytes 163872 | tf_op jit(solution)/shard_map/all_to_all | solution.py:661
  42.5 1.6 %collective-permute-done.7.refs_1_ = f32[320,128]{1,0:T(8,128)S(1)} collective-permute-done((f32[320,128]{1,0:T(8,128)}, f32[320,128]{1,0:T(8,128)S(1)}, u32[]{:S(2)}, u32[]{:S(2)}) %collective-permute-start.7) | collective-permute-done | bytes 163872 | tf_op jit(solution)/shard_map/ppermute | solution.py:635
  44.1 3.4 %sample_modes.1 = (bf16[8,256,128]{2,1,0:T(8,128)(2,1)S(1)}, f32[8,128]{1,0:T(8,128)S(1)}) custom-call(f32[320,128]{1,0:T(8,128)} %bitcast.10.refs_0_, f32[320,128]{1,0:T(8,128)S(1)} %collective-permute-done.7.refs_1_), custom_call_target="tpu_custom_call" | custom-call | flops 200000000 | bytes 1024 | tf_op jit(solution)/shard_map/sample_modes/pallas_call | solution.py:333
  48.7 1.9 %collective-permute-done.15.refs_3_.refs_10_ = bf16[1024,128]{1,0:T(8,128)(2,1)S(1)} collective-permute-done((bf16[1024,128]{1,0:T(8,128)(2,1)}, bf16[1024,128]{1,0:T(8,128)(2,1)S(1)}, u32[]{:S(2)}, u32[]{:S(2)}) %collective-permute-start.15) | collective-permute-done | bytes 262176 | tf_op jit(solution)/shard_map/ppermute | solution.py:632
  50.7 1.4 %collective-permute-start.17 = (bf16[1024,128]{1,0:T(8,128)(2,1)S(1)}, bf16[1024,128]{1,0:T(8,128)(2,1)S(1)}, u32[]{:S(2)}, u32[]{:S(2)}) collective-permute-start(bf16[1024,128]{1,0:T(8,128)(2,1)S(1)} %get-tuple-element.51.after_ref), channel_id=1, source_target_pairs={{0,8},{2,10},{8,16},{10,18},{16,24},{18,26},{24,28},{26,30},{28,20... | collective-permute-start | bytes 786440 | tf_op jit(solution)/shard_map/ppermute | solution.py:629
  52.8 3.5 %spread_modes.1.modes_ref = bf16[64,256,256]{2,1,0:T(8,128)(2,1)S(1)} custom-call(bf16[8,256,128]{2,1,0:T(8,128)(2,1)S(1)} %get-tuple-element.40.modes_ref, bf16[1024,128]{1,0:T(8,128)(2,1)S(1)} %get-tuple-element.51.after_ref), custom_call_target="tpu_custom_call" | custom-call | flops 200000000 | bytes 1024 | tf_op jit(solution)/shard_map/spread_modes/pallas_call | solution.py:373
  57.1 2.2 %grad_chunk.2 = (f32[4,2048,128]{2,1,0:T(8,128)}, f32[4,512,128]{2,1,0:T(8,128)S(1)}) custom-call(bf16[64,256,256]{2,1,0:T(8,128)(2,1)S(1)} %spread_modes.1.modes_ref, bf16[1024,128]{1,0:T(8,128)(2,1)S(1)} %get-tuple-element.31.refs_0_, bf16[1024,128]{1,0:T(8,128)(2,1)S(1)} %collective-permute-done.1.after_hbm.refs_1_, ...), custom_call_target="tpu_custom_call" | custom-call | flops 1000000000 | bytes 1024 | tf_op jit(solution)/shard_map/grad_chunk/pallas_call | solution.py:448
  59.4 2.2 %grad_chunk.3 = (f32[4,2048,128]{2,1,0:T(8,128)}, f32[4,512,128]{2,1,0:T(8,128)S(1)}) custom-call(bf16[64,256,256]{2,1,0:T(8,128)(2,1)S(1)} %spread_modes.1.modes_ref, bf16[1024,128]{1,0:T(8,128)(2,1)S(1)} %get-tuple-element.31.refs_0_, bf16[1024,128]{1,0:T(8,128)(2,1)S(1)} %collective-permute-done.1.after_hbm.refs_1_, ...), custom_call_target="tpu_custom_call", output_to_operand_aliasing={{0}: (16, {})} | custom-call | flops 1000000000 | bytes 1024 | tf_op jit(solution)/shard_map/grad_chunk/pallas_call | solution.py:448
  63.1 1.3 %collective-permute-done.18.part_ref = f32[4,512,128]{2,1,0:T(8,128)S(1)} collective-permute-done((f32[4,512,128]{2,1,0:T(8,128)S(1)}, f32[4,512,128]{2,1,0:T(8,128)S(1)}, u32[]{:S(2)}, u32[]{:S(2)}) %collective-permute-start.18) | collective-permute-done | bytes 1048608 | tf_op jit(solution)/shard_map/ppermute | solution.py:635
  (37 shorter events, 9.4 us)
Async XLA Ops:
  0.0 26.4 %copy-start.2 = (bf16[64,64]{1,0:T(8,128)(2,1)S(1)}, bf16[64,64]{1,0:T(8,128)(2,1)}, u32[]{:S(2)}) copy-start(bf16[64,64]{1,0:T(8,128)(2,1)} %refs_2_.1) | copy-start | bytes 24580
  1.3 3.2 %collective-permute-start.1 = (bf16[1024,128]{1,0:T(8,128)(2,1)S(1)}, bf16[1024,128]{1,0:T(8,128)(2,1)S(1)}, u32[]{:S(2)}, u32[]{:S(2)}) collective-permute-start(bf16[1024,128]{1,0:T(8,128)(2,1)S(1)} %get-tuple-element.32), channel_id=1, source_target_pairs={{0,2},{2,0},{4,6},{6,4},{8,10},{10,8},{12,14},{14,12},{16,18},{18,... | collective-permute-start | bytes 786440 | tf_op jit(solution)/shard_map/ppermute | solution.py:635
  1.8 11.9 %collective-permute-start.3 = (bf16[1024,128]{1,0:T(8,128)(2,1)S(1)}, bf16[1024,128]{1,0:T(8,128)(2,1)S(1)}, u32[]{:S(2)}, u32[]{:S(2)}) collective-permute-start(bf16[1024,128]{1,0:T(8,128)(2,1)S(1)} %get-tuple-element.31.refs_0_), channel_id=1, source_target_pairs={{0,4},{2,6},{8,0},{10,2},{16,8},{18,10},{24,16},{26,18},{28,24},{3... | collective-permute-start | bytes 786440 | tf_op jit(solution)/shard_map/ppermute | solution.py:632
  4.3 9.3 %collective-permute-start = (bf16[1024,128]{1,0:T(8,128)(2,1)S(1)}, bf16[1024,128]{1,0:T(8,128)(2,1)S(1)}, u32[]{:S(2)}, u32[]{:S(2)}) collective-permute-start(bf16[1024,128]{1,0:T(8,128)(2,1)S(1)} %get-tuple-element.31.refs_0_), channel_id=1, source_target_pairs={{0,8},{2,10},{8,16},{10,18},{16,24},{18,26},{24,28},{26,30},{28,20... | collective-permute-start | bytes 786440 | tf_op jit(solution)/shard_map/ppermute | solution.py:629
  4.5 12.4 %collective-permute-start.4 = (bf16[1024,128]{1,0:T(8,128)(2,1)S(1)}, bf16[1024,128]{1,0:T(8,128)(2,1)S(1)}, u32[]{:S(2)}, u32[]{:S(2)}) collective-permute-start(bf16[1024,128]{1,0:T(8,128)(2,1)S(1)} %collective-permute-done.1.after_hbm.refs_1_), channel_id=1, source_target_pairs={{0,4},{2,6},{8,0},{10,2},{16,8},{18,10},{24,16},{26,18},{28,24},{3... | collective-permute-start | bytes 786440 | tf_op jit(solution)/shard_map/ppermute | solution.py:632
  6.4 12.0 %collective-permute-start.2 = (bf16[1024,128]{1,0:T(8,128)(2,1)S(1)}, bf16[1024,128]{1,0:T(8,128)(2,1)S(1)}, u32[]{:S(2)}, u32[]{:S(2)}) collective-permute-start(bf16[1024,128]{1,0:T(8,128)(2,1)S(1)} %collective-permute-done.1.after_hbm.refs_1_), channel_id=1, source_target_pairs={{0,8},{2,10},{8,16},{10,18},{16,24},{18,26},{24,28},{26,30},{28,20... | collective-permute-start | bytes 786440 | tf_op jit(solution)/shard_map/ppermute | solution.py:629
  18.4 17.6 %copy-start = (bf16[1024,128]{1,0:T(8,128)(2,1)}, bf16[1024,128]{1,0:T(8,128)(2,1)S(1)}, u32[]{:S(2)}) copy-start(bf16[1024,128]{1,0:T(8,128)(2,1)S(1)} %get-tuple-element.44.refs_14_) | copy-start | bytes 786436
  18.4 6.3 %collective-permute-start.5 = (f32[264,128]{1,0:T(8,128)S(1)}, f32[264,128]{1,0:T(8,128)S(1)}, u32[]{:S(2)}, u32[]{:S(2)}) collective-permute-start(f32[264,128]{1,0:T(8,128)S(1)} %get-tuple-element.35.refs_0_), channel_id=1, source_target_pairs={{0,1},{1,0},{2,3},{3,2},{4,5},{5,4},{6,7},{7,6},{8,9},{9,8},{10,11... | collective-permute-start | bytes 405512 | tf_op jit(solution)/shard_map/ppermute | solution.py:656
  20.0 6.3 %collective-permute-start.6 = (f32[264,128]{1,0:T(8,128)S(1)}, f32[264,128]{1,0:T(8,128)S(1)}, u32[]{:S(2)}, u32[]{:S(2)}) collective-permute-start(f32[264,128]{1,0:T(8,128)S(1)} %get-tuple-element.36.refs_1_), channel_id=1, source_target_pairs={{0,1},{1,0},{2,3},{3,2},{4,5},{5,4},{6,7},{7,6},{8,9},{9,8},{10,11... | collective-permute-start | bytes 405512 | tf_op jit(solution)/shard_map/ppermute | solution.py:656
  20.5 13.2 %collective-permute-start.8 = (bf16[1024,128]{1,0:T(8,128)(2,1)S(1)}, bf16[1024,128]{1,0:T(8,128)(2,1)S(1)}, u32[]{:S(2)}, u32[]{:S(2)}) collective-permute-start(bf16[1024,128]{1,0:T(8,128)(2,1)S(1)} %get-tuple-element.41.refs_2_), channel_id=1, source_target_pairs={{0,8},{2,10},{8,16},{10,18},{16,24},{18,26},{24,28},{26,30},{28,20... | collective-permute-start | bytes 786440 | tf_op jit(solution)/shard_map/ppermute | solution.py:629
  20.9 12.8 %collective-permute-start.9 = (bf16[1024,128]{1,0:T(8,128)(2,1)S(1)}, bf16[1024,128]{1,0:T(8,128)(2,1)S(1)}, u32[]{:S(2)}, u32[]{:S(2)}) collective-permute-start(bf16[1024,128]{1,0:T(8,128)(2,1)S(1)} %get-tuple-element.42.refs_3_), channel_id=1, source_target_pairs={{0,8},{2,10},{8,16},{10,18},{16,24},{18,26},{24,28},{26,30},{28,20... | collective-permute-start | bytes 786440 | tf_op jit(solution)/shard_map/ppermute | solution.py:629
  22.6 11.1 %collective-permute-start.10 = (bf16[1024,128]{1,0:T(8,128)(2,1)S(1)}, bf16[1024,128]{1,0:T(8,128)(2,1)S(1)}, u32[]{:S(2)}, u32[]{:S(2)}) collective-permute-start(bf16[1024,128]{1,0:T(8,128)(2,1)S(1)} %get-tuple-element.43.refs_13_), channel_id=1, source_target_pairs={{0,4},{2,6},{8,0},{10,2},{16,8},{18,10},{24,16},{26,18},{28,24},{3... | collective-permute-start | bytes 786440 | tf_op jit(solution)/shard_map/ppermute | solution.py:632
  24.8 10.2 %collective-permute-start.11 = (bf16[1024,128]{1,0:T(8,128)(2,1)S(1)}, bf16[1024,128]{1,0:T(8,128)(2,1)S(1)}, u32[]{:S(2)}, u32[]{:S(2)}) collective-permute-start(bf16[1024,128]{1,0:T(8,128)(2,1)S(1)} %get-tuple-element.44.refs_14_), channel_id=1, source_target_pairs={{0,4},{2,6},{8,0},{10,2},{16,8},{18,10},{24,16},{26,18},{28,24},{3... | collective-permute-start | bytes 786440 | tf_op jit(solution)/shard_map/ppermute | solution.py:632
  28.9 13.6 %all-to-all-start = ((f32[8,40,128]{2,1,0:T(8,128)}), f32[8,40,128]{2,1,0:T(8,128)}, u32[]{:S(2)}, u32[]{:S(2)}) async-start(f32[8,40,128]{2,1,0:T(8,128)} %bitcast.9), calls=%async_computation | async-start | bytes 327680 | tf_op jit(solution)/shard_map/all_to_all | solution.py:661
  36.0 11.6 %collective-permute-start.12 = (bf16[1024,128]{1,0:T(8,128)(2,1)}, bf16[1024,128]{1,0:T(8,128)(2,1)S(1)}, u32[]{:S(2)}, u32[]{:S(2)}) collective-permute-start(bf16[1024,128]{1,0:T(8,128)(2,1)} %get-tuple-element.46), channel_id=1, source_target_pairs={{0,8},{2,10},{8,16},{10,18},{16,24},{18,26},{24,28},{26,30},{28,20... | collective-permute-start | bytes 786440 | tf_op jit(solution)/shard_map/ppermute | solution.py:629
  37.6 11.1 %collective-permute-start.13 = (bf16[1024,128]{1,0:T(8,128)(2,1)}, bf16[1024,128]{1,0:T(8,128)(2,1)S(1)}, u32[]{:S(2)}, u32[]{:S(2)}) collective-permute-start(bf16[1024,128]{1,0:T(8,128)(2,1)} %get-tuple-element.47), channel_id=1, source_target_pairs={{0,8},{2,10},{8,16},{10,18},{16,24},{18,26},{24,28},{26,30},{28,20... | collective-permute-start | bytes 786440 | tf_op jit(solution)/shard_map/ppermute | solution.py:629
  39.1 9.6 %collective-permute-start.14 = (bf16[1024,128]{1,0:T(8,128)(2,1)}, bf16[1024,128]{1,0:T(8,128)(2,1)S(1)}, u32[]{:S(2)}, u32[]{:S(2)}) collective-permute-start(bf16[1024,128]{1,0:T(8,128)(2,1)} %get-tuple-element.48), channel_id=1, source_target_pairs={{0,4},{2,6},{8,0},{10,2},{16,8},{18,10},{24,16},{26,18},{28,24},{3... | collective-permute-start | bytes 786440 | tf_op jit(solution)/shard_map/ppermute | solution.py:632
  39.6 11.0 %collective-permute-start.15 = (bf16[1024,128]{1,0:T(8,128)(2,1)}, bf16[1024,128]{1,0:T(8,128)(2,1)S(1)}, u32[]{:S(2)}, u32[]{:S(2)}) collective-permute-start(bf16[1024,128]{1,0:T(8,128)(2,1)} %get-tuple-element.49), channel_id=1, source_target_pairs={{0,4},{2,6},{8,0},{10,2},{16,8},{18,10},{24,16},{26,18},{28,24},{3... | collective-permute-start | bytes 786440 | tf_op jit(solution)/shard_map/ppermute | solution.py:632
  42.5 1.6 %collective-permute-start.7 = (f32[320,128]{1,0:T(8,128)}, f32[320,128]{1,0:T(8,128)S(1)}, u32[]{:S(2)}, u32[]{:S(2)}) collective-permute-start(f32[320,128]{1,0:T(8,128)} %bitcast.10.refs_0_), channel_id=1, source_target_pairs={{0,2},{2,0},{4,6},{6,4},{8,10},{10,8},{12,14},{14,12},{16,18},{18,... | collective-permute-start | bytes 491528 | tf_op jit(solution)/shard_map/ppermute | solution.py:635
  50.7 6.4 %collective-permute-start.17 = (bf16[1024,128]{1,0:T(8,128)(2,1)S(1)}, bf16[1024,128]{1,0:T(8,128)(2,1)S(1)}, u32[]{:S(2)}, u32[]{:S(2)}) collective-permute-start(bf16[1024,128]{1,0:T(8,128)(2,1)S(1)} %get-tuple-element.51.after_ref), channel_id=1, source_target_pairs={{0,8},{2,10},{8,16},{10,18},{16,24},{18,26},{24,28},{26,30},{28,20... | collective-permute-start | bytes 786440 | tf_op jit(solution)/shard_map/ppermute | solution.py:629
  52.1 7.3 %collective-permute-start.16 = (bf16[1024,128]{1,0:T(8,128)(2,1)S(1)}, bf16[1024,128]{1,0:T(8,128)(2,1)S(1)}, u32[]{:S(2)}, u32[]{:S(2)}) collective-permute-start(bf16[1024,128]{1,0:T(8,128)(2,1)S(1)} %get-tuple-element.52), channel_id=1, source_target_pairs={{0,4},{2,6},{8,0},{10,2},{16,8},{18,10},{24,16},{26,18},{28,24},{3... | collective-permute-start | bytes 786440 | tf_op jit(solution)/shard_map/ppermute | solution.py:632
  52.8 4.3 %copy-start.1 = (bf16[1024,128]{1,0:T(8,128)(2,1)S(1)}, bf16[1024,128]{1,0:T(8,128)(2,1)}, u32[]{:S(2)}) copy-start(bf16[1024,128]{1,0:T(8,128)(2,1)} %copy-done) | copy-start | bytes 786436
  59.3 2.8 %collective-permute-start.19 = (f32[4,512,128]{2,1,0:T(8,128)S(1)}, f32[4,512,128]{2,1,0:T(8,128)S(1)}, u32[]{:S(2)}, u32[]{:S(2)}) collective-permute-start(f32[4,512,128]{2,1,0:T(8,128)S(1)} %get-tuple-element.55), channel_id=1, source_target_pairs={{0,2},{2,0},{4,6},{6,4},{8,10},{10,8},{12,14},{14,12},{16,18},{18,... | collective-permute-start | bytes 3145736 | tf_op jit(solution)/shard_map/ppermute | solution.py:635
  61.5 2.8 %collective-permute-start.18 = (f32[4,512,128]{2,1,0:T(8,128)S(1)}, f32[4,512,128]{2,1,0:T(8,128)S(1)}, u32[]{:S(2)}, u32[]{:S(2)}) collective-permute-start(f32[4,512,128]{2,1,0:T(8,128)S(1)} %get-tuple-element.54), channel_id=1, source_target_pairs={{0,2},{2,0},{4,6},{6,4},{8,10},{10,8},{12,14},{14,12},{16,18},{18,... | collective-permute-start | bytes 3145736 | tf_op jit(solution)/shard_map/ppermute | solution.py:635

commit v4 on v3

--- a/solution.py
+++ b/solution.py
@@ -251,7 +251,7 @@
             pltpu.VMEM((kept * GZ, lanes), jnp.float32),
         ],
         compiler_params=pltpu.CompilerParams(
-            vmem_limit_bytes=(8 if slabs <= 2 else 48) * MIB
+            vmem_limit_bytes=(6 if slabs <= 2 else 48) * MIB
         ),
         cost_estimate=work(0.1),
         name="lift_slots",
@@ -339,7 +339,7 @@
         in_specs=[vmem] * len(recv),
         out_specs=[vmem] * 2,
         scratch_shapes=[pltpu.VMEM((lanes // GZ, total * samples, GZ), jnp.float32)],
-        compiler_params=pltpu.CompilerParams(vmem_limit_bytes=(8 if slabs <= 2 else 32) * MIB),
+        compiler_params=pltpu.CompilerParams(vmem_limit_bytes=(5 if slabs <= 2 else 32) * MIB),
         cost_estimate=work(0.2),
         name="sample_modes",
     )(*recv)
@@ -383,7 +383,7 @@
             pltpu.VMEM((columns, group * span), jnp.bfloat16),
             pltpu.VMEM((lanes, span), jnp.float32),
         ],
-        compiler_params=pltpu.CompilerParams(vmem_limit_bytes=8 * MIB),
+        compiler_params=pltpu.CompilerParams(vmem_limit_bytes=5 * MIB),
         cost_estimate=work(0.2),
         name="spread_modes",
     )(modes, after)
@@ -495,7 +495,7 @@
         out_specs=hbm,
         scratch_shapes=[pltpu.SemaphoreType.DMA((part.shape[0],))],
         input_output_aliases={1: 0},
-        compiler_params=pltpu.CompilerParams(vmem_limit_bytes=8 * MIB),
+        compiler_params=pltpu.CompilerParams(vmem_limit_bytes=2 * MIB),
         cost_estimate=work(0.2),
         name="place_chunk",
     )(part, result)
@@ -597,7 +597,7 @@
         ],
         in_specs=[vmem] * len(operands),
         out_specs=[vmem] * len(spans),
-        compiler_params=pltpu.CompilerParams(vmem_limit_bytes=4 * MIB),
+        compiler_params=pltpu.CompilerParams(vmem_limit_bytes=2 * MIB),
         cost_estimate=work(0.01),
         name="joint",
     )(*operands)
@@ -647,12 +647,12 @@
         twin,
     )
     pair = {}
-    *outs, first, second = joint([*ups, *downs, *sent])
-    pair[1], pair[chips - 1], sent = outs[:2], outs[2:], [first, second]
+    outs = joint([*ups, *downs], sent[0])
+    pair[1], pair[chips - 1] = outs[:2], outs[2:]
 
     pair[2] = [up(rows) for rows in pair[1]]
     pair[chips - 2] = [down(rows) for rows in pair[chips - 1]]
-    terms = [sent] + [
+    terms = [list(sent)] + [
         [lax.ppermute(x, "slab", [(t, (t + s) % slabs) for t in range(slabs)]) for x in sent]
         for s in range(1, slabs)
     ]
@@ -662,8 +662,8 @@
         payload.reshape(chips, -1, GZ), "dp", split_axis=0, concat_axis=0, tiled=True,
         axis_index_groups=[list(range(c, devices, 2)) for c in range(2)],
     ).reshape(payload.shape)
-    outs = joint([*pair[2], *pair[chips - 2]], lift_done)
-    sent_on = {2: outs[:2], chips - 2: outs[2:]}
+    outs = joint([pair[2][0], pair[chips - 2][0]], lift_done)
+    sent_on = {2: [outs[0], pair[2][1]], chips - 2: [outs[1], pair[chips - 2][1]]}
 
     for s in range(3, far):
         pair[s] = [up(rows) for rows in sent_on.get(s - 1, pair[s - 1])]
@@ -682,6 +682,8 @@
         ],
         modes_done,
     )
+
+    pair[2][1], pair[chips - 2][1] = joint([pair[2][1], pair[chips - 2][1]], modes_done)
 
     ends = [up(first), down(second)]
     modes = spread_modes(modes, group, mode_count, first)

time: 65.6 us -> 62 us (0.945)
  waiting for transfers between devices: 17 us -> 10.8 us
  starting transfers between devices: 22.9 us -> 24.7 us
  Pallas kernels: 25.3 us -> 26.1 us
    ppermute x7, waiting for transfers between devices: 6.41 us -> 3.27 us  [down(): return lax.ppermute(rows, 'dp', ring_perm(chips, -1))]
    ppermute x7, starting transfers between devices: 7.84 us -> 9.71 us  [down(): return lax.ppermute(rows, 'dp', ring_perm(chips, -1))]
    ppermute x2, waiting for transfers between devices: 1.85 us -> 0.01 us  [per_device(): lax.ppermute(x, 'slab', [(t, (t + s) % slabs) for t in range(slabs)])]
    ppermute x7, waiting for transfers between devices: 3.33 us -> 2.05 us  [up(): return lax.ppermute(rows, 'dp', ring_perm(chips, 1))]
    pallas_call x4 -> x5, Pallas kernels: 1.19 us -> 1.95 us  [joint(): pl.pallas_call(functools.partial(joint_kernel, spans, len(operands)), out...]
  transfers between devices with their start and end apart: 21 -> 21, of which waited for: 10 -> 7; matrix products, arithmetic and copies ran while one was open for 0% -> 0% of each run, Pallas kernels for 35% -> 39%
where the time goes in v4:
time: 62 us; the launch traced here: 61.7 us
  Pallas kernels  26.1 us (42%)
  starting transfers between devices  24.7 us (40%)
  waiting for transfers between devices  10.8 us (17%)
    ppermute x7, starting transfers between devices, down(): return lax.ppermute(rows, 'dp', ring_perm(chips, -1))  9.71 us
    pallas_call x1, Pallas kernels, slot_terms(): pl.pallas_call(functools.partial(slot_kernel, slabs, planes), out_shape=[...  7.09 us
    ppermute x7, starting transfers between devices, up(): return lax.ppermute(rows, 'dp', ring_perm(chips, 1))  6.67 us
    all_to_all x1, starting transfers between devices, per_device(): lax.all_to_all(payload.reshape(chips, -1, GZ), 'dp', split_axis=0, concat...  5.07 us
    pallas_call x2, Pallas kernels, grad_chunk(): pl.pallas_call(functools.partial(grad_kernel, chunk, chunks, depth, first...  4.32 us
    pallas_call x1, Pallas kernels, spread_modes(): pl.pallas_call(functools.partial(spread_kernel, depth), out_shape=jax.Sha...  3.55 us
    pallas_call x1, Pallas kernels, sample_modes(): pl.pallas_call(functools.partial(modes_kernel, chips, slabs, slots, plane...  3.43 us
    ppermute x7, waiting for transfers between devices, down(): return lax.ppermute(rows, 'dp', ring_perm(chips, -1))  3.27 us
  transfers between devices with their start and end apart: 21, of which 7 were waited for; matrix products, arithmetic and copies ran while one was open for 0% of the time, Pallas kernels for 39%

profile of v4, /device:TPU:0, one launch (start us, length us, event | category | flops | bytes accessed | tf_op | source)
XLA Modules:
  0.0 61.7 jit_solution(13592060642736546197)
XLA Ops:
  0.0 1.2 %cast_rows.1 = (bf16[1024,128]{1,0:T(8,128)(2,1)S(1)}, bf16[1024,128]{1,0:T(8,128)(2,1)S(1)}) custom-call(f32[2048,128]{1,0:T(8,128)} %bitcast.13), custom_call_target="tpu_custom_call" | custom-call | flops 100000000 | bytes 1024 | tf_op jit(solution)/shard_map/cast_rows/pallas_call | solution.py:529
  1.8 2.6 %collective-permute-start.6 = (bf16[1024,128]{1,0:T(8,128)(2,1)S(1)}, bf16[1024,128]{1,0:T(8,128)(2,1)S(1)}, u32[]{:S(2)}, u32[]{:S(2)}) collective-permute-start(bf16[1024,128]{1,0:T(8,128)(2,1)S(1)} %get-tuple-element.36.refs_0_), channel_id=1, source_target_pairs={{0,4},{2,6},{8,0},{10,2},{16,8},{18,10},{24,16},{26,18},{28,24},{3... | collective-permute-start | bytes 786440 | tf_op jit(solution)/shard_map/ppermute | solution.py:632
  4.5 1.9 %collective-permute-start.7 = (bf16[1024,128]{1,0:T(8,128)(2,1)S(1)}, bf16[1024,128]{1,0:T(8,128)(2,1)S(1)}, u32[]{:S(2)}, u32[]{:S(2)}) collective-permute-start(bf16[1024,128]{1,0:T(8,128)(2,1)S(1)} %collective-permute-done.after_hbm.refs_1_), channel_id=1, source_target_pairs={{0,4},{2,6},{8,0},{10,2},{16,8},{18,10},{24,16},{26,18},{28,24},{3... | collective-permute-start | bytes 786440 | tf_op jit(solution)/shard_map/ppermute | solution.py:632
  6.5 7.1 %slot_terms.1 = (f32[264,128]{1,0:T(8,128)S(1)}, f32[264,128]{1,0:T(8,128)S(1)}) custom-call(s32[2,4]{1,0:T(2,128)} %bitcast.17, s32[2,4]{1,0:T(2,128)} %bitcast.18, s32[2]{0:T(128)} %bitcast.19, bf16[4,64,128]{2,1,0:T(8,128)(2,1)} %bitcast.14, bf16[3,4,128]{2,1,0:T(4,128)(2,1)} %bitcast.15, f32[3,64]{1,0:T(4,128)} %bitcast.16, f32[1,64]{1,0:T(1,128)} %bitcast.20, ...), custom_call_target="tpu_custom_call" | custom-call | flops 1000000000 | bytes 1024 | tf_op jit(solution)/shard_map/slot_terms/pallas_call | solution.py:135
  13.6 2.0 %collective-permute-start.2 = (f32[264,128]{1,0:T(8,128)S(1)}, f32[264,128]{1,0:T(8,128)S(1)}, u32[]{:S(2)}, u32[]{:S(2)}) collective-permute-start(f32[264,128]{1,0:T(8,128)S(1)} %get-tuple-element.31.refs_1_), channel_id=1, source_target_pairs={{0,1},{1,0},{2,3},{3,2},{4,5},{5,4},{6,7},{7,6},{8,9},{9,8},{10,11... | collective-permute-start | bytes 405512 | tf_op jit(solution)/shard_map/ppermute | solution.py:656
  15.7 1.2 %collective-permute-done.7.refs_3_ = bf16[1024,128]{1,0:T(8,128)(2,1)S(1)} collective-permute-done((bf16[1024,128]{1,0:T(8,128)(2,1)S(1)}, bf16[1024,128]{1,0:T(8,128)(2,1)S(1)}, u32[]{:S(2)}, u32[]{:S(2)}) %collective-permute-start.7) | collective-permute-done | bytes 262176 | tf_op jit(solution)/shard_map/ppermute | solution.py:632
  16.9 1.4 %collective-permute-done.5.refs_1_ = bf16[1024,128]{1,0:T(8,128)(2,1)S(1)} collective-permute-done((bf16[1024,128]{1,0:T(8,128)(2,1)S(1)}, bf16[1024,128]{1,0:T(8,128)(2,1)S(1)}, u32[]{:S(2)}, u32[]{:S(2)}) %collective-permute-start.5) | collective-permute-done | bytes 262176 | tf_op jit(solution)/shard_map/ppermute | solution.py:629
  18.8 1.7 %collective-permute-start.9 = (bf16[1024,128]{1,0:T(8,128)(2,1)S(1)}, bf16[1024,128]{1,0:T(8,128)(2,1)S(1)}, u32[]{:S(2)}, u32[]{:S(2)}) collective-permute-start(bf16[1024,128]{1,0:T(8,128)(2,1)S(1)} %get-tuple-element.38.refs_13_), channel_id=1, source_target_pairs={{0,4},{2,6},{8,0},{10,2},{16,8},{18,10},{24,16},{26,18},{28,24},{3... | collective-permute-start | bytes 786440 | tf_op jit(solution)/shard_map/ppermute | solution.py:632
  20.8 1.7 %collective-permute-start.14 = (bf16[1024,128]{1,0:T(8,128)(2,1)S(1)}, bf16[1024,128]{1,0:T(8,128)(2,1)}, u32[]{:S(2)}, u32[]{:S(2)}) collective-permute-start(bf16[1024,128]{1,0:T(8,128)(2,1)S(1)} %get-tuple-element.43.refs_14_), channel_id=1, source_target_pairs={{0,4},{2,6},{8,0},{10,2},{16,8},{18,10},{24,16},{26,18},{28,24},{3... | collective-permute-start | bytes 786440 | tf_op jit(solution)/shard_map/ppermute | solution.py:632
  22.6 2.5 %lift_slots.1 = (f32[320,128]{1,0:T(8,128)}, f32[8,128]{1,0:T(8,128)S(1)}) custom-call(f32[528,128]{1,0:T(8,128)S(1)} %get-tuple-element.32.refs_0_, f32[528,128]{1,0:T(8,128)S(1)} %get-tuple-element.33.refs_1_, bf16[64,64]{1,0:T(8,128)(2,1)S(1)} %copy-done), custom_call_target="tpu_custom_call" | custom-call | flops 100000000 | bytes 1024 | tf_op jit(solution)/shard_map/lift_slots/pallas_call | solution.py:239
  25.1 5.1 %all-to-all-start = ((f32[8,40,128]{2,1,0:T(8,128)}), f32[8,40,128]{2,1,0:T(8,128)}, u32[]{:S(2)}, u32[]{:S(2)}) async-start(f32[8,40,128]{2,1,0:T(8,128)} %bitcast.9), calls=%async_computation | async-start | bytes 327680 | tf_op jit(solution)/shard_map/all_to_all | solution.py:661
  31.0 2.0 %collective-permute-start.10 = (bf16[1024,128]{1,0:T(8,128)(2,1)}, bf16[1024,128]{1,0:T(8,128)(2,1)S(1)}, u32[]{:S(2)}, u32[]{:S(2)}) collective-permute-start(bf16[1024,128]{1,0:T(8,128)(2,1)} %get-tuple-element.40), channel_id=1, source_target_pairs={{0,8},{2,10},{8,16},{10,18},{16,24},{18,26},{24,28},{26,30},{28,20... | collective-permute-start | bytes 786440 | tf_op jit(solution)/shard_map/ppermute | solution.py:629
  33.0 1.5 %collective-permute-start.12 = (bf16[1024,128]{1,0:T(8,128)(2,1)S(1)}, bf16[1024,128]{1,0:T(8,128)(2,1)S(1)}, u32[]{:S(2)}, u32[]{:S(2)}) collective-permute-start(bf16[1024,128]{1,0:T(8,128)(2,1)S(1)} %collective-permute-done.11.refs_0_), channel_id=1, source_target_pairs={{0,8},{2,10},{8,16},{10,18},{16,24},{18,26},{24,28},{26,30},{28,20... | collective-permute-start | bytes 786440 | tf_op jit(solution)/shard_map/ppermute | solution.py:629
  35.0 1.4 %collective-permute-start.13 = (bf16[1024,128]{1,0:T(8,128)(2,1)}, bf16[1024,128]{1,0:T(8,128)(2,1)S(1)}, u32[]{:S(2)}, u32[]{:S(2)}) collective-permute-start(bf16[1024,128]{1,0:T(8,128)(2,1)} %get-tuple-element.42), channel_id=1, source_target_pairs={{0,4},{2,6},{8,0},{10,2},{16,8},{18,10},{24,16},{26,18},{28,24},{3... | collective-permute-start | bytes 786440 | tf_op jit(solution)/shard_map/ppermute | solution.py:632
  36.5 2.5 %all-to-all-done = f32[8,40,128]{2,1,0:T(8,128)} async-done(((f32[8,40,128]{2,1,0:T(8,128)}), f32[8,40,128]{2,1,0:T(8,128)}, u32[]{:S(2)}, u32[]{:S(2)}) %all-to-all-start) | async-done | bytes 163872 | tf_op jit(solution)/shard_map/all_to_all | solution.py:661
  39.0 1.6 %collective-permute-done.3.refs_1_ = f32[320,128]{1,0:T(8,128)S(1)} collective-permute-done((f32[320,128]{1,0:T(8,128)}, f32[320,128]{1,0:T(8,128)S(1)}, u32[]{:S(2)}, u32[]{:S(2)}) %collective-permute-start.3) | collective-permute-done | bytes 163872 | tf_op jit(solution)/shard_map/ppermute | solution.py:635
  40.6 3.4 %sample_modes.1 = (bf16[8,256,128]{2,1,0:T(8,128)(2,1)S(1)}, f32[8,128]{1,0:T(8,128)S(1)}) custom-call(f32[320,128]{1,0:T(8,128)} %bitcast.10.refs_0_, f32[320,128]{1,0:T(8,128)S(1)} %collective-permute-done.3.refs_1_), custom_call_target="tpu_custom_call" | custom-call | flops 200000000 | bytes 1024 | tf_op jit(solution)/shard_map/sample_modes/pallas_call | solution.py:333
  44.7 2.0 %collective-permute-done.13.refs_2_.refs_9_ = bf16[1024,128]{1,0:T(8,128)(2,1)S(1)} collective-permute-done((bf16[1024,128]{1,0:T(8,128)(2,1)}, bf16[1024,128]{1,0:T(8,128)(2,1)S(1)}, u32[]{:S(2)}, u32[]{:S(2)}) %collective-permute-start.13) | collective-permute-done | bytes 262176 | tf_op jit(solution)/shard_map/ppermute | solution.py:632
  46.8 2.1 %collective-permute-start.17 = (bf16[1024,128]{1,0:T(8,128)(2,1)S(1)}, bf16[1024,128]{1,0:T(8,128)(2,1)S(1)}, u32[]{:S(2)}, u32[]{:S(2)}) collective-permute-start(bf16[1024,128]{1,0:T(8,128)(2,1)S(1)} %get-tuple-element.45.after_ref), channel_id=1, source_target_pairs={{0,8},{2,10},{8,16},{10,18},{16,24},{18,26},{24,28},{26,30},{28,20... | collective-permute-start | bytes 786440 | tf_op jit(solution)/shard_map/ppermute | solution.py:629
  49.9 3.5 %spread_modes.1.modes_ref = bf16[64,256,256]{2,1,0:T(8,128)(2,1)S(1)} custom-call(bf16[8,256,128]{2,1,0:T(8,128)(2,1)S(1)} %get-tuple-element.35.modes_ref, bf16[1024,128]{1,0:T(8,128)(2,1)S(1)} %get-tuple-element.45.after_ref), custom_call_target="tpu_custom_call" | custom-call | flops 200000000 | bytes 1024 | tf_op jit(solution)/shard_map/spread_modes/pallas_call | solution.py:373
  53.4 2.2 %grad_chunk.2 = (f32[4,2048,128]{2,1,0:T(8,128)}, f32[4,512,128]{2,1,0:T(8,128)S(1)}) custom-call(bf16[64,256,256]{2,1,0:T(8,128)(2,1)S(1)} %spread_modes.1.modes_ref, bf16[1024,128]{1,0:T(8,128)(2,1)S(1)} %get-tuple-element.36.refs_0_, bf16[1024,128]{1,0:T(8,128)(2,1)S(1)} %collective-permute-done.after_hbm.refs_1_, ...), custom_call_target="tpu_custom_call" | custom-call | flops 1000000000 | bytes 1024 | tf_op jit(solution)/shard_map/grad_chunk/pallas_call | solution.py:448
  55.7 2.2 %grad_chunk.3 = (f32[4,2048,128]{2,1,0:T(8,128)}, f32[4,512,128]{2,1,0:T(8,128)S(1)}) custom-call(bf16[64,256,256]{2,1,0:T(8,128)(2,1)S(1)} %spread_modes.1.modes_ref, bf16[1024,128]{1,0:T(8,128)(2,1)S(1)} %get-tuple-element.36.refs_0_, bf16[1024,128]{1,0:T(8,128)(2,1)S(1)} %collective-permute-done.after_hbm.refs_1_, ...), custom_call_target="tpu_custom_call", output_to_operand_aliasing={{0}: (16, {})} | custom-call | flops 1000000000 | bytes 1024 | tf_op jit(solution)/shard_map/grad_chunk/pallas_call | solution.py:448
  58.4 1.0 %place_chunk.2.old_hbm = f32[4,2048,128]{2,1,0:T(8,128)} custom-call(f32[4,512,128]{2,1,0:T(8,128)S(1)} %collective-permute-done.19.part_ref, f32[4,2048,128]{2,1,0:T(8,128)} %get-tuple-element.52.old_hbm), custom_call_target="tpu_custom_call", output_to_operand_aliasing={{}: (1, {})} | custom-call | flops 200000000 | bytes 1024 | tf_op jit(solution)/shard_map/place_chunk/pallas_call | solution.py:491
  59.4 1.3 %collective-permute-done.18.part_ref = f32[4,512,128]{2,1,0:T(8,128)S(1)} collective-permute-done((f32[4,512,128]{2,1,0:T(8,128)S(1)}, f32[4,512,128]{2,1,0:T(8,128)S(1)}, u32[]{:S(2)}, u32[]{:S(2)}) %collective-permute-start.18) | collective-permute-done | bytes 1048608 | tf_op jit(solution)/shard_map/ppermute | solution.py:635
  (34 shorter events, 6.6 us)
Async XLA Ops:
  0.0 22.5 %copy-start = (bf16[64,64]{1,0:T(8,128)(2,1)S(1)}, bf16[64,64]{1,0:T(8,128)(2,1)}, u32[]{:S(2)}) copy-start(bf16[64,64]{1,0:T(8,128)(2,1)} %refs_2_.1) | copy-start | bytes 24580
  1.3 3.2 %collective-permute-start = (bf16[1024,128]{1,0:T(8,128)(2,1)S(1)}, bf16[1024,128]{1,0:T(8,128)(2,1)S(1)}, u32[]{:S(2)}, u32[]{:S(2)}) collective-permute-start(bf16[1024,128]{1,0:T(8,128)(2,1)S(1)} %get-tuple-element.29), channel_id=1, source_target_pairs={{0,2},{2,0},{4,6},{6,4},{8,10},{10,8},{12,14},{14,12},{16,18},{18,... | collective-permute-start | bytes 786440 | tf_op jit(solution)/shard_map/ppermute | solution.py:635
  1.8 13.8 %collective-permute-start.6 = (bf16[1024,128]{1,0:T(8,128)(2,1)S(1)}, bf16[1024,128]{1,0:T(8,128)(2,1)S(1)}, u32[]{:S(2)}, u32[]{:S(2)}) collective-permute-start(bf16[1024,128]{1,0:T(8,128)(2,1)S(1)} %get-tuple-element.36.refs_0_), channel_id=1, source_target_pairs={{0,4},{2,6},{8,0},{10,2},{16,8},{18,10},{24,16},{26,18},{28,24},{3... | collective-permute-start | bytes 786440 | tf_op jit(solution)/shard_map/ppermute | solution.py:632
  4.3 11.4 %collective-permute-start.4 = (bf16[1024,128]{1,0:T(8,128)(2,1)S(1)}, bf16[1024,128]{1,0:T(8,128)(2,1)S(1)}, u32[]{:S(2)}, u32[]{:S(2)}) collective-permute-start(bf16[1024,128]{1,0:T(8,128)(2,1)S(1)} %get-tuple-element.36.refs_0_), channel_id=1, source_target_pairs={{0,8},{2,10},{8,16},{10,18},{16,24},{18,26},{24,28},{26,30},{28,20... | collective-permute-start | bytes 786440 | tf_op jit(solution)/shard_map/ppermute | solution.py:629
  4.5 12.4 %collective-permute-start.7 = (bf16[1024,128]{1,0:T(8,128)(2,1)S(1)}, bf16[1024,128]{1,0:T(8,128)(2,1)S(1)}, u32[]{:S(2)}, u32[]{:S(2)}) collective-permute-start(bf16[1024,128]{1,0:T(8,128)(2,1)S(1)} %collective-permute-done.after_hbm.refs_1_), channel_id=1, source_target_pairs={{0,4},{2,6},{8,0},{10,2},{16,8},{18,10},{24,16},{26,18},{28,24},{3... | collective-permute-start | bytes 786440 | tf_op jit(solution)/shard_map/ppermute | solution.py:632
  6.4 12.0 %collective-permute-start.5 = (bf16[1024,128]{1,0:T(8,128)(2,1)S(1)}, bf16[1024,128]{1,0:T(8,128)(2,1)S(1)}, u32[]{:S(2)}, u32[]{:S(2)}) collective-permute-start(bf16[1024,128]{1,0:T(8,128)(2,1)S(1)} %collective-permute-done.after_hbm.refs_1_), channel_id=1, source_target_pairs={{0,8},{2,10},{8,16},{10,18},{16,24},{18,26},{24,28},{26,30},{28,20... | collective-permute-start | bytes 786440 | tf_op jit(solution)/shard_map/ppermute | solution.py:629
  13.6 7.2 %collective-permute-start.2 = (f32[264,128]{1,0:T(8,128)S(1)}, f32[264,128]{1,0:T(8,128)S(1)}, u32[]{:S(2)}, u32[]{:S(2)}) collective-permute-start(f32[264,128]{1,0:T(8,128)S(1)} %get-tuple-element.31.refs_1_), channel_id=1, source_target_pairs={{0,1},{1,0},{2,3},{3,2},{4,5},{5,4},{6,7},{7,6},{8,9},{9,8},{10,11... | collective-permute-start | bytes 405512 | tf_op jit(solution)/shard_map/ppermute | solution.py:656
  15.6 6.9 %collective-permute-start.1 = (f32[264,128]{1,0:T(8,128)S(1)}, f32[264,128]{1,0:T(8,128)S(1)}, u32[]{:S(2)}, u32[]{:S(2)}) collective-permute-start(f32[264,128]{1,0:T(8,128)S(1)} %get-tuple-element.30.refs_0_.refs_4_), channel_id=1, source_target_pairs={{0,1},{1,0},{2,3},{3,2},{4,5},{5,4},{6,7},{7,6},{8,9},{9,8},{10,11... | collective-permute-start | bytes 405512 | tf_op jit(solution)/shard_map/ppermute | solution.py:656
  18.4 11.8 %collective-permute-start.8 = (bf16[1024,128]{1,0:T(8,128)(2,1)S(1)}, bf16[1024,128]{1,0:T(8,128)(2,1)S(1)}, u32[]{:S(2)}, u32[]{:S(2)}) collective-permute-start(bf16[1024,128]{1,0:T(8,128)(2,1)S(1)} %get-tuple-element.37.refs_2_), channel_id=1, source_target_pairs={{0,8},{2,10},{8,16},{10,18},{16,24},{18,26},{24,28},{26,30},{28,20... | collective-permute-start | bytes 786440 | tf_op jit(solution)/shard_map/ppermute | solution.py:629
  18.8 11.4 %collective-permute-start.9 = (bf16[1024,128]{1,0:T(8,128)(2,1)S(1)}, bf16[1024,128]{1,0:T(8,128)(2,1)S(1)}, u32[]{:S(2)}, u32[]{:S(2)}) collective-permute-start(bf16[1024,128]{1,0:T(8,128)(2,1)S(1)} %get-tuple-element.38.refs_13_), channel_id=1, source_target_pairs={{0,4},{2,6},{8,0},{10,2},{16,8},{18,10},{24,16},{26,18},{28,24},{3... | collective-permute-start | bytes 786440 | tf_op jit(solution)/shard_map/ppermute | solution.py:632
  20.5 12.5 %collective-permute-start.11 = (bf16[1024,128]{1,0:T(8,128)(2,1)S(1)}, bf16[1024,128]{1,0:T(8,128)(2,1)S(1)}, u32[]{:S(2)}, u32[]{:S(2)}) collective-permute-start(bf16[1024,128]{1,0:T(8,128)(2,1)S(1)} %get-tuple-element.41.refs_3_), channel_id=1, source_target_pairs={{0,8},{2,10},{8,16},{10,18},{16,24},{18,26},{24,28},{26,30},{28,20... | collective-permute-start | bytes 786440 | tf_op jit(solution)/shard_map/ppermute | solution.py:629
  20.8 13.6 %collective-permute-start.14 = (bf16[1024,128]{1,0:T(8,128)(2,1)S(1)}, bf16[1024,128]{1,0:T(8,128)(2,1)}, u32[]{:S(2)}, u32[]{:S(2)}) collective-permute-start(bf16[1024,128]{1,0:T(8,128)(2,1)S(1)} %get-tuple-element.43.refs_14_), channel_id=1, source_target_pairs={{0,4},{2,6},{8,0},{10,2},{16,8},{18,10},{24,16},{26,18},{28,24},{3... | collective-permute-start | bytes 786440 | tf_op jit(solution)/shard_map/ppermute | solution.py:632
  25.1 13.9 %all-to-all-start = ((f32[8,40,128]{2,1,0:T(8,128)}), f32[8,40,128]{2,1,0:T(8,128)}, u32[]{:S(2)}, u32[]{:S(2)}) async-start(f32[8,40,128]{2,1,0:T(8,128)} %bitcast.9), calls=%async_computation | async-start | bytes 327680 | tf_op jit(solution)/shard_map/all_to_all | solution.py:661
  31.0 13.7 %collective-permute-start.10 = (bf16[1024,128]{1,0:T(8,128)(2,1)}, bf16[1024,128]{1,0:T(8,128)(2,1)S(1)}, u32[]{:S(2)}, u32[]{:S(2)}) collective-permute-start(bf16[1024,128]{1,0:T(8,128)(2,1)} %get-tuple-element.40), channel_id=1, source_target_pairs={{0,8},{2,10},{8,16},{10,18},{16,24},{18,26},{24,28},{26,30},{28,20... | collective-permute-start | bytes 786440 | tf_op jit(solution)/shard_map/ppermute | solution.py:629
  33.0 11.7 %collective-permute-start.12 = (bf16[1024,128]{1,0:T(8,128)(2,1)S(1)}, bf16[1024,128]{1,0:T(8,128)(2,1)S(1)}, u32[]{:S(2)}, u32[]{:S(2)}) collective-permute-start(bf16[1024,128]{1,0:T(8,128)(2,1)S(1)} %collective-permute-done.11.refs_0_), channel_id=1, source_target_pairs={{0,8},{2,10},{8,16},{10,18},{16,24},{18,26},{24,28},{26,30},{28,20... | collective-permute-start | bytes 786440 | tf_op jit(solution)/shard_map/ppermute | solution.py:629
  34.5 10.2 %collective-permute-start.15 = (bf16[1024,128]{1,0:T(8,128)(2,1)}, bf16[1024,128]{1,0:T(8,128)(2,1)S(1)}, u32[]{:S(2)}, u32[]{:S(2)}) collective-permute-start(bf16[1024,128]{1,0:T(8,128)(2,1)} %collective-permute-done.14.refs_1_), channel_id=1, source_target_pairs={{0,4},{2,6},{8,0},{10,2},{16,8},{18,10},{24,16},{26,18},{28,24},{3... | collective-permute-start | bytes 786440 | tf_op jit(solution)/shard_map/ppermute | solution.py:632
  35.0 11.7 %collective-permute-start.13 = (bf16[1024,128]{1,0:T(8,128)(2,1)}, bf16[1024,128]{1,0:T(8,128)(2,1)S(1)}, u32[]{:S(2)}, u32[]{:S(2)}) collective-permute-start(bf16[1024,128]{1,0:T(8,128)(2,1)} %get-tuple-element.42), channel_id=1, source_target_pairs={{0,4},{2,6},{8,0},{10,2},{16,8},{18,10},{24,16},{26,18},{28,24},{3... | collective-permute-start | bytes 786440 | tf_op jit(solution)/shard_map/ppermute | solution.py:632
  39.0 1.6 %collective-permute-start.3 = (f32[320,128]{1,0:T(8,128)}, f32[320,128]{1,0:T(8,128)S(1)}, u32[]{:S(2)}, u32[]{:S(2)}) collective-permute-start(f32[320,128]{1,0:T(8,128)} %bitcast.10.refs_0_), channel_id=1, source_target_pairs={{0,2},{2,0},{4,6},{6,4},{8,10},{10,8},{12,14},{14,12},{16,18},{18,... | collective-permute-start | bytes 491528 | tf_op jit(solution)/shard_map/ppermute | solution.py:635
  46.8 6.6 %collective-permute-start.17 = (bf16[1024,128]{1,0:T(8,128)(2,1)S(1)}, bf16[1024,128]{1,0:T(8,128)(2,1)S(1)}, u32[]{:S(2)}, u32[]{:S(2)}) collective-permute-start(bf16[1024,128]{1,0:T(8,128)(2,1)S(1)} %get-tuple-element.45.after_ref), channel_id=1, source_target_pairs={{0,8},{2,10},{8,16},{10,18},{16,24},{18,26},{24,28},{26,30},{28,20... | collective-permute-start | bytes 786440 | tf_op jit(solution)/shard_map/ppermute | solution.py:629
  48.8 6.8 %collective-permute-start.16 = (bf16[1024,128]{1,0:T(8,128)(2,1)S(1)}, bf16[1024,128]{1,0:T(8,128)(2,1)S(1)}, u32[]{:S(2)}, u32[]{:S(2)}) collective-permute-start(bf16[1024,128]{1,0:T(8,128)(2,1)S(1)} %get-tuple-element.47), channel_id=1, source_target_pairs={{0,4},{2,6},{8,0},{10,2},{16,8},{18,10},{24,16},{26,18},{28,24},{3... | collective-permute-start | bytes 786440 | tf_op jit(solution)/shard_map/ppermute | solution.py:632
  55.6 2.8 %collective-permute-start.19 = (f32[4,512,128]{2,1,0:T(8,128)S(1)}, f32[4,512,128]{2,1,0:T(8,128)S(1)}, u32[]{:S(2)}, u32[]{:S(2)}) collective-permute-start(f32[4,512,128]{2,1,0:T(8,128)S(1)} %get-tuple-element.51), channel_id=1, source_target_pairs={{0,2},{2,0},{4,6},{6,4},{8,10},{10,8},{12,14},{14,12},{16,18},{18,... | collective-permute-start | bytes 3145736 | tf_op jit(solution)/shard_map/ppermute | solution.py:635
  57.9 2.8 %collective-permute-start.18 = (f32[4,512,128]{2,1,0:T(8,128)S(1)}, f32[4,512,128]{2,1,0:T(8,128)S(1)}, u32[]{:S(2)}, u32[]{:S(2)}) collective-permute-start(f32[4,512,128]{2,1,0:T(8,128)S(1)} %get-tuple-element.50), channel_id=1, source_target_pairs={{0,2},{2,0},{4,6},{6,4},{8,10},{10,8},{12,14},{14,12},{16,18},{18,... | collective-permute-start | bytes 3145736 | tf_op jit(solution)/shard_map/ppermute | solution.py:635

commit v5 on v4

--- a/solution.py
+++ b/solution.py
@@ -389,79 +389,92 @@
     )(modes, after)
 
 
-def grad_kernel(chunk, chunks, depth, firsts, aliased, modes_ref, *refs):
-    count = 1 + max(index for index, _ in firsts)
-    out_hbm, other_ref, own_ref, sems = refs[count + aliased :]
+def grad_kernel(chunks, size, depth, firsts, mine, modes_ref, *refs):
+    count = 1 + max(index for places in firsts for index, _ in places)
+    if mine:
+        out_hbm, held_ref, sems = refs[count:]
+    else:
+        held_ref = refs[count]
     half_rows = modes_ref.shape[1] // 2
-    kept, size, width = other_ref.shape
+    part_rows = half_rows // 2
+    kept, _, width = held_ref.shape
     half = width // 2
     core = lax.rem(lax.axis_index("dp"), 2)
-    first = core == 0
+    head = core if mine else 1 - core
     group = min(16, size // depth)
     tile = group * depth
     steps = size // tile
-
-    def write(s):
-        start = pl.multiple_of(s * tile, tile)
-        place = pl.multiple_of((core * chunks + chunk) * size + s * tile, tile)
-        return pltpu.make_async_copy(
-            own_ref.at[:, pl.ds(start, tile), :], out_hbm.at[:, pl.ds(place, tile), :], sems.at[s]
-        )
-
-    for s in range(steps):
-        for g in range(group):
-            start = s * tile + g * depth
-            right = jnp.concatenate(
-                [refs[i][at + start : at + start + depth, :] for i, at in firsts], axis=0
-            )
-            left = modes_ref[(chunk * steps + s) * group + g]
-            both = jnp.dot(left, right, preferred_element_type=jnp.float32)
-            plain, turned = both[:half_rows], both[half_rows:]
-            total = plain + jnp.concatenate([turned[:, half:], -turned[:, :half]], axis=1)
-            low, high = total[: half_rows // 2], total[half_rows // 2 :]
-            own, other = jnp.where(first, low, high), jnp.where(first, high, low)
-            for i in range(kept):
-                own_ref[i, pl.ds(start, depth), :] = own[i * depth : (i + 1) * depth]
-                other_ref[i, pl.ds(start, depth), :] = other[i * depth : (i + 1) * depth]
-        write(s).start()
-    for s in range(steps):
-        write(s).wait()
-
-
-def grad_chunk(modes, rows, kept, depth, chunk, chunks, previous):
+    copies = []
+    for n, (chunk, places) in enumerate(zip(chunks, firsts)):
+        for s in range(steps):
+            for g in range(group):
+                start = s * tile + g * depth
+                right = jnp.concatenate(
+                    [refs[i][at + start : at + start + depth, :] for i, at in places], axis=0
+                )
+                index = (chunk * steps + s) * group + g
+                left = jnp.concatenate(
+                    [
+                        modes_ref[
+                            index,
+                            pl.ds(
+                                pl.multiple_of(p * half_rows + head * part_rows, part_rows),
+                                part_rows,
+                            ),
+                            :,
+                        ]
+                        for p in range(2)
+                    ],
+                    axis=0,
+                )
+                both = jnp.dot(left, right, preferred_element_type=jnp.float32)
+                plain, turned = both[:part_rows], both[part_rows:]
+                total = plain + jnp.concatenate([turned[:, half:], -turned[:, :half]], axis=1)
+                for i in range(kept):
+                    held_ref[i, n * size + start : n * size + start + depth, :] = total[
+                        i * depth : (i + 1) * depth
+                    ]
+            if mine:
+                place = pl.multiple_of(core * (len(chunks) * size) + n * size + s * tile, tile)
+                copies.append(
+                    pltpu.make_async_copy(
+                        held_ref.at[:, n * size + s * tile : n * size + (s + 1) * tile, :],
+                        out_hbm.at[:, pl.ds(place, tile), :],
+                        sems.at[n * steps + s],
+                    )
+                )
+                copies[-1].start()
+    for copy in copies:
+        copy.wait()
+
+
+def grad_rows(modes, rows, kept, depth, chunks, mine):
     arrays, firsts = [], []
-    for array, first in rows:
-        if not any(array is known for known in arrays):
-            arrays.append(array)
-        firsts.append(([array is known for known in arrays].index(True), first))
-    size, width = arrays[0].shape[0] // chunks, arrays[0].shape[1]
-    hbm = pl.BlockSpec(memory_space=pl.ANY)
+    for part in rows:
+        firsts.append([])
+        for array, first in part:
+            if not any(array is known for known in arrays):
+                arrays.append(array)
+            firsts[-1].append(([array is known for known in arrays].index(True), first))
+    size, width = arrays[0].shape[0] // 2, arrays[0].shape[1]
     vmem = pl.BlockSpec(memory_space=pltpu.VMEM)
-    operands = [modes, *arrays]
-    in_specs = [vmem] * len(operands)
-    aliases = {}
-    if previous is not None:
-        in_specs.append(hbm)
-        aliases = {len(operands): 0}
-        operands.append(previous)
+    shape = (kept, len(chunks) * size, width)
     steps = size // depth // min(16, size // depth)
     return pl.pallas_call(
-        functools.partial(grad_kernel, chunk, chunks, depth, firsts, int(previous is not None)),
-        out_shape=[
-            jax.ShapeDtypeStruct((kept, 2 * chunks * size, width), jnp.float32),
-            jax.ShapeDtypeStruct((kept, size, width), jnp.float32),
-        ],
-        in_specs=in_specs,
-        out_specs=[hbm, vmem],
+        functools.partial(grad_kernel, chunks, size, depth, firsts, mine),
+        out_shape=jax.ShapeDtypeStruct(
+            (kept, 2 * shape[1], width) if mine else shape, jnp.float32
+        ),
+        in_specs=[vmem] * (1 + len(arrays)),
+        out_specs=pl.BlockSpec(memory_space=pl.ANY) if mine else vmem,
         scratch_shapes=[
-            pltpu.VMEM((kept, size, width), jnp.float32),
-            pltpu.SemaphoreType.DMA((steps,)),
-        ],
-        input_output_aliases=aliases,
-        compiler_params=pltpu.CompilerParams(vmem_limit_bytes=12 * MIB),
+            pltpu.VMEM(shape, jnp.float32),
+            pltpu.SemaphoreType.DMA((len(chunks) * steps,)),
+        ] if mine else [],
+        compiler_params=pltpu.CompilerParams(vmem_limit_bytes=14 * MIB),
         cost_estimate=work(1),
-        name="grad_chunk",
-    )(*operands)
+        name="grad_rows",
+    )(modes, *arrays)
 
 
 def place_kernel(chunk, chunks, part_ref, old_hbm, out_hbm, sems):
@@ -688,16 +701,19 @@
     ends = [up(first), down(second)]
     modes = spread_modes(modes, group, mode_count, first)
 
-    result, parts = None, []
+    rows = []
     for c in range(chunks):
-        rows = [(own, c * half), (twin, c * half)]
+        rows.append([(own, c * half), (twin, c * half)])
         for p in range(1, chips):
             if p == far:
-                rows += [(ends[c], 0), (ends[c], half)]
+                rows[c] += [(ends[c], 0), (ends[c], half)]
             else:
-                rows += [(array, c * half) for array in pair[p]]
-        result, part = grad_chunk(modes, rows, kept, mode_count, c, chunks, result)
-        parts.append(swap(part))
+                rows[c] += [(array, c * half) for array in pair[p]]
+    parts = [
+        swap(grad_rows(modes, rows[c : c + 1], kept, mode_count, [c], False))
+        for c in range(chunks)
+    ]
+    result = grad_rows(modes, rows, kept, mode_count, list(range(chunks)), True)
     for c, part in enumerate(parts):
         result = place_chunk(part, result, c, chunks)
     return result.reshape(kept, local_x, mode_count, mode_count, width)

time: 62 us -> 60.7 us (0.979)
    ppermute x4, waiting for transfers between devices: 2.89 us -> 1.61 us  [swap(): return lax.ppermute(rows, 'dp', [(d, d ^ 1) for d in range(devices)])]
    ppermute x7, waiting for transfers between devices: 3.27 us -> 4.19 us  [down(): return lax.ppermute(rows, 'dp', ring_perm(chips, -1))]
    pallas_call x2 -> x3, Pallas kernels: 4.32 us -> 3.73 us  [grad_rows(): pl.pallas_call(functools.partial(grad_kernel, chunks, size, depth, firsts...]
where the time goes in v5:
time: 60.7 us; the launch traced here: 60.3 us
  Pallas kernels  25.6 us (42%)
  starting transfers between devices  24.2 us (40%)
  waiting for transfers between devices  10.4 us (17%)
    ppermute x7, starting transfers between devices, down(): return lax.ppermute(rows, 'dp', ring_perm(chips, -1))  9.7 us
    pallas_call x1, Pallas kernels, slot_terms(): pl.pallas_call(functools.partial(slot_kernel, slabs, planes), out_shape=[...  7.09 us
    ppermute x7, starting transfers between devices, up(): return lax.ppermute(rows, 'dp', ring_perm(chips, 1))  6.66 us
    all_to_all x1, starting transfers between devices, per_device(): lax.all_to_all(payload.reshape(chips, -1, GZ), 'dp', split_axis=0, concat...  5.07 us
    ppermute x7, waiting for transfers between devices, down(): return lax.ppermute(rows, 'dp', ring_perm(chips, -1))  4.19 us
    pallas_call x3, Pallas kernels, grad_rows(): pl.pallas_call(functools.partial(grad_kernel, chunks, size, depth, firsts...  3.73 us
    pallas_call x1, Pallas kernels, spread_modes(): pl.pallas_call(functools.partial(spread_kernel, depth), out_shape=jax.Sha...  3.55 us
    pallas_call x1, Pallas kernels, sample_modes(): pl.pallas_call(functools.partial(modes_kernel, chips, slabs, slots, plane...  3.43 us
  transfers between devices with their start and end apart: 21, of which 7 were waited for; matrix products, arithmetic and copies ran while one was open for 0% of the time, Pallas kernels for 39%

profile of v5, /device:TPU:0, one launch (start us, length us, event | category | flops | bytes accessed | tf_op | source)
XLA Modules:
  0.0 60.3 jit_solution(7490648410039596255)
XLA Ops:
  0.0 1.2 %cast_rows.1 = (bf16[1024,128]{1,0:T(8,128)(2,1)S(1)}, bf16[1024,128]{1,0:T(8,128)(2,1)S(1)}) custom-call(f32[2048,128]{1,0:T(8,128)} %bitcast.13), custom_call_target="tpu_custom_call" | custom-call | flops 100000000 | bytes 1024 | tf_op jit(solution)/shard_map/cast_rows/pallas_call | solution.py:542
  1.8 2.6 %collective-permute-start.6 = (bf16[1024,128]{1,0:T(8,128)(2,1)S(1)}, bf16[1024,128]{1,0:T(8,128)(2,1)S(1)}, u32[]{:S(2)}, u32[]{:S(2)}) collective-permute-start(bf16[1024,128]{1,0:T(8,128)(2,1)S(1)} %get-tuple-element.32.refs_0_), channel_id=1, source_target_pairs={{0,4},{2,6},{8,0},{10,2},{16,8},{18,10},{24,16},{26,18},{28,24},{3... | collective-permute-start | bytes 786440 | tf_op jit(solution)/shard_map/ppermute | solution.py:645
  4.5 1.9 %collective-permute-start.7 = (bf16[1024,128]{1,0:T(8,128)(2,1)S(1)}, bf16[1024,128]{1,0:T(8,128)(2,1)S(1)}, u32[]{:S(2)}, u32[]{:S(2)}) collective-permute-start(bf16[1024,128]{1,0:T(8,128)(2,1)S(1)} %collective-permute-done.after_hbm.refs_1_), channel_id=1, source_target_pairs={{0,4},{2,6},{8,0},{10,2},{16,8},{18,10},{24,16},{26,18},{28,24},{3... | collective-permute-start | bytes 786440 | tf_op jit(solution)/shard_map/ppermute | solution.py:645
  6.5 7.1 %slot_terms.1 = (f32[264,128]{1,0:T(8,128)S(1)}, f32[264,128]{1,0:T(8,128)S(1)}) custom-call(s32[2,4]{1,0:T(2,128)} %bitcast.17, s32[2,4]{1,0:T(2,128)} %bitcast.18, s32[2]{0:T(128)} %bitcast.19, bf16[4,64,128]{2,1,0:T(8,128)(2,1)} %bitcast.14, bf16[3,4,128]{2,1,0:T(4,128)(2,1)} %bitcast.15, f32[3,64]{1,0:T(4,128)} %bitcast.16, f32[1,64]{1,0:T(1,128)} %bitcast.20, ...), custom_call_target="tpu_custom_call" | custom-call | flops 1000000000 | bytes 1024 | tf_op jit(solution)/shard_map/slot_terms/pallas_call | solution.py:135
  13.6 2.0 %collective-permute-start.2 = (f32[264,128]{1,0:T(8,128)S(1)}, f32[264,128]{1,0:T(8,128)S(1)}, u32[]{:S(2)}, u32[]{:S(2)}) collective-permute-start(f32[264,128]{1,0:T(8,128)S(1)} %get-tuple-element.27.refs_1_), channel_id=1, source_target_pairs={{0,1},{1,0},{2,3},{3,2},{4,5},{5,4},{6,7},{7,6},{8,9},{9,8},{10,11... | collective-permute-start | bytes 405512 | tf_op jit(solution)/shard_map/ppermute | solution.py:669
  15.7 1.2 %collective-permute-done.7.refs_3_ = bf16[1024,128]{1,0:T(8,128)(2,1)S(1)} collective-permute-done((bf16[1024,128]{1,0:T(8,128)(2,1)S(1)}, bf16[1024,128]{1,0:T(8,128)(2,1)S(1)}, u32[]{:S(2)}, u32[]{:S(2)}) %collective-permute-start.7) | collective-permute-done | bytes 262176 | tf_op jit(solution)/shard_map/ppermute | solution.py:645
  16.9 1.4 %collective-permute-done.5.refs_1_ = bf16[1024,128]{1,0:T(8,128)(2,1)S(1)} collective-permute-done((bf16[1024,128]{1,0:T(8,128)(2,1)S(1)}, bf16[1024,128]{1,0:T(8,128)(2,1)S(1)}, u32[]{:S(2)}, u32[]{:S(2)}) %collective-permute-start.5) | collective-permute-done | bytes 262176 | tf_op jit(solution)/shard_map/ppermute | solution.py:642
  18.8 1.7 %collective-permute-start.9 = (bf16[1024,128]{1,0:T(8,128)(2,1)S(1)}, bf16[1024,128]{1,0:T(8,128)(2,1)S(1)}, u32[]{:S(2)}, u32[]{:S(2)}) collective-permute-start(bf16[1024,128]{1,0:T(8,128)(2,1)S(1)} %get-tuple-element.34.refs_13_), channel_id=1, source_target_pairs={{0,4},{2,6},{8,0},{10,2},{16,8},{18,10},{24,16},{26,18},{28,24},{3... | collective-permute-start | bytes 786440 | tf_op jit(solution)/shard_map/ppermute | solution.py:645
  20.8 1.7 %collective-permute-start.14 = (bf16[1024,128]{1,0:T(8,128)(2,1)S(1)}, bf16[1024,128]{1,0:T(8,128)(2,1)}, u32[]{:S(2)}, u32[]{:S(2)}) collective-permute-start(bf16[1024,128]{1,0:T(8,128)(2,1)S(1)} %get-tuple-element.39.refs_14_), channel_id=1, source_target_pairs={{0,4},{2,6},{8,0},{10,2},{16,8},{18,10},{24,16},{26,18},{28,24},{3... | collective-permute-start | bytes 786440 | tf_op jit(solution)/shard_map/ppermute | solution.py:645
  22.6 2.5 %lift_slots.1 = (f32[320,128]{1,0:T(8,128)}, f32[8,128]{1,0:T(8,128)S(1)}) custom-call(f32[528,128]{1,0:T(8,128)S(1)} %get-tuple-element.28.refs_0_, f32[528,128]{1,0:T(8,128)S(1)} %get-tuple-element.29.refs_1_, bf16[64,64]{1,0:T(8,128)(2,1)S(1)} %copy-done), custom_call_target="tpu_custom_call" | custom-call | flops 100000000 | bytes 1024 | tf_op jit(solution)/shard_map/lift_slots/pallas_call | solution.py:239
  25.1 5.1 %all-to-all-start = ((f32[8,40,128]{2,1,0:T(8,128)}), f32[8,40,128]{2,1,0:T(8,128)}, u32[]{:S(2)}, u32[]{:S(2)}) async-start(f32[8,40,128]{2,1,0:T(8,128)} %bitcast.9), calls=%async_computation | async-start | bytes 327680 | tf_op jit(solution)/shard_map/all_to_all | solution.py:674
  31.0 2.0 %collective-permute-start.10 = (bf16[1024,128]{1,0:T(8,128)(2,1)}, bf16[1024,128]{1,0:T(8,128)(2,1)S(1)}, u32[]{:S(2)}, u32[]{:S(2)}) collective-permute-start(bf16[1024,128]{1,0:T(8,128)(2,1)} %get-tuple-element.36), channel_id=1, source_target_pairs={{0,8},{2,10},{8,16},{10,18},{16,24},{18,26},{24,28},{26,30},{28,20... | collective-permute-start | bytes 786440 | tf_op jit(solution)/shard_map/ppermute | solution.py:642
  33.0 1.5 %collective-permute-start.12 = (bf16[1024,128]{1,0:T(8,128)(2,1)S(1)}, bf16[1024,128]{1,0:T(8,128)(2,1)S(1)}, u32[]{:S(2)}, u32[]{:S(2)}) collective-permute-start(bf16[1024,128]{1,0:T(8,128)(2,1)S(1)} %collective-permute-done.11.refs_0_), channel_id=1, source_target_pairs={{0,8},{2,10},{8,16},{10,18},{16,24},{18,26},{24,28},{26,30},{28,20... | collective-permute-start | bytes 786440 | tf_op jit(solution)/shard_map/ppermute | solution.py:642
  35.1 1.4 %collective-permute-start.13 = (bf16[1024,128]{1,0:T(8,128)(2,1)}, bf16[1024,128]{1,0:T(8,128)(2,1)S(1)}, u32[]{:S(2)}, u32[]{:S(2)}) collective-permute-start(bf16[1024,128]{1,0:T(8,128)(2,1)} %get-tuple-element.38), channel_id=1, source_target_pairs={{0,4},{2,6},{8,0},{10,2},{16,8},{18,10},{24,16},{26,18},{28,24},{3... | collective-permute-start | bytes 786440 | tf_op jit(solution)/shard_map/ppermute | solution.py:645
  36.5 2.5 %all-to-all-done = f32[8,40,128]{2,1,0:T(8,128)} async-done(((f32[8,40,128]{2,1,0:T(8,128)}), f32[8,40,128]{2,1,0:T(8,128)}, u32[]{:S(2)}, u32[]{:S(2)}) %all-to-all-start) | async-done | bytes 163872 | tf_op jit(solution)/shard_map/all_to_all | solution.py:674
  39.0 1.6 %collective-permute-done.3.refs_1_ = f32[320,128]{1,0:T(8,128)S(1)} collective-permute-done((f32[320,128]{1,0:T(8,128)}, f32[320,128]{1,0:T(8,128)S(1)}, u32[]{:S(2)}, u32[]{:S(2)}) %collective-permute-start.3) | collective-permute-done | bytes 163872 | tf_op jit(solution)/shard_map/ppermute | solution.py:648
  40.6 3.4 %sample_modes.1 = (bf16[8,256,128]{2,1,0:T(8,128)(2,1)S(1)}, f32[8,128]{1,0:T(8,128)S(1)}) custom-call(f32[320,128]{1,0:T(8,128)} %bitcast.10.refs_0_, f32[320,128]{1,0:T(8,128)S(1)} %collective-permute-done.3.refs_1_), custom_call_target="tpu_custom_call" | custom-call | flops 200000000 | bytes 1024 | tf_op jit(solution)/shard_map/sample_modes/pallas_call | solution.py:333
  44.7 2.0 %collective-permute-done.13.refs_2_.refs_9_ = bf16[1024,128]{1,0:T(8,128)(2,1)S(1)} collective-permute-done((bf16[1024,128]{1,0:T(8,128)(2,1)}, bf16[1024,128]{1,0:T(8,128)(2,1)S(1)}, u32[]{:S(2)}, u32[]{:S(2)}) %collective-permute-start.13) | collective-permute-done | bytes 262176 | tf_op jit(solution)/shard_map/ppermute | solution.py:645
  46.8 2.1 %collective-permute-start.18 = (bf16[1024,128]{1,0:T(8,128)(2,1)S(1)}, bf16[1024,128]{1,0:T(8,128)(2,1)S(1)}, u32[]{:S(2)}, u32[]{:S(2)}) collective-permute-start(bf16[1024,128]{1,0:T(8,128)(2,1)S(1)} %get-tuple-element.41.after_ref), channel_id=1, source_target_pairs={{0,8},{2,10},{8,16},{10,18},{16,24},{18,26},{24,28},{26,30},{28,20... | collective-permute-start | bytes 786440 | tf_op jit(solution)/shard_map/ppermute | solution.py:642
  48.9 1.0 %joint.9 = (bf16[1024,128]{1,0:T(8,128)(2,1)S(1)}, bf16[1024,128]{1,0:T(8,128)(2,1)S(1)}) custom-call(bf16[1024,128]{1,0:T(8,128)(2,1)S(1)} %collective-permute-done.11.refs_0_, bf16[1024,128]{1,0:T(8,128)(2,1)} %collective-permute-done.14.refs_1_, f32[8,128]{1,0:T(8,128)S(1)} %get-tuple-element.40.refs_4_.refs_2_), custom_call_target="tpu_custom_call" | custom-call | flops 10000000 | bytes 1024 | tf_op jit(solution)/shard_map/joint/pallas_call | solution.py:602
  49.9 3.5 %spread_modes.1.modes_ref = bf16[64,256,256]{2,1,0:T(8,128)(2,1)S(1)} custom-call(bf16[8,256,128]{2,1,0:T(8,128)(2,1)S(1)} %get-tuple-element.31.modes_ref, bf16[1024,128]{1,0:T(8,128)(2,1)S(1)} %get-tuple-element.41.after_ref), custom_call_target="tpu_custom_call" | custom-call | flops 200000000 | bytes 1024 | tf_op jit(solution)/shard_map/spread_modes/pallas_call | solution.py:373
  56.1 2.2 %grad_rows.5.old_hbm = f32[4,2048,128]{2,1,0:T(8,128)} custom-call(bf16[64,256,256]{2,1,0:T(8,128)(2,1)S(1)} %spread_modes.1.modes_ref, bf16[1024,128]{1,0:T(8,128)(2,1)S(1)} %get-tuple-element.32.refs_0_, bf16[1024,128]{1,0:T(8,128)(2,1)S(1)} %collective-permute-done.after_hbm.refs_1_, bf16[1024,128]{1,0:T(8,128)(2,1)S(1)} %get-tuple-element.33.refs_2_, ...), custom_call_target="tpu_custom_call" | custom-call | flops 1000000000 | bytes 1024 | tf_op jit(solution)/shard_map/grad_rows/pallas_call | solution.py:463
  58.3 1.0 %place_chunk.2.old_hbm = f32[4,2048,128]{2,1,0:T(8,128)} custom-call(f32[4,512,128]{2,1,0:T(8,128)S(1)} %collective-permute-done.19.part_ref, f32[4,2048,128]{2,1,0:T(8,128)} %grad_rows.5.old_hbm), custom_call_target="tpu_custom_call", output_to_operand_aliasing={{}: (1, {})} | custom-call | flops 200000000 | bytes 1024 | tf_op jit(solution)/shard_map/place_chunk/pallas_call | solution.py:504
  59.3 1.0 %place_chunk.3 = f32[4,2048,128]{2,1,0:T(8,128)} custom-call(f32[4,512,128]{2,1,0:T(8,128)S(1)} %collective-permute-done.17.part_ref, f32[4,2048,128]{2,1,0:T(8,128)} %place_chunk.2.old_hbm), custom_call_target="tpu_custom_call", output_to_operand_aliasing={{}: (1, {})} | custom-call | flops 200000000 | bytes 1024 | tf_op jit(solution)/shard_map/place_chunk/pallas_call | solution.py:504
  (35 shorter events, 6.7 us)
Async XLA Ops:
  0.0 22.5 %copy-start = (bf16[64,64]{1,0:T(8,128)(2,1)S(1)}, bf16[64,64]{1,0:T(8,128)(2,1)}, u32[]{:S(2)}) copy-start(bf16[64,64]{1,0:T(8,128)(2,1)} %refs_2_.1) | copy-start | bytes 24580
  1.3 3.2 %collective-permute-start = (bf16[1024,128]{1,0:T(8,128)(2,1)S(1)}, bf16[1024,128]{1,0:T(8,128)(2,1)S(1)}, u32[]{:S(2)}, u32[]{:S(2)}) collective-permute-start(bf16[1024,128]{1,0:T(8,128)(2,1)S(1)} %get-tuple-element.25), channel_id=1, source_target_pairs={{0,2},{2,0},{4,6},{6,4},{8,10},{10,8},{12,14},{14,12},{16,18},{18,... | collective-permute-start | bytes 786440 | tf_op jit(solution)/shard_map/ppermute | solution.py:648
  1.8 13.8 %collective-permute-start.6 = (bf16[1024,128]{1,0:T(8,128)(2,1)S(1)}, bf16[1024,128]{1,0:T(8,128)(2,1)S(1)}, u32[]{:S(2)}, u32[]{:S(2)}) collective-permute-start(bf16[1024,128]{1,0:T(8,128)(2,1)S(1)} %get-tuple-element.32.refs_0_), channel_id=1, source_target_pairs={{0,4},{2,6},{8,0},{10,2},{16,8},{18,10},{24,16},{26,18},{28,24},{3... | collective-permute-start | bytes 786440 | tf_op jit(solution)/shard_map/ppermute | solution.py:645
  4.3 11.4 %collective-permute-start.4 = (bf16[1024,128]{1,0:T(8,128)(2,1)S(1)}, bf16[1024,128]{1,0:T(8,128)(2,1)S(1)}, u32[]{:S(2)}, u32[]{:S(2)}) collective-permute-start(bf16[1024,128]{1,0:T(8,128)(2,1)S(1)} %get-tuple-element.32.refs_0_), channel_id=1, source_target_pairs={{0,8},{2,10},{8,16},{10,18},{16,24},{18,26},{24,28},{26,30},{28,20... | collective-permute-start | bytes 786440 | tf_op jit(solution)/shard_map/ppermute | solution.py:642
  4.5 12.4 %collective-permute-start.7 = (bf16[1024,128]{1,0:T(8,128)(2,1)S(1)}, bf16[1024,128]{1,0:T(8,128)(2,1)S(1)}, u32[]{:S(2)}, u32[]{:S(2)}) collective-permute-start(bf16[1024,128]{1,0:T(8,128)(2,1)S(1)} %collective-permute-done.after_hbm.refs_1_), channel_id=1, source_target_pairs={{0,4},{2,6},{8,0},{10,2},{16,8},{18,10},{24,16},{26,18},{28,24},{3... | collective-permute-start | bytes 786440 | tf_op jit(solution)/shard_map/ppermute | solution.py:645
  6.4 12.0 %collective-permute-start.5 = (bf16[1024,128]{1,0:T(8,128)(2,1)S(1)}, bf16[1024,128]{1,0:T(8,128)(2,1)S(1)}, u32[]{:S(2)}, u32[]{:S(2)}) collective-permute-start(bf16[1024,128]{1,0:T(8,128)(2,1)S(1)} %collective-permute-done.after_hbm.refs_1_), channel_id=1, source_target_pairs={{0,8},{2,10},{8,16},{10,18},{16,24},{18,26},{24,28},{26,30},{28,20... | collective-permute-start | bytes 786440 | tf_op jit(solution)/shard_map/ppermute | solution.py:642
  13.6 7.2 %collective-permute-start.2 = (f32[264,128]{1,0:T(8,128)S(1)}, f32[264,128]{1,0:T(8,128)S(1)}, u32[]{:S(2)}, u32[]{:S(2)}) collective-permute-start(f32[264,128]{1,0:T(8,128)S(1)} %get-tuple-element.27.refs_1_), channel_id=1, source_target_pairs={{0,1},{1,0},{2,3},{3,2},{4,5},{5,4},{6,7},{7,6},{8,9},{9,8},{10,11... | collective-permute-start | bytes 405512 | tf_op jit(solution)/shard_map/ppermute | solution.py:669
  15.6 6.9 %collective-permute-start.1 = (f32[264,128]{1,0:T(8,128)S(1)}, f32[264,128]{1,0:T(8,128)S(1)}, u32[]{:S(2)}, u32[]{:S(2)}) collective-permute-start(f32[264,128]{1,0:T(8,128)S(1)} %get-tuple-element.26.refs_0_.refs_4_), channel_id=1, source_target_pairs={{0,1},{1,0},{2,3},{3,2},{4,5},{5,4},{6,7},{7,6},{8,9},{9,8},{10,11... | collective-permute-start | bytes 405512 | tf_op jit(solution)/shard_map/ppermute | solution.py:669
  18.4 11.8 %collective-permute-start.8 = (bf16[1024,128]{1,0:T(8,128)(2,1)S(1)}, bf16[1024,128]{1,0:T(8,128)(2,1)S(1)}, u32[]{:S(2)}, u32[]{:S(2)}) collective-permute-start(bf16[1024,128]{1,0:T(8,128)(2,1)S(1)} %get-tuple-element.33.refs_2_), channel_id=1, source_target_pairs={{0,8},{2,10},{8,16},{10,18},{16,24},{18,26},{24,28},{26,30},{28,20... | collective-permute-start | bytes 786440 | tf_op jit(solution)/shard_map/ppermute | solution.py:642
  18.8 11.4 %collective-permute-start.9 = (bf16[1024,128]{1,0:T(8,128)(2,1)S(1)}, bf16[1024,128]{1,0:T(8,128)(2,1)S(1)}, u32[]{:S(2)}, u32[]{:S(2)}) collective-permute-start(bf16[1024,128]{1,0:T(8,128)(2,1)S(1)} %get-tuple-element.34.refs_13_), channel_id=1, source_target_pairs={{0,4},{2,6},{8,0},{10,2},{16,8},{18,10},{24,16},{26,18},{28,24},{3... | collective-permute-start | bytes 786440 | tf_op jit(solution)/shard_map/ppermute | solution.py:645
  20.5 12.6 %collective-permute-start.11 = (bf16[1024,128]{1,0:T(8,128)(2,1)S(1)}, bf16[1024,128]{1,0:T(8,128)(2,1)S(1)}, u32[]{:S(2)}, u32[]{:S(2)}) collective-permute-start(bf16[1024,128]{1,0:T(8,128)(2,1)S(1)} %get-tuple-element.37.refs_3_), channel_id=1, source_target_pairs={{0,8},{2,10},{8,16},{10,18},{16,24},{18,26},{24,28},{26,30},{28,20... | collective-permute-start | bytes 786440 | tf_op jit(solution)/shard_map/ppermute | solution.py:642
  20.8 13.7 %collective-permute-start.14 = (bf16[1024,128]{1,0:T(8,128)(2,1)S(1)}, bf16[1024,128]{1,0:T(8,128)(2,1)}, u32[]{:S(2)}, u32[]{:S(2)}) collective-permute-start(bf16[1024,128]{1,0:T(8,128)(2,1)S(1)} %get-tuple-element.39.refs_14_), channel_id=1, source_target_pairs={{0,4},{2,6},{8,0},{10,2},{16,8},{18,10},{24,16},{26,18},{28,24},{3... | collective-permute-start | bytes 786440 | tf_op jit(solution)/shard_map/ppermute | solution.py:645
  25.1 13.9 %all-to-all-start = ((f32[8,40,128]{2,1,0:T(8,128)}), f32[8,40,128]{2,1,0:T(8,128)}, u32[]{:S(2)}, u32[]{:S(2)}) async-start(f32[8,40,128]{2,1,0:T(8,128)} %bitcast.9), calls=%async_computation | async-start | bytes 327680 | tf_op jit(solution)/shard_map/all_to_all | solution.py:674
  31.0 13.7 %collective-permute-start.10 = (bf16[1024,128]{1,0:T(8,128)(2,1)}, bf16[1024,128]{1,0:T(8,128)(2,1)S(1)}, u32[]{:S(2)}, u32[]{:S(2)}) collective-permute-start(bf16[1024,128]{1,0:T(8,128)(2,1)} %get-tuple-element.36), channel_id=1, source_target_pairs={{0,8},{2,10},{8,16},{10,18},{16,24},{18,26},{24,28},{26,30},{28,20... | collective-permute-start | bytes 786440 | tf_op jit(solution)/shard_map/ppermute | solution.py:642
  33.0 11.7 %collective-permute-start.12 = (bf16[1024,128]{1,0:T(8,128)(2,1)S(1)}, bf16[1024,128]{1,0:T(8,128)(2,1)S(1)}, u32[]{:S(2)}, u32[]{:S(2)}) collective-permute-start(bf16[1024,128]{1,0:T(8,128)(2,1)S(1)} %collective-permute-done.11.refs_0_), channel_id=1, source_target_pairs={{0,8},{2,10},{8,16},{10,18},{16,24},{18,26},{24,28},{26,30},{28,20... | collective-permute-start | bytes 786440 | tf_op jit(solution)/shard_map/ppermute | solution.py:642
  34.5 10.2 %collective-permute-start.15 = (bf16[1024,128]{1,0:T(8,128)(2,1)}, bf16[1024,128]{1,0:T(8,128)(2,1)S(1)}, u32[]{:S(2)}, u32[]{:S(2)}) collective-permute-start(bf16[1024,128]{1,0:T(8,128)(2,1)} %collective-permute-done.14.refs_1_), channel_id=1, source_target_pairs={{0,4},{2,6},{8,0},{10,2},{16,8},{18,10},{24,16},{26,18},{28,24},{3... | collective-permute-start | bytes 786440 | tf_op jit(solution)/shard_map/ppermute | solution.py:645
  35.1 11.7 %collective-permute-start.13 = (bf16[1024,128]{1,0:T(8,128)(2,1)}, bf16[1024,128]{1,0:T(8,128)(2,1)S(1)}, u32[]{:S(2)}, u32[]{:S(2)}) collective-permute-start(bf16[1024,128]{1,0:T(8,128)(2,1)} %get-tuple-element.38), channel_id=1, source_target_pairs={{0,4},{2,6},{8,0},{10,2},{16,8},{18,10},{24,16},{26,18},{28,24},{3... | collective-permute-start | bytes 786440 | tf_op jit(solution)/shard_map/ppermute | solution.py:645
  39.0 1.6 %collective-permute-start.3 = (f32[320,128]{1,0:T(8,128)}, f32[320,128]{1,0:T(8,128)S(1)}, u32[]{:S(2)}, u32[]{:S(2)}) collective-permute-start(f32[320,128]{1,0:T(8,128)} %bitcast.10.refs_0_), channel_id=1, source_target_pairs={{0,2},{2,0},{4,6},{6,4},{8,10},{10,8},{12,14},{14,12},{16,18},{18,... | collective-permute-start | bytes 491528 | tf_op jit(solution)/shard_map/ppermute | solution.py:648
  46.8 6.6 %collective-permute-start.18 = (bf16[1024,128]{1,0:T(8,128)(2,1)S(1)}, bf16[1024,128]{1,0:T(8,128)(2,1)S(1)}, u32[]{:S(2)}, u32[]{:S(2)}) collective-permute-start(bf16[1024,128]{1,0:T(8,128)(2,1)S(1)} %get-tuple-element.41.after_ref), channel_id=1, source_target_pairs={{0,8},{2,10},{8,16},{10,18},{16,24},{18,26},{24,28},{26,30},{28,20... | collective-permute-start | bytes 786440 | tf_op jit(solution)/shard_map/ppermute | solution.py:642
  48.9 6.4 %collective-permute-start.16 = (bf16[1024,128]{1,0:T(8,128)(2,1)S(1)}, bf16[1024,128]{1,0:T(8,128)(2,1)S(1)}, u32[]{:S(2)}, u32[]{:S(2)}) collective-permute-start(bf16[1024,128]{1,0:T(8,128)(2,1)S(1)} %get-tuple-element.43), channel_id=1, source_target_pairs={{0,4},{2,6},{8,0},{10,2},{16,8},{18,10},{24,16},{26,18},{28,24},{3... | collective-permute-start | bytes 786440 | tf_op jit(solution)/shard_map/ppermute | solution.py:645
  54.2 4.1 %collective-permute-start.19 = (f32[4,512,128]{2,1,0:T(8,128)S(1)}, f32[4,512,128]{2,1,0:T(8,128)S(1)}, u32[]{:S(2)}, u32[]{:S(2)}) collective-permute-start(f32[4,512,128]{2,1,0:T(8,128)S(1)} %grad_rows.4), channel_id=1, source_target_pairs={{0,2},{2,0},{4,6},{6,4},{8,10},{10,8},{12,14},{14,12},{16,18},{18,... | collective-permute-start | bytes 3145736 | tf_op jit(solution)/shard_map/ppermute | solution.py:648
  56.0 3.3 %collective-permute-start.17 = (f32[4,512,128]{2,1,0:T(8,128)S(1)}, f32[4,512,128]{2,1,0:T(8,128)S(1)}, u32[]{:S(2)}, u32[]{:S(2)}) collective-permute-start(f32[4,512,128]{2,1,0:T(8,128)S(1)} %grad_rows.3), channel_id=1, source_target_pairs={{0,2},{2,0},{4,6},{6,4},{8,10},{10,8},{12,14},{14,12},{16,18},{18,... | collective-permute-start | bytes 3145736 | tf_op jit(solution)/shard_map/ppermute | solution.py:648
